TPU v7x, 32 devices: a whole 2x2x4 slice. The times are simulated.
32 devices in a mesh: blk: 8 (over z, y), order: 4 (over x, core).
Axes of the slice: x: 2, y: 2, z: 4, core: 2. Of those that a mesh axis runs over, the one named last changes fastest.
Arguments:
- harmonics: float32 [64, 4, 8192], P('order', None, 'blk'), may hold values from -6 to 6
- legendre: float32 [64, 2, 64, 8192], P('order', None, 'blk'), may hold values from -0.0078125 to 0.0078125
- sky_map: float32 [64, 2, 16384], P(('blk', 'order')), may hold values from -6 to 6
- cycle_length: int32 [64], P(('blk', 'order')), may hold values from 4 to 16384, as said below
- cycle_offset: int32 [64], P(('blk', 'order')), may hold values from 0 to 1, as said below
- cycle_weight: float32 [64], P(('blk', 'order')), may hold values from 0.1 to 0.4
- order_ids: int32 [64], P('order'), may hold values from 0 to 8191, as said below
Outputs:
- refined: float32 [64, 4, 8192], P('order', None, 'blk')
- residual: float32 [64, 2, 16384], P(('blk', 'order'))
Inputs may be any that keep to these rules, and one draw needn't show every extreme that they name: `cycle_length`: cycle lengths are multiples of 4. Of each device's 2 consecutive cycles, those at even places have 4 * 4096 pixels, those at odd places 4 j pixels for some j from 1 to 4095. `cycle_offset`: 1 on every cycle of fewer than 16384 pixels. `order_ids`: the orders are distinct; 0 and 8191 are among them. Slot s (from 0) of each index of order holds an order from s * 512 to (s + 1) * 512 - 1.
All inputs are finite; a program needn't handle non-finite values.
Results may differ from a plain program's by a relative error of at most 0.0003.
Values sent between devices are 32-bit elements; how exact they have to be, the bound alone decides.
No kernel may reach another device: no remote copies, remote signals or barrier semaphores. Data moves between devices by JAX's collectives and lax.ppermute only.
A program may use at most 192 MiB of HBM per device.

v0:
```python
import math

import jax
import jax.numpy as jnp
from jax import lax
from jax.sharding import PartitionSpec as P

HIGHEST = lax.Precision.HIGHEST


def cycle_tables(orders, length, offset, first_pixel, block_width):
    pixels = first_pixel + lax.iota(jnp.int32, block_width)
    phase_turns = orders[:, None] * (2 * pixels + offset)[None, :] % (2 * length)
    angles = phase_turns.astype(jnp.float32) * (math.pi / length.astype(jnp.float32))
    inside = (pixels < length).astype(jnp.float32)
    return (jnp.concatenate([jnp.cos(angles), jnp.sin(angles)], axis=0), inside)


def synth_weights(phases, factor):
    scaled = phases * factor[:, None]
    first_row = jnp.concatenate([scaled[:, 0], -scaled[:, 1]])
    second_row = jnp.concatenate([scaled[:, 2], -scaled[:, 3]])
    return jnp.stack([first_row, second_row])


def fold_totals(totals, weighting):
    half = totals.shape[1] // 2
    return weighting * jnp.stack(
        [totals[0, :half], -totals[0, half:], totals[1, :half], -totals[1, half:]], axis=1
    )


def assemble(products):
    positive = products[:, 0]
    negative = products[:, 1]
    return jnp.stack(
        [
            -positive[:, 0] + negative[:, 3],
            -positive[:, 1] - negative[:, 2],
            -positive[:, 2] - negative[:, 1],
            -positive[:, 3] + negative[:, 0],
        ],
        axis=1,
    )


def adjoint_coeffs(returned):
    positive = -returned
    negative = jnp.stack([returned[:, 3], -returned[:, 2], -returned[:, 1], returned[:, 0]], axis=1)
    return jnp.stack([positive, negative], axis=1)


def block_count(padded_length, block_width):
    return padded_length // block_width


def owner_cycle(inputs, orders, factor, normalise, block_width):
    cycle_phases, sky_row, length, offset, weight = inputs
    padded_length = sky_row.shape[1]
    weights = synth_weights(cycle_phases, factor)

    def advance(block_index, state_pair):
        residual, totals = state_pair
        first_pixel = block_index * block_width
        trig_table, inside = cycle_tables(orders, length, offset, first_pixel, block_width)
        modelled = jnp.dot(weights, trig_table, precision=HIGHEST)
        observed = lax.dynamic_slice_in_dim(sky_row, first_pixel, block_width, 1)
        section = (observed - modelled) * inside[None, :]
        residual = lax.dynamic_update_slice_in_dim(residual, section, first_pixel, 1)
        totals = totals + lax.dot_general(
            section, trig_table, (((1,), (1,)), ((), ())), precision=HIGHEST
        )
        return (residual, totals)

    start_state = (jnp.zeros_like(sky_row), jnp.zeros((2, weights.shape[1]), jnp.float32))
    residual, totals = lax.fori_loop(
        0, block_count(padded_length, block_width), advance, start_state
    )
    return (residual, fold_totals(totals, weight * normalise))


def body(harmonics, legendre, sky_map, cycle_length, cycle_offset, cycle_weight, order_ids):
    order_size = lax.axis_size("order")
    blk_size = lax.axis_size("blk")
    local_orders = order_ids.shape[0]
    ell_count = legendre.shape[3]
    padded_length = sky_map.shape[2]
    block_width = min(2048, padded_length)
    cycle_total = cycle_length.shape[0] * order_size * blk_size
    normalise = math.sqrt(ell_count * local_orders * order_size / (cycle_total * padded_length))
    floors = jnp.maximum(order_ids, 2)
    section = lax.all_gather(harmonics, "blk", axis=2, tiled=True)
    section_width = section.shape[2]
    degrees = lax.iota(jnp.int32, section_width)
    keep_mask = (degrees[None, :] >= floors[:, None]).astype(jnp.float32)
    products = jnp.einsum(
        "mtrl,mcl->mtcr", legendre, section * keep_mask[:, None, :], precision=HIGHEST
    )
    phases = assemble(products)
    all_orders = lax.all_gather(order_ids, "order", axis=0, tiled=True)
    factor = jnp.where(all_orders == 0, 1.0, 2.0).astype(jnp.float32)
    cycle_phases = lax.all_to_all(phases, "order", split_axis=2, concat_axis=0, tiled=True)

    def one_cycle(inputs):
        return owner_cycle(inputs, all_orders, factor, normalise, block_width)

    residual, analysed = lax.map(
        one_cycle,
        (jnp.transpose(cycle_phases, (2, 0, 1)), sky_map, cycle_length, cycle_offset, cycle_weight),
    )
    returned = lax.all_to_all(
        jnp.transpose(analysed, (1, 2, 0)), "order", split_axis=0, concat_axis=2, tiled=True
    )
    coeffs = adjoint_coeffs(returned)
    shard_width = harmonics.shape[2]
    update = jnp.einsum("mtrl,mtar->mal", legendre, coeffs, precision=HIGHEST)
    own_update = lax.psum_scatter(update, "blk", scatter_dimension=2, tiled=True)
    degrees = lax.axis_index("blk") * shard_width + lax.iota(jnp.int32, shard_width)
    valid_mask = (degrees[None, :] >= floors[:, None]).astype(jnp.float32)
    refined = valid_mask[:, None, :] * (harmonics + own_update)
    return (refined, residual)


def solution(mesh):
    return jax.shard_map(
        body,
        mesh=mesh,
        in_specs=(
            P("order", None, "blk"),
            P("order", None, "blk", None),
            P(("blk", "order"), None, None),
            P(("blk", "order")),
            P(("blk", "order")),
            P(("blk", "order")),
            P("order"),
        ),
        out_specs=(P("order", None, "blk"), P(("blk", "order"), None, None)),
        check_vma=False,
    )
```

profile of v0, /device:TPU:0, one launch (start us, length us, event | category | flops | bytes accessed | tf_op | source)
XLA Modules:
  0.0 492.9 jit_solution(10969325561648089969)
XLA Ops:
  17.8 44.4 %all-gather.2.cloned.1.call-done = f32[16,4,8192]{2,1,0:T(4,128)} async-done(((f32[16,4,1024]{2,1,0:T(4,128)}), f32[16,4,8192]{2,1,0:T(4,128)}) %all-gather.2.cloned.1.call-update) | async-done | bytes 2097168 | tf_op jit(solution)/shard_map/all_gather | solution.py:92
  62.2 57.8 %fusion.18 = f32[16,2,4,8]{3,2,1,0:T(4,128)S(1)} fusion(f32[16,2,8,8192]{3,2,1,0:T(8,128)} %param.12, f32[16,4,8192]{2,1,0:T(4,128)} %all-gather.2.cloned.1.call-done, f32[16,8192]{1,0:T(8,128)S(1)} %fusion.22), kind=kOutput, calls=%fused_computation.43 | convolution fusion | flops 101187584 | bytes 11014144 | tf_op jit(solution)/shard_map/mtrl,mcl->mtcr/dot_general | solution.py:96
  129.2 165.0 %while.31 = (s32[]{:T(128)}, f32[2,2,16384]{2,1,0:T(2,128)S(1)}, f32[2,64,4]{1,2,0:T(4,128)S(1)}, s32[2]{0:T(128)S(1)}, s32[2]{0:T(128)S(1)}, /*index=5*/f32[2,6...) while((s32[]{:T(128)}, f32[2,2,16384]{2,1,0:T(2,128)S(1)}, ...), condition=%wide.region_3.4_spmd, body=%wide.region_0.3_spmd.sunk | while | flops 14440976 | bytes 3920030 | solution.py:107
  132.0 78.4 %while.32 = (s32[]{:T(128)}, f32[2,16384]{1,0:T(2,128)S(1)}, f32[2,128]{1,0:T(2,128)S(1)}, f32[2,16384]{1,0:T(2,128)S(1)}, s32[64]{0:T(128)S(1)}, /*index=5*/s32...) while((s32[]{:T(128)}, f32[2,16384]{1,0:T(2,128)S(1)}, ...), condition=%wide.region_2.2_spmd.clone, body=%wide.region_1.1_spmd.clone.sunk | while | flops 14438919 | bytes 3247586 | solution.py:76
  132.6 7.0 %fusion.41 = (f32[64,2048]{1,0:T(8,128)S(1)}, f32[64,2048]{1,0:T(8,128)S(1)}) fusion(f32[]{:T(128)} %get-tuple-element.609, s32[]{:T(128)} %get-tuple-element.607, s32[2048]{0:T(1024)S(1)} %multiply_add_fusion.2, s32[64]{0:T(128)S(1)} %get-tuple-element.605, pred[]{:T(512)} %get-tuple-element.608), kind=kLoop, calls=%fused_computation.12.clone.1 | loop fusion | flops 1310720 | bytes 1057033 | tf_op jit(solution)/shard_map/while/body/eval_jaxpr/while/body/eval_jaxpr/cos | solution.py:16
  142.4 7.0 %fusion.41 = (f32[64,2048]{1,0:T(8,128)S(1)}, f32[64,2048]{1,0:T(8,128)S(1)}) fusion(f32[]{:T(128)} %get-tuple-element.609, s32[]{:T(128)} %get-tuple-element.607, s32[2048]{0:T(1024)S(1)} %multiply_add_fusion.2, s32[64]{0:T(128)S(1)} %get-tuple-element.605, pred[]{:T(512)} %get-tuple-element.608), kind=kLoop, calls=%fused_computation.12.clone.1 | loop fusion | flops 1310720 | bytes 1057033 | tf_op jit(solution)/shard_map/while/body/eval_jaxpr/while/body/eval_jaxpr/cos | solution.py:16
  152.1 7.0 %fusion.41 = (f32[64,2048]{1,0:T(8,128)S(1)}, f32[64,2048]{1,0:T(8,128)S(1)}) fusion(f32[]{:T(128)} %get-tuple-element.609, s32[]{:T(128)} %get-tuple-element.607, s32[2048]{0:T(1024)S(1)} %multiply_add_fusion.2, s32[64]{0:T(128)S(1)} %get-tuple-element.605, pred[]{:T(512)} %get-tuple-element.608), kind=kLoop, calls=%fused_computation.12.clone.1 | loop fusion | flops 1310720 | bytes 1057033 | tf_op jit(solution)/shard_map/while/body/eval_jaxpr/while/body/eval_jaxpr/cos | solution.py:16
  161.9 7.0 %fusion.41 = (f32[64,2048]{1,0:T(8,128)S(1)}, f32[64,2048]{1,0:T(8,128)S(1)}) fusion(f32[]{:T(128)} %get-tuple-element.609, s32[]{:T(128)} %get-tuple-element.607, s32[2048]{0:T(1024)S(1)} %multiply_add_fusion.2, s32[64]{0:T(128)S(1)} %get-tuple-element.605, pred[]{:T(512)} %get-tuple-element.608), kind=kLoop, calls=%fused_computation.12.clone.1 | loop fusion | flops 1310720 | bytes 1057033 | tf_op jit(solution)/shard_map/while/body/eval_jaxpr/while/body/eval_jaxpr/cos | solution.py:16
  171.7 7.0 %fusion.41 = (f32[64,2048]{1,0:T(8,128)S(1)}, f32[64,2048]{1,0:T(8,128)S(1)}) fusion(f32[]{:T(128)} %get-tuple-element.609, s32[]{:T(128)} %get-tuple-element.607, s32[2048]{0:T(1024)S(1)} %multiply_add_fusion.2, s32[64]{0:T(128)S(1)} %get-tuple-element.605, pred[]{:T(512)} %get-tuple-element.608), kind=kLoop, calls=%fused_computation.12.clone.1 | loop fusion | flops 1310720 | bytes 1057033 | tf_op jit(solution)/shard_map/while/body/eval_jaxpr/while/body/eval_jaxpr/cos | solution.py:16
  181.5 7.0 %fusion.41 = (f32[64,2048]{1,0:T(8,128)S(1)}, f32[64,2048]{1,0:T(8,128)S(1)}) fusion(f32[]{:T(128)} %get-tuple-element.609, s32[]{:T(128)} %get-tuple-element.607, s32[2048]{0:T(1024)S(1)} %multiply_add_fusion.2, s32[64]{0:T(128)S(1)} %get-tuple-element.605, pred[]{:T(512)} %get-tuple-element.608), kind=kLoop, calls=%fused_computation.12.clone.1 | loop fusion | flops 1310720 | bytes 1057033 | tf_op jit(solution)/shard_map/while/body/eval_jaxpr/while/body/eval_jaxpr/cos | solution.py:16
  191.3 7.0 %fusion.41 = (f32[64,2048]{1,0:T(8,128)S(1)}, f32[64,2048]{1,0:T(8,128)S(1)}) fusion(f32[]{:T(128)} %get-tuple-element.609, s32[]{:T(128)} %get-tuple-element.607, s32[2048]{0:T(1024)S(1)} %multiply_add_fusion.2, s32[64]{0:T(128)S(1)} %get-tuple-element.605, pred[]{:T(512)} %get-tuple-element.608), kind=kLoop, calls=%fused_computation.12.clone.1 | loop fusion | flops 1310720 | bytes 1057033 | tf_op jit(solution)/shard_map/while/body/eval_jaxpr/while/body/eval_jaxpr/cos | solution.py:16
  201.1 7.0 %fusion.41 = (f32[64,2048]{1,0:T(8,128)S(1)}, f32[64,2048]{1,0:T(8,128)S(1)}) fusion(f32[]{:T(128)} %get-tuple-element.609, s32[]{:T(128)} %get-tuple-element.607, s32[2048]{0:T(1024)S(1)} %multiply_add_fusion.2, s32[64]{0:T(128)S(1)} %get-tuple-element.605, pred[]{:T(512)} %get-tuple-element.608), kind=kLoop, calls=%fused_computation.12.clone.1 | loop fusion | flops 1310720 | bytes 1057033 | tf_op jit(solution)/shard_map/while/body/eval_jaxpr/while/body/eval_jaxpr/cos | solution.py:16
  214.5 78.4 %while.32 = (s32[]{:T(128)}, f32[2,16384]{1,0:T(2,128)S(1)}, f32[2,128]{1,0:T(2,128)S(1)}, f32[2,16384]{1,0:T(2,128)S(1)}, s32[64]{0:T(128)S(1)}, /*index=5*/s32...) while((s32[]{:T(128)}, f32[2,16384]{1,0:T(2,128)S(1)}, ...), condition=%wide.region_2.2_spmd.clone, body=%wide.region_1.1_spmd.clone.sunk | while | flops 14438919 | bytes 3247586 | solution.py:76
  215.0 7.0 %fusion.41 = (f32[64,2048]{1,0:T(8,128)S(1)}, f32[64,2048]{1,0:T(8,128)S(1)}) fusion(f32[]{:T(128)} %get-tuple-element.609, s32[]{:T(128)} %get-tuple-element.607, s32[2048]{0:T(1024)S(1)} %multiply_add_fusion.2, s32[64]{0:T(128)S(1)} %get-tuple-element.605, pred[]{:T(512)} %get-tuple-element.608), kind=kLoop, calls=%fused_computation.12.clone.1 | loop fusion | flops 1310720 | bytes 1057033 | tf_op jit(solution)/shard_map/while/body/eval_jaxpr/while/body/eval_jaxpr/cos | solution.py:16
  224.8 7.0 %fusion.41 = (f32[64,2048]{1,0:T(8,128)S(1)}, f32[64,2048]{1,0:T(8,128)S(1)}) fusion(f32[]{:T(128)} %get-tuple-element.609, s32[]{:T(128)} %get-tuple-element.607, s32[2048]{0:T(1024)S(1)} %multiply_add_fusion.2, s32[64]{0:T(128)S(1)} %get-tuple-element.605, pred[]{:T(512)} %get-tuple-element.608), kind=kLoop, calls=%fused_computation.12.clone.1 | loop fusion | flops 1310720 | bytes 1057033 | tf_op jit(solution)/shard_map/while/body/eval_jaxpr/while/body/eval_jaxpr/cos | solution.py:16
  234.6 7.0 %fusion.41 = (f32[64,2048]{1,0:T(8,128)S(1)}, f32[64,2048]{1,0:T(8,128)S(1)}) fusion(f32[]{:T(128)} %get-tuple-element.609, s32[]{:T(128)} %get-tuple-element.607, s32[2048]{0:T(1024)S(1)} %multiply_add_fusion.2, s32[64]{0:T(128)S(1)} %get-tuple-element.605, pred[]{:T(512)} %get-tuple-element.608), kind=kLoop, calls=%fused_computation.12.clone.1 | loop fusion | flops 1310720 | bytes 1057033 | tf_op jit(solution)/shard_map/while/body/eval_jaxpr/while/body/eval_jaxpr/cos | solution.py:16
  244.4 7.0 %fusion.41 = (f32[64,2048]{1,0:T(8,128)S(1)}, f32[64,2048]{1,0:T(8,128)S(1)}) fusion(f32[]{:T(128)} %get-tuple-element.609, s32[]{:T(128)} %get-tuple-element.607, s32[2048]{0:T(1024)S(1)} %multiply_add_fusion.2, s32[64]{0:T(128)S(1)} %get-tuple-element.605, pred[]{:T(512)} %get-tuple-element.608), kind=kLoop, calls=%fused_computation.12.clone.1 | loop fusion | flops 1310720 | bytes 1057033 | tf_op jit(solution)/shard_map/while/body/eval_jaxpr/while/body/eval_jaxpr/cos | solution.py:16
  254.2 7.0 %fusion.41 = (f32[64,2048]{1,0:T(8,128)S(1)}, f32[64,2048]{1,0:T(8,128)S(1)}) fusion(f32[]{:T(128)} %get-tuple-element.609, s32[]{:T(128)} %get-tuple-element.607, s32[2048]{0:T(1024)S(1)} %multiply_add_fusion.2, s32[64]{0:T(128)S(1)} %get-tuple-element.605, pred[]{:T(512)} %get-tuple-element.608), kind=kLoop, calls=%fused_computation.12.clone.1 | loop fusion | flops 1310720 | bytes 1057033 | tf_op jit(solution)/shard_map/while/body/eval_jaxpr/while/body/eval_jaxpr/cos | solution.py:16
  273.8 7.0 %fusion.41 = (f32[64,2048]{1,0:T(8,128)S(1)}, f32[64,2048]{1,0:T(8,128)S(1)}) fusion(f32[]{:T(128)} %get-tuple-element.609, s32[]{:T(128)} %get-tuple-element.607, s32[2048]{0:T(1024)S(1)} %multiply_add_fusion.2, s32[64]{0:T(128)S(1)} %get-tuple-element.605, pred[]{:T(512)} %get-tuple-element.608), kind=kLoop, calls=%fused_computation.12.clone.1 | loop fusion | flops 1310720 | bytes 1057033 | tf_op jit(solution)/shard_map/while/body/eval_jaxpr/while/body/eval_jaxpr/cos | solution.py:16
  302.0 7.7 %convolution_bitcast_fusion.1 = f32[16,4,8192]{2,1,0:T(4,128)S(1)} fusion(f32[16,2,8,8192]{3,2,1,0:T(8,128)} %param.12, f32[16,1,4,8]{3,2,1,0:T(4,128)S(1)} %maximum_bitcast_fusion.2, f32[16,1,4,8]{3,2,1,0:T(4,128)S(1)} %copy.41), kind=kOutput, calls=%fused_computation.39 | convolution fusion | flops 100664320 | bytes 10489856 | tf_op jit(solution)/shard_map/mtrl,mtar->mal/dot_general | solution.py:116
  309.6 31.5 %copy.44 = f32[16,4,8192]{1,0,2:T(8,128)} copy(f32[16,4,8192]{2,1,0:T(4,128)S(1)} %convolution_bitcast_fusion.1) | data formatting | bytes 4194304
  341.1 46.1 %reshape.163 = f32[8192,64]{1,0:T(8,128)} reshape(f32[8192,16,4]{2,1,0:T(8,128)} %bitcast.35) | data formatting | bytes 4194304
  387.3 85.7 %reduce-scatter.4.cloned.1.call-done = f32[1024,64]{1,0:T(8,128)} async-done(((f32[8192,64]{1,0:T(8,128)}), f32[1024,64]{1,0:T(8,128)}) %reduce-scatter.4.cloned.1.call-update) | async-done | bytes 262160
  473.0 7.0 %reshape.164 = f32[1024,16,4]{2,1,0:T(8,128)} reshape(f32[1024,64]{1,0:T(8,128)} %reduce-scatter.4.cloned.1.call-done) | data formatting | bytes 524288
  (153 shorter events, 95.4 us)
Async XLA Ops:
  7.2 122.0 %copy-start = (f32[2,2,16384]{2,1,0:T(2,128)S(1)}, f32[2,2,16384]{2,1,0:T(2,128)}, u32[]{:S(2)}) copy-start(f32[2,2,16384]{2,1,0:T(2,128)} %param.13) | copy-start | bytes 786436
  7.2 122.0 %copy-start.4 = (s32[2]{0:T(128)S(1)}, s32[2]{0:T(128)}, u32[]{:S(2)}) copy-start(s32[2]{0:T(128)} %param.14) | copy-start | bytes 28
  7.2 122.0 %copy-start.3 = (s32[2]{0:T(128)S(1)}, s32[2]{0:T(128)}, u32[]{:S(2)}) copy-start(s32[2]{0:T(128)} %param.15) | copy-start | bytes 28
  7.2 122.0 %copy-start.5 = (f32[2]{0:T(128)S(1)}, f32[2]{0:T(128)}, u32[]{:S(2)}) copy-start(f32[2]{0:T(128)} %param.16) | copy-start | bytes 28
  7.2 55.0 %all-gather.2.cloned.1.call-start = ((), (), s32[]{:S(2)}) async-start(), calls=%async_computation.3 | async-start | bytes 2359296 | tf_op jit(solution)/shard_map/all_gather | solution.py:92
  120.9 6.9 %all-to-all-start = ((f32[4,1,128]{2,1,0:T(1,128)}), f32[4,1,128]{2,1,0:T(1,128)S(1)}, u32[]{:S(2)}, u32[]{:S(2)}) async-start(f32[4,1,128]{2,1,0:T(1,128)} %reshape.165), calls=%async_computation | async-start | bytes 4096 | tf_op jit(solution)/shard_map/all_to_all | solution.py:102
  124.2 348.9 %reduce-scatter.4.cloned.1.call-start = ((), (), s32[]{:S(2)}) async-start(), calls=%async_computation.4 | async-start | bytes 4718592
  294.2 46.9 %copy-start.2 = (f32[2,2,16384]{2,1,0:T(2,128)}, f32[2,2,16384]{2,1,0:T(2,128)S(1)}, u32[]{:S(2)}) copy-start(f32[2,2,16384]{2,1,0:T(2,128)S(1)} %get-tuple-element.263) | copy-start | bytes 786436
  387.3 97.9 %copy-start.1 = (f32[16,4,1024]{2,1,0:T(4,128)S(1)}, f32[16,4,1024]{2,1,0:T(4,128)}, u32[]{:S(2)}) copy-start(f32[16,4,1024]{2,1,0:T(4,128)} %param.11) | copy-start | bytes 786436
Sparse Core Ops, SparseCore 0:
  10.2 51.9 all-gather.1
  387.4 85.6 reduce-scatter.3
where the time goes:
time: 494 us; the launch traced here: 493 us
  waiting for transfers between devices  134 us (27%)
  other arithmetic  134 us (27%)
  local copies, waits for them, and re-layouts  98.1 us (20%)
  matrix products  90.6 us (18%)
  between operations  14.9 us (3%)
  blocking collectives  12.4 us (3%)
  loops' own time  5.14 us (1%)
    cos x16, other arithmetic, cycle_tables(): return (jnp.concatenate([jnp.cos(angles), jnp.sin(angles)], axis=0), inside)  111 us
    unnamed x28, local copies, waits for them, and re-layouts  93.2 us
    unnamed x3, waiting for transfers between devices  86.4 us
    dot_general x1, matrix products, body(): jnp.einsum('mtrl,mcl->mtcr', legendre, section * keep_mask[:, None, :], p...  57.8 us
    all_gather x1, waiting for transfers between devices, body(): section = lax.all_gather(harmonics, 'blk', axis=2, tiled=True)  44.4 us
    dot_general x16, matrix products, advance(): lax.dot_general(section, trig_table, (((1,), (1,)), ((), ())), precision=...  14.5 us
    dot_general x16, matrix products, advance(): modelled = jnp.dot(weights, trig_table, precision=HIGHEST)  10.6 us
    convert_element_type x16, other arithmetic, cycle_tables(): inside = (pixels < length).astype(jnp.float32)  10.2 us
  transfers between devices with their start and end apart: 3, of which 3 were waited for; matrix products, arithmetic and copies ran while one was open for 1% of the time, Pallas kernels for 0%

commit v1 on v0

v1 whole, which is shorter than its diff:
```python
import math

import jax
import jax.numpy as jnp
from jax import lax
from jax.experimental import pallas as pl
from jax.experimental.pallas import tpu as pltpu
from jax.sharding import PartitionSpec as P

HIGHEST = lax.Precision.HIGHEST
LANES = 128
VMEM = pltpu.VMEM
MIB = 1024 * 1024


def slot_ranges(slots):
    return [(0, slots // 2), (slots // 2, slots)]


def needed(block, first_slot, width, stratum):
    return (block + 1) * width > stratum * first_slot


def trig_tables(ids, length, offset, rows, columns):
    period = (2 * length)[:, None, None]
    scale = (math.pi / length.astype(jnp.float32))[:, None, None]
    coarse = 2 * columns * lax.iota(jnp.int32, rows)[None, :, None] + offset[:, None, None]
    angle = (ids[None, None, :] * coarse % period).astype(jnp.float32) * scale
    cos_a, sin_a = jnp.cos(angle), jnp.sin(angle)
    fine = 2 * lax.iota(jnp.int32, columns)[None, None, :]
    angle = (ids[None, :, None] * fine % period).astype(jnp.float32) * scale
    table_b = jnp.concatenate([jnp.cos(angle), jnp.sin(angle)], axis=1)
    return (
        jnp.concatenate([cos_a, -sin_a], axis=2),
        jnp.concatenate([sin_a, cos_a], axis=2),
        table_b,
    )


def pixel_mask(shape, length):
    pixel = lax.broadcasted_iota(jnp.int32, shape, 0) * shape[1]
    pixel = pixel + lax.broadcasted_iota(jnp.int32, shape, 1)
    return pixel < length


def sky_kernel(
    normalise, groups, slots, cycles,
    ids_ref, meta_ref, length_ref, lanes_ref, sky_ref, acs_ref, asc_ref, bt_ref,
    pieces_ref, gram_ref,
):
    me = lax.axis_index("order")
    rows, both = acs_ref.shape[1:]
    every = both // 2
    row8 = lax.broadcasted_iota(jnp.int32, (8, both), 0)
    sums = [jnp.zeros((8, both), jnp.float32) for _ in range(4)]
    for c in range(cycles):
        inside = pixel_mask((rows, LANES), length_ref[c])
        scale = meta_ref[0, slots + 2 * cycles + c] * normalise
        for q in range(2):
            section = jnp.where(inside, sky_ref[c, q], 0.0)
            spun = lax.dot_general(
                section, bt_ref[c], (((1,), (1,)), ((), ())), precision=HIGHEST,
                preferred_element_type=jnp.float32,
            )
            even = jnp.sum(spun * acs_ref[c], axis=0, keepdims=True) * scale
            odd = jnp.sum(spun * asc_ref[c], axis=0, keepdims=True) * -scale
            sums[2 * q] = jnp.where(row8 == c, even, sums[2 * q])
            sums[2 * q + 1] = jnp.where(row8 == c, odd, sums[2 * q + 1])
    source = lax.broadcasted_iota(jnp.int32, (both, LANES), 0) % every
    lane = lax.broadcasted_iota(jnp.int32, (both, LANES), 1)
    for d in range(groups):
        piece = jnp.zeros((8, LANES), jnp.float32)
        for a in range(4):
            place = ((lane - a * slots) == (source - d * slots)) & (lane // slots == a)
            piece = piece + jnp.dot(
                sums[a], place.astype(jnp.float32), precision=HIGHEST,
                preferred_element_type=jnp.float32,
            )
        pieces_ref[d] = piece
    count, wide = gram_ref.shape[1:]
    row = lax.broadcasted_iota(jnp.int32, (count, wide), 0)
    length = jnp.ones((count, wide), jnp.float32)
    offset = jnp.zeros((count, wide), jnp.float32)
    weight = jnp.zeros((count, wide), jnp.float32)
    for r in range(count):
        d = (r // cycles) ^ me
        c = r % cycles
        length = jnp.where(row == r, meta_ref[d, slots + c], length)
        offset = jnp.where(row == r, meta_ref[d, slots + cycles + c], offset)
        weight = jnp.where(row == r, meta_ref[d, slots + 2 * cycles + c], weight)
    others = jnp.broadcast_to(lanes_ref[...], (count, wide))
    lane = lax.broadcasted_iota(jnp.int32, (count, wide), 1)
    cosine = (lane // slots) % 2 == 0
    factor = jnp.where(others == 0.0, 0.5, 1.0) * normalise * weight * length

    def response(n):
        turns = jnp.round(n / length)
        sign = jnp.where((offset > 0.5) & (turns.astype(jnp.int32) % 2 != 0), -1.0, 1.0)
        return jnp.where(turns * length == n, sign, 0.0)

    def one(m, carry):
        mine = ids_ref[m].astype(jnp.float32)
        near = response(mine - others)
        far = response(mine + others)
        gram_ref[m] = factor * (near + jnp.where(cosine, far, -far))
        return carry

    lax.fori_loop(0, gram_ref.shape[0], one, 0)


def load_tables(legendre, tables, sems, stratum):
    copies = []
    for m in range(tables.shape[0]):
        part = (m, slice(None), slice(None), pl.ds(stratum * m, tables.shape[3] - stratum * m))
        copies.append(pltpu.make_async_copy(legendre.at[part], tables.at[part], sems.at[m]))
    return copies


def forward_kernel(ranges, blocks, groups, stratum, ids_ref, legendre, pieces_ref, *rest):
    parts = rest[: len(ranges) * blocks]
    phases_ref, *messages, tables, sems = rest[len(ranges) * blocks :]
    me = lax.axis_index("blk")
    slots = tables.shape[0]
    count = tables.shape[2]
    width = parts[0].shape[2]
    copies = load_tables(legendre, tables, sems, stratum)
    for copy in copies:
        copy.start()
    lane = lax.broadcasted_iota(jnp.int32, (count, LANES), 1)
    phases = jnp.zeros((count, LANES), jnp.float32)
    for index, (low, high) in enumerate(ranges):
        for m in range(low, high):
            copies[m].wait()
            floor = jnp.maximum(ids_ref[m], 2)
            total = [jnp.zeros((count, LANES), jnp.float32)] * 4
            for d in range(blocks):
                block = me ^ d
                part = parts[index * blocks + d]

                def use(carry, part=part, block=block, m=m, low=low, floor=floor):
                    t0, t1, t2, t3 = carry
                    first = pl.multiple_of(block * width, LANES)
                    for t in range(width // LANES):
                        keep = lane >= floor - first - t * LANES
                        span = pl.ds(first + t * LANES, LANES)
                        plus = jnp.where(keep, tables[m, 0, :, span], 0.0)
                        minus = jnp.where(keep, tables[m, 1, :, span], 0.0)
                        here = pl.ds(t * LANES, LANES)
                        c0, c1, c2, c3 = [part[m - low, a : a + 1, here] for a in range(4)]
                        t0 = t0 - plus * c0 + minus * c3
                        t1 = t1 - plus * c1 - minus * c2
                        t2 = t2 - plus * c2 - minus * c1
                        t3 = t3 - plus * c3 + minus * c0
                    return [t0, t1, t2, t3]

                total = lax.cond(
                    (block + 1) * width > stratum * m, use, lambda carry: carry, total
                )
            for a in range(4):
                value = jnp.sum(total[a], axis=1, keepdims=True)
                phases = jnp.where(lane == a * slots + m, value, phases)
    phases_ref[...] = phases
    for d in range(1, groups):
        messages[d - 1][:count] = phases
        messages[d - 1][count:] = pieces_ref[d]


def fold_rows(values, row):
    for step in (1, 2, 4):
        low = (row & step) == 0
        values = [
            jnp.where(low, values[i], values[i + 1])
            + pltpu.roll(jnp.where(low, values[i + 1], values[i]), step, 0)
            for i in range(0, len(values), 2)
        ]
    return values[0]


def backward_kernel(
    ranges, blocks, groups, cycles, stratum, legendre, gram_ref, pieces_ref, phases_ref, *rest
):
    messages = rest[: groups - 1]
    outs = rest[groups - 1 : groups - 1 + len(ranges) * blocks]
    tables, sky, sems = rest[groups - 1 + len(ranges) * blocks :]
    me = lax.axis_index("blk")
    owner = lax.axis_index("order")
    slots = tables.shape[0]
    count = tables.shape[2]
    width = outs[0].shape[2]
    copies = load_tables(legendre, tables, sems, stratum)
    for copy in copies:
        copy.start()
    wide = 4 * slots
    pairs = []
    for d in range(groups):
        phases = phases_ref[...] if d == 0 else messages[d - 1][:count]
        piece = pieces_ref[0] if d == 0 else messages[d - 1][count:]
        sky[pl.ds((owner ^ d) * cycles, cycles)] = piece[:cycles]
        pairs.append(phases)
    lane = lax.broadcasted_iota(jnp.int32, (count, LANES), 1)
    row8 = lax.broadcasted_iota(jnp.int32, (8, LANES), 0)
    per = LANES // wide
    packed = []
    for start in range(0, groups, per):
        value = pairs[start]
        for k in range(1, per):
            value = jnp.where(
                lane // wide == k, pltpu.roll(pairs[start + k], k * wide, 1), value
            )
        packed.append(value)
    observed = sky[...]
    for index, (low, high) in enumerate(ranges):
        for m in range(low, high):
            total = jnp.where((lane < wide) & (lane % slots == m), observed, 0.0)
            for k, value in enumerate(packed):
                total = total - gram_ref[m, :, k * LANES : (k + 1) * LANES] * value
            an = []
            for a in range(4):
                value = jnp.where((lane % wide) // slots == a, total, 0.0)
                value = jnp.sum(value, axis=1, keepdims=True)
                an.append(jnp.broadcast_to(value, (count, LANES)))
            copies[m].wait()
            for d in range(blocks):
                block = me ^ d
                out = outs[index * blocks + d]

                @pl.when((block + 1) * width > stratum * m)
                def _(an=an, out=out, block=block, m=m, low=low):
                    first = pl.multiple_of(block * width, LANES)
                    for t in range(0, width // LANES, 2):
                        values = []
                        for u in range(2):
                            span = pl.ds(first + (t + u) * LANES, LANES)
                            plus = tables[m, 0, :, span]
                            minus = tables[m, 1, :, span]
                            four = [
                                minus * an[3] - plus * an[0],
                                -(plus * an[1] + minus * an[2]),
                                -(plus * an[2] + minus * an[1]),
                                minus * an[0] - plus * an[3],
                            ]
                            values += [
                                sum(v[8 * k : 8 * k + 8] for k in range(count // 8)) for v in four
                            ]
                        folded = fold_rows(values, row8)
                        for u in range(2):
                            out[m - low, :, pl.ds((t + u) * LANES, LANES)] = folded[
                                4 * u : 4 * u + 4
                            ]


def residual_kernel(
    groups, slots, cycles,
    length_ref, ids_ref, sky_ref, acs_ref, asc_ref, bt_ref, phases_ref, *rest
):
    messages = rest[: groups - 1]
    out_ref, spread = rest[groups - 1 :]
    owner = lax.axis_index("order")
    rows, both = acs_ref.shape[1:]
    every = both // 2
    count = phases_ref.shape[0]
    source = lax.broadcasted_iota(jnp.int32, (LANES, both), 0)
    lane = lax.broadcasted_iota(jnp.int32, (LANES, both), 1) % every
    factor = jnp.where(ids_ref[...] == 0.0, 1.0, 2.0)
    for a in range(4):
        total = jnp.zeros((count, both), jnp.float32)
        for d in range(groups):
            phases = phases_ref[...] if d == 0 else messages[d - 1][:count]
            place = (lane - d * slots == source - a * slots) & (lane // slots == d)
            total = total + jnp.dot(
                phases, place.astype(jnp.float32), precision=HIGHEST,
                preferred_element_type=jnp.float32,
            )
        spread[a] = total * factor
    for c in range(cycles):
        inside = pixel_mask((rows, LANES), length_ref[c])
        for q in range(2):
            real = spread[2 * q, pl.ds(owner * cycles + c, 1)]
            imag = spread[2 * q + 1, pl.ds(owner * cycles + c, 1)]
            weights = real * acs_ref[c] - imag * asc_ref[c]
            model = jnp.dot(
                weights, bt_ref[c], precision=HIGHEST, preferred_element_type=jnp.float32
            )
            out_ref[c, q] = jnp.where(inside, sky_ref[c, q] - model, 0.0)


def smem():
    return pl.BlockSpec(memory_space=pltpu.SMEM)


def vmem():
    return pl.BlockSpec(memory_space=VMEM)


def shape(*dims):
    return jax.ShapeDtypeStruct(dims, jnp.float32)


def body(harmonics, legendre, sky_map, cycle_length, cycle_offset, cycle_weight, order_ids):
    groups = lax.axis_size("order")
    blocks = lax.axis_size("blk")
    slots, _, width = harmonics.shape
    count, degrees = legendre.shape[2:]
    cycles, _, pixels = sky_map.shape
    rows = pixels // LANES
    stratum = degrees // slots
    every = slots * groups
    normalise = math.sqrt(degrees * every / (cycles * groups * blocks * pixels))
    ranges = slot_ranges(slots)

    meta = jnp.concatenate(
        [
            order_ids.astype(jnp.float32),
            cycle_length.astype(jnp.float32),
            cycle_offset.astype(jnp.float32),
            cycle_weight,
        ]
    )
    meta = jnp.pad(meta, (0, LANES - meta.shape[0]))[None]

    def swap(value, axis, step, keep=lambda source: True):
        size = lax.axis_size(axis)
        return lax.ppermute(
            value, axis, [(i, i ^ step) for i in range(size) if keep(i)]
        )

    metas = jnp.concatenate([meta] + [swap(meta, "order", d) for d in range(1, groups)])

    parts = []
    for low, high in ranges:
        own = harmonics[low:high]

        def far(block, low=low):
            return needed(block, low, width, stratum)

        got = [own] + [swap(own, "blk", d, far) for d in range(2, blocks, 2)]
        line = []
        for k, value in enumerate(got):
            line += [value, swap(value, "blk", 1, lambda b, k=k: far(b ^ (2 * k)))]
        parts += line

    ids = metas[:, :slots].reshape(every)
    acs, asc, table_b = trig_tables(
        ids.astype(jnp.int32), cycle_length, cycle_offset, rows, LANES
    )
    sky = sky_map.reshape(cycles, 2, rows, LANES)
    lane_ids = jnp.broadcast_to(ids.reshape(groups, 1, slots), (groups, 4, slots))
    lane_ids = lane_ids.reshape(1, 4 * every)
    pieces, gram = pl.pallas_call(
        lambda *refs: sky_kernel(normalise, groups, slots, cycles, *refs),
        out_shape=(shape(groups, 8, LANES), shape(slots, count, 4 * every)),
        in_specs=[smem(), smem(), smem()] + [vmem()] * 5,
        out_specs=(vmem(), vmem()),
        compiler_params=pltpu.CompilerParams(vmem_limit_bytes=16 * MIB),
        cost_estimate=pl.CostEstimate(flops=10**8, bytes_accessed=2 * MIB, transcendentals=0),
        name="sky_analysis",
    )(order_ids, metas, cycle_length, lane_ids, sky, acs, asc, table_b)

    table_scratch = [
        pltpu.VMEM(legendre.shape, jnp.float32),
        pltpu.SemaphoreType.DMA((slots,)),
    ]
    hbm = pl.BlockSpec(memory_space=pl.ANY)
    outs = pl.pallas_call(
        lambda *refs: forward_kernel(ranges, blocks, groups, stratum, *refs),
        out_shape=[shape(count, LANES)] + [shape(count + 8, LANES)] * (groups - 1),
        in_specs=[smem(), hbm, vmem()] + [vmem()] * len(parts),
        out_specs=[vmem()] * groups,
        scratch_shapes=table_scratch,
        compiler_params=pltpu.CompilerParams(vmem_limit_bytes=40 * MIB),
        cost_estimate=pl.CostEstimate(flops=10**8, bytes_accessed=8 * MIB, transcendentals=0),
        name="forward",
    )(order_ids, legendre, pieces, *parts)
    phases = outs[0]
    messages = [swap(outs[d], "order", d) for d in range(1, groups)]

    partial = pl.pallas_call(
        lambda *refs: backward_kernel(ranges, blocks, groups, cycles, stratum, *refs),
        out_shape=[shape(high - low, 4, width) for low, high in ranges for _ in range(blocks)],
        in_specs=[hbm] + [vmem()] * (2 + groups),
        out_specs=[vmem()] * (len(ranges) * blocks),
        scratch_shapes=[table_scratch[0], pltpu.VMEM((count, LANES), jnp.float32), table_scratch[1]],
        compiler_params=pltpu.CompilerParams(vmem_limit_bytes=40 * MIB),
        cost_estimate=pl.CostEstimate(flops=10**8, bytes_accessed=8 * MIB, transcendentals=0),
        name="backward",
    )(legendre, gram, pieces, phases, *messages)

    residual = pl.pallas_call(
        lambda *refs: residual_kernel(groups, slots, cycles, *refs),
        out_shape=shape(cycles, 2, rows, LANES),
        in_specs=[smem()] + [vmem()] * (5 + groups),
        out_specs=vmem(),
        scratch_shapes=[pltpu.VMEM((4, count, 2 * every), jnp.float32)],
        compiler_params=pltpu.CompilerParams(vmem_limit_bytes=16 * MIB),
        cost_estimate=pl.CostEstimate(flops=10**8, bytes_accessed=2 * MIB, transcendentals=0),
        name="residual",
    )(cycle_length, jnp.concatenate([ids, ids])[None], sky, acs, asc, table_b, phases, *messages)
    residual = residual.reshape(sky_map.shape)

    updates = []
    for index, (low, high) in enumerate(ranges):
        piece = partial[index * blocks : (index + 1) * blocks]

        def far(block, low=low):
            return needed(block, low, width, stratum)

        sums = {}
        for k in reversed(range(blocks // 2)):
            moved = swap(piece[2 * k + 1], "blk", 1, lambda b, k=k: far(b ^ 1 ^ (2 * k)))
            sums[k] = piece[2 * k] + moved
        total = sums[0]
        for k in reversed(range(1, blocks // 2)):
            total = total + swap(sums[k], "blk", 2 * k, lambda b, k=k: far(b ^ (2 * k)))
        updates.append(total)
    update = jnp.concatenate(updates)
    floors = jnp.maximum(order_ids, 2)
    degree = lax.axis_index("blk") * width + lax.iota(jnp.int32, width)
    valid = degree[None, :] >= floors[:, None]
    refined = jnp.where(valid[:, None, :], harmonics + update, 0.0)
    return (refined, residual)


def solution(mesh):
    return jax.shard_map(
        body,
        mesh=mesh,
        in_specs=(
            P("order", None, "blk"),
            P("order", None, "blk", None),
            P(("blk", "order"), None, None),
            P(("blk", "order")),
            P(("blk", "order")),
            P(("blk", "order")),
            P("order"),
        ),
        out_specs=(P("order", None, "blk"), P(("blk", "order"), None, None)),
        check_vma=False,
    )
```

time: 494 us -> 110 us (0.22)
  the two profiles are of different devices: /device:TPU:0 before, /device:TPU:24 now
where the time goes in v1:
time: 110 us
  starting transfers between devices  56 us (51%)
  Pallas kernels  16.3 us (15%)
  waiting for transfers between devices  15.2 us (14%)
  other arithmetic  13 us (12%)
  local copies, waits for them, and re-layouts  7.9 us (7%)
    ppermute x34, starting transfers between devices, swap(): lax.ppermute(value, axis, [(i, i ^ step) for i in range(size) if keep(i)])  56 us
    ppermute x34, waiting for transfers between devices, swap(): lax.ppermute(value, axis, [(i, i ^ step) for i in range(size) if keep(i)])  15.2 us
    pallas_call x1, Pallas kernels, body(): pl.pallas_call(lambda *refs: backward_kernel(ranges, blocks, groups, cycl...  6.4 us
    pallas_call x1, Pallas kernels, body(): pl.pallas_call(lambda *refs: forward_kernel(ranges, blocks, groups, strat...  5.92 us
    unnamed x14, local copies, waits for them, and re-layouts  4.7 us
    add x6, other arithmetic, body(): sums[k] = piece[2 * k] + moved  2.94 us
    pallas_call x1, Pallas kernels, body(): pl.pallas_call(lambda *refs: sky_kernel(normalise, groups, slots, cycles,...  2.52 us
  transfers between devices with their start and end apart: 34, of which 9 were waited for; matrix products, arithmetic and copies ran while one was open for 11% of the time, Pallas kernels for 4%

profile of v1, /device:TPU:24, one launch (start us, length us, event | category | flops | bytes accessed | tf_op | source)
XLA Modules:
  0.0 109.5 jit_solution(6596532608339769908)
XLA Ops:
  3.5 1.6 %collective-permute-start.1 = (f32[1,128]{1,0:T(1,128)S(1)}, f32[1,128]{1,0:T(1,128)S(1)}, u32[]{:S(2)}, u32[]{:S(2)}) collective-permute-start(f32[1,128]{1,0:T(1,128)S(1)} %fusion.16), channel_id=1, source_target_pairs={{0,2},{1,3},{2,0},{3,1},{4,6},{5,7},{6,4},{7,5},{8,10},{9,11},{10,... | collective-permute-start | bytes 1544 | tf_op jit(solution)/shard_map/ppermute | solution.py:323
  6.4 2.4 %collective-permute-start.11 = (f32[8,4,1024]{2,1,0:T(4,128)S(1)}, f32[8,4,1024]{2,1,0:T(4,128)S(1)}, u32[]{:S(2)}, u32[]{:S(2)}) collective-permute-start(f32[8,4,1024]{2,1,0:T(4,128)S(1)} %get-tuple-element.46.refs_11_), channel_id=1, source_target_pairs={{16,24},{20,28},{24,16},{28,20},{17,25},{21,29},{25,17},{29,21},{1... | collective-permute-start | bytes 393224 | tf_op jit(solution)/shard_map/ppermute | solution.py:323
  14.6 1.6 %collective-permute-start.4 = (f32[8,4,1024]{2,1,0:T(4,128)S(1)}, f32[8,4,1024]{2,1,0:T(4,128)S(1)}, u32[]{:S(2)}, u32[]{:S(2)}) collective-permute-start(f32[8,4,1024]{2,1,0:T(4,128)S(1)} %get-tuple-element.47.refs_3_), channel_id=1, source_target_pairs={{0,8},{4,12},{8,0},{12,4},{16,24},{20,28},{24,16},{28,20},{1,9},{5... | collective-permute-start | bytes 393224 | tf_op jit(solution)/shard_map/ppermute | solution.py:323
  16.4 1.9 %fusion.5 = (f32[2,128,64]{2,1,0:T(8,128)S(1)}, f32[2,128,64]{2,1,0:T(8,128)S(1)}, f32[2,128,64]{2,1,0:T(8,128)S(1)}) fusion(f32[2]{0:T(128)S(1)} %broadcast_divide_fusion, s32[2]{0:T(128)S(1)} %get-tuple-element.57, s32[2,128]{1,0:T(2,128)S(1)} %broadcast_add_fusion, s32[64]{0:T(128)S(1)} %convert_element_type.32, pred[2]{0:T(512)(128)(4,1)S(1)} %broadcast_compare_fusion.1), kind=kLoop, calls=%fused_computation.17 | loop fusion | flops 180224 | bytes 197906 | tf_op jit(solution)/shard_map/sin | solution.py:29
  18.4 2.9 %collective-permute-start.8 = (f32[8,4,1024]{2,1,0:T(4,128)S(1)}, f32[8,4,1024]{2,1,0:T(4,128)S(1)}, u32[]{:S(2)}, u32[]{:S(2)}) collective-permute-start(f32[8,4,1024]{2,1,0:T(4,128)S(1)} %get-tuple-element.47.refs_3_), channel_id=1, source_target_pairs={{0,24},{4,28},{8,16},{12,20},{16,8},{20,12},{24,0},{28,4},{1,25},{... | collective-permute-start | bytes 393224 | tf_op jit(solution)/shard_map/ppermute | solution.py:323
  21.3 3.4 %collective-permute-start.10 = (f32[8,4,1024]{2,1,0:T(4,128)S(1)}, f32[8,4,1024]{2,1,0:T(4,128)S(1)}, u32[]{:S(2)}, u32[]{:S(2)}) collective-permute-start(f32[8,4,1024]{2,1,0:T(4,128)S(1)} %get-tuple-element.46.refs_11_), channel_id=1, source_target_pairs={{16,20},{20,16},{24,28},{28,24},{17,21},{21,17},{25,29},{29,25},{1... | collective-permute-start | bytes 393224 | tf_op jit(solution)/shard_map/ppermute | solution.py:323
  25.3 3.4 %collective-permute-start.12 = (f32[8,4,1024]{2,1,0:T(4,128)S(1)}, f32[8,4,1024]{2,1,0:T(4,128)S(1)}, u32[]{:S(2)}, u32[]{:S(2)}) collective-permute-start(f32[8,4,1024]{2,1,0:T(4,128)S(1)} %collective-permute-done.11.refs_13_), channel_id=1, source_target_pairs={{16,20},{20,16},{24,28},{28,24},{17,21},{21,17},{25,29},{29,25},{1... | collective-permute-start | bytes 393224 | tf_op jit(solution)/shard_map/ppermute | solution.py:323
  32.0 1.6 %collective-permute-start.7 = (f32[8,4,1024]{2,1,0:T(4,128)S(1)}, f32[8,4,1024]{2,1,0:T(4,128)S(1)}, u32[]{:S(2)}, u32[]{:S(2)}) collective-permute-start(f32[8,4,1024]{2,1,0:T(4,128)S(1)} %collective-permute-done.6.refs_7_), channel_id=1, source_target_pairs={{0,4},{4,0},{8,12},{12,8},{16,20},{20,16},{24,28},{28,24},{1,5},{5... | collective-permute-start | bytes 393224 | tf_op jit(solution)/shard_map/ppermute | solution.py:323
  34.6 1.8 %collective-permute-start.9 = (f32[8,4,1024]{2,1,0:T(4,128)S(1)}, f32[8,4,1024]{2,1,0:T(4,128)S(1)}, u32[]{:S(2)}, u32[]{:S(2)}) collective-permute-start(f32[8,4,1024]{2,1,0:T(4,128)S(1)} %collective-permute-done.8.refs_9_), channel_id=1, source_target_pairs={{0,4},{4,0},{8,12},{12,8},{16,20},{20,16},{24,28},{28,24},{1,5},{5... | collective-permute-start | bytes 393224 | tf_op jit(solution)/shard_map/ppermute | solution.py:323
  37.8 2.5 %sky_analysis.1 = (f32[4,8,128]{2,1,0:T(8,128)S(1)}, f32[16,8,256]{2,1,0:T(8,128)S(1)}) custom-call(s32[16]{0:T(128)S(1)} %copy-done.4, f32[4,128]{1,0:T(4,128)S(1)} %pad_maximum_fusion.3.refs_1_, s32[2]{0:T(128)S(1)} %copy-done.2, f32[1,256]{1,0:T(1,128)S(1)} %reshape.135.refs_3_, f32[2,2,128,128]{3,2,1,0:T(8,128)S(1)} %reshape.136.refs_4_.refs_2_, ...), custom_call_target="tpu_custom_call" | custom-call | flops 100000000 | bytes 2097152 | tf_op jit(solution)/shard_map/sky_analysis/pallas_call | solution.py:349
  41.8 3.4 %copy-done = f32[16,2,8,8192]{3,2,1,0:T(8,128)S(1)} copy-done((f32[16,2,8,8192]{3,2,1,0:T(8,128)S(1)}, f32[16,2,8,8192]{3,2,1,0:T(8,128)}, u32[]{:S(2)}) %copy-start) | copy-done | bytes 8388632
  45.2 5.9 %forward.1 = (f32[8,128]{1,0:T(8,128)S(1)}, f32[16,128]{1,0:T(8,128)S(1)}, f32[16,128]{1,0:T(8,128)S(1)}, f32[16,128]{1,0:T(8,128)S(1)}) custom-call(s32[16]{0:T(128)S(1)} %copy-done.4, f32[16,2,8,8192]{3,2,1,0:T(8,128)S(1)} %copy-done, f32[4,8,128]{2,1,0:T(8,128)S(1)} %get-tuple-element.25.refs_2_, f32[8,4,1024]{2,1,0:T(4,128)S(1)} %get-tuple-element.47.refs_3_, ...), custom_call_target="tpu_custom_call" | custom-call | flops 100000000 | bytes 8388608 | tf_op jit(solution)/shard_map/forward/pallas_call | solution.py:364
  51.2 1.6 %collective-permute-start.18 = (f32[16,128]{1,0:T(8,128)S(1)}, f32[16,128]{1,0:T(8,128)S(1)}, u32[]{:S(2)}, u32[]{:S(2)}) collective-permute-start(f32[16,128]{1,0:T(8,128)S(1)} %get-tuple-element.28), channel_id=1, source_target_pairs={{0,2},{1,3},{2,0},{3,1},{4,6},{5,7},{6,4},{7,5},{8,10},{9,11},{10,... | collective-permute-start | bytes 24584 | tf_op jit(solution)/shard_map/ppermute | solution.py:323
  53.1 1.9 %collective-permute-done.18.refs_5_.refs_8_ = f32[16,128]{1,0:T(8,128)S(1)} collective-permute-done((f32[16,128]{1,0:T(8,128)S(1)}, f32[16,128]{1,0:T(8,128)S(1)}, u32[]{:S(2)}, u32[]{:S(2)}) %collective-permute-start.18) | collective-permute-done | bytes 8224 | tf_op jit(solution)/shard_map/ppermute | solution.py:323
  55.9 6.4 %backward.1 = (f32[8,4,1024]{2,1,0:T(4,128)S(1)}, f32[8,4,1024]{2,1,0:T(4,128)S(1)}, f32[8,4,1024]{2,1,0:T(4,128)S(1)}, f32[8,4,1024]{2,1,0:T(4,128)S(1)}, f32[8...) custom-call(f32[16,2,8,8192]{3,2,1,0:T(8,128)S(1)} %copy-done.1, ...), custom_call_target="tpu_custom_call" | custom-call | flops 100000000 | bytes 8388608 | tf_op jit(solution)/shard_map/backward/pallas_call | solution.py:377
  62.3 1.6 %collective-permute-start.21 = (f32[8,4,1024]{2,1,0:T(4,128)S(1)}, f32[8,4,1024]{2,1,0:T(4,128)S(1)}, u32[]{:S(2)}, u32[]{:S(2)}) collective-permute-start(f32[8,4,1024]{2,1,0:T(4,128)S(1)} %get-tuple-element.33), channel_id=1, source_target_pairs={{0,4},{4,0},{8,12},{12,8},{16,20},{20,16},{24,28},{28,24},{1,5},{5... | collective-permute-start | bytes 393224 | tf_op jit(solution)/shard_map/ppermute | solution.py:323
  64.4 1.6 %collective-permute-start.25 = (f32[8,4,1024]{2,1,0:T(4,128)S(1)}, f32[8,4,1024]{2,1,0:T(4,128)}, u32[]{:S(2)}, u32[]{:S(2)}) collective-permute-start(f32[8,4,1024]{2,1,0:T(4,128)S(1)} %get-tuple-element.37), channel_id=1, source_target_pairs={{0,4},{4,0},{8,12},{12,8},{16,20},{20,16},{24,28},{28,24},{1,5},{5... | collective-permute-start | bytes 393224 | tf_op jit(solution)/shard_map/ppermute | solution.py:323
  68.7 1.6 %collective-permute-start.20 = (f32[8,4,1024]{2,1,0:T(4,128)S(1)}, f32[8,4,1024]{2,1,0:T(4,128)S(1)}, u32[]{:S(2)}, u32[]{:S(2)}) collective-permute-start(f32[8,4,1024]{2,1,0:T(4,128)S(1)} %get-tuple-element.31), channel_id=1, source_target_pairs={{0,4},{4,0},{8,12},{12,8},{16,20},{20,16},{24,28},{28,24},{1,5},{5... | collective-permute-start | bytes 393224 | tf_op jit(solution)/shard_map/ppermute | solution.py:323
  71.6 3.5 %collective-permute-start.32 = (f32[8,4,1024]{2,1,0:T(4,128)S(1)}, f32[8,4,1024]{2,1,0:T(4,128)S(1)}, u32[]{:S(2)}, u32[]{:S(2)}) collective-permute-start(f32[8,4,1024]{2,1,0:T(4,128)S(1)} %get-tuple-element.45), channel_id=1, source_target_pairs={{16,20},{20,16},{24,28},{28,24},{17,21},{21,17},{25,29},{29,25},{1... | collective-permute-start | bytes 393224 | tf_op jit(solution)/shard_map/ppermute | solution.py:323
  76.0 10.1 %collective-permute-start.22 = (f32[8,4,1024]{2,1,0:T(4,128)S(1)}, f32[8,4,1024]{2,1,0:T(4,128)}, u32[]{:S(2)}, u32[]{:S(2)}) collective-permute-start(f32[8,4,1024]{2,1,0:T(4,128)S(1)} %add.103), channel_id=1, source_target_pairs={{0,24},{4,28},{8,16},{12,20},{16,8},{20,12},{24,0},{28,4},{1,25},{... | collective-permute-start | bytes 393224 | tf_op jit(solution)/shard_map/ppermute | solution.py:323
  91.3 3.5 %collective-permute-start.27 = (f32[8,4,1024]{2,1,0:T(4,128)S(1)}, f32[8,4,1024]{2,1,0:T(4,128)S(1)}, u32[]{:S(2)}, u32[]{:S(2)}) collective-permute-start(f32[8,4,1024]{2,1,0:T(4,128)S(1)} %get-tuple-element.39), channel_id=1, source_target_pairs={{16,20},{20,16},{24,28},{28,24},{17,21},{21,17},{25,29},{29,25},{1... | collective-permute-start | bytes 393224 | tf_op jit(solution)/shard_map/ppermute | solution.py:323
  97.4 2.4 %collective-permute-start.33 = (f32[8,4,1024]{2,1,0:T(4,128)S(1)}, f32[8,4,1024]{2,1,0:T(4,128)S(1)}, u32[]{:S(2)}, u32[]{:S(2)}) collective-permute-start(f32[8,4,1024]{2,1,0:T(4,128)S(1)} %add.114), channel_id=1, source_target_pairs={{16,24},{20,28},{24,16},{28,20},{17,25},{21,29},{25,17},{29,21},{1... | collective-permute-start | bytes 393224 | tf_op jit(solution)/shard_map/ppermute | solution.py:323
  100.8 2.7 %collective-permute-done.29 = f32[8,4,1024]{2,1,0:T(4,128)S(1)} collective-permute-done((f32[8,4,1024]{2,1,0:T(4,128)S(1)}, f32[8,4,1024]{2,1,0:T(4,128)S(1)}, u32[]{:S(2)}, u32[]{:S(2)}) %collective-permute-start.29) | collective-permute-done | bytes 131104 | tf_op jit(solution)/shard_map/ppermute | solution.py:323
  103.5 5.1 %collective-permute-done.31 = f32[8,4,1024]{2,1,0:T(4,128)S(1)} collective-permute-done((f32[8,4,1024]{2,1,0:T(4,128)S(1)}, f32[8,4,1024]{2,1,0:T(4,128)S(1)}, u32[]{:S(2)}, u32[]{:S(2)}) %collective-permute-start.31) | collective-permute-done | bytes 131104 | tf_op jit(solution)/shard_map/ppermute | solution.py:323
  (95 shorter events, 34.5 us)
Async XLA Ops:
  3.5 9.8 %collective-permute-start = (f32[1,128]{1,0:T(1,128)S(1)}, f32[1,128]{1,0:T(1,128)S(1)}, u32[]{:S(2)}, u32[]{:S(2)}) collective-permute-start(f32[1,128]{1,0:T(1,128)S(1)} %fusion.16), channel_id=1, source_target_pairs={{0,1},{1,0},{2,3},{3,2},{4,5},{5,4},{6,7},{7,6},{8,9},{9,8},{10,11... | collective-permute-start | bytes 1544 | tf_op jit(solution)/shard_map/ppermute | solution.py:323
  3.5 11.1 %collective-permute-start.1 = (f32[1,128]{1,0:T(1,128)S(1)}, f32[1,128]{1,0:T(1,128)S(1)}, u32[]{:S(2)}, u32[]{:S(2)}) collective-permute-start(f32[1,128]{1,0:T(1,128)S(1)} %fusion.16), channel_id=1, source_target_pairs={{0,2},{1,3},{2,0},{3,1},{4,6},{5,7},{6,4},{7,5},{8,10},{9,11},{10,... | collective-permute-start | bytes 1544 | tf_op jit(solution)/shard_map/ppermute | solution.py:323
  5.1 11.2 %collective-permute-start.2 = (f32[1,128]{1,0:T(1,128)S(1)}, f32[1,128]{1,0:T(1,128)S(1)}, u32[]{:S(2)}, u32[]{:S(2)}) collective-permute-start(f32[1,128]{1,0:T(1,128)S(1)} %fusion.16), channel_id=1, source_target_pairs={{0,3},{1,2},{2,1},{3,0},{4,7},{5,6},{6,5},{7,4},{8,11},{9,10},{10,... | collective-permute-start | bytes 1544 | tf_op jit(solution)/shard_map/ppermute | solution.py:323
  6.4 12.0 %collective-permute-start.11 = (f32[8,4,1024]{2,1,0:T(4,128)S(1)}, f32[8,4,1024]{2,1,0:T(4,128)S(1)}, u32[]{:S(2)}, u32[]{:S(2)}) collective-permute-start(f32[8,4,1024]{2,1,0:T(4,128)S(1)} %get-tuple-element.46.refs_11_), channel_id=1, source_target_pairs={{16,24},{20,28},{24,16},{28,20},{17,25},{21,29},{25,17},{29,21},{1... | collective-permute-start | bytes 393224 | tf_op jit(solution)/shard_map/ppermute | solution.py:323
  8.7 12.5 %collective-permute-start.13 = (f32[8,4,1024]{2,1,0:T(4,128)S(1)}, f32[8,4,1024]{2,1,0:T(4,128)S(1)}, u32[]{:S(2)}, u32[]{:S(2)}) collective-permute-start(f32[8,4,1024]{2,1,0:T(4,128)S(1)} %get-tuple-element.46.refs_11_), channel_id=1, source_target_pairs={{16,0},{20,4},{24,8},{28,12},{17,1},{21,5},{25,9},{29,13},{18,2},{... | collective-permute-start | bytes 393224 | tf_op jit(solution)/shard_map/ppermute | solution.py:323
  13.3 11.4 %collective-permute-start.15 = (f32[8,4,1024]{2,1,0:T(4,128)S(1)}, f32[8,4,1024]{2,1,0:T(4,128)S(1)}, u32[]{:S(2)}, u32[]{:S(2)}) collective-permute-start(f32[8,4,1024]{2,1,0:T(4,128)S(1)} %get-tuple-element.46.refs_11_), channel_id=1, source_target_pairs={{16,8},{20,12},{24,0},{28,4},{17,9},{21,13},{25,1},{29,5},{18,10},... | collective-permute-start | bytes 393224 | tf_op jit(solution)/shard_map/ppermute | solution.py:323
  14.6 10.7 %collective-permute-start.4 = (f32[8,4,1024]{2,1,0:T(4,128)S(1)}, f32[8,4,1024]{2,1,0:T(4,128)S(1)}, u32[]{:S(2)}, u32[]{:S(2)}) collective-permute-start(f32[8,4,1024]{2,1,0:T(4,128)S(1)} %get-tuple-element.47.refs_3_), channel_id=1, source_target_pairs={{0,8},{4,12},{8,0},{12,4},{16,24},{20,28},{24,16},{28,20},{1,9},{5... | collective-permute-start | bytes 393224 | tf_op jit(solution)/shard_map/ppermute | solution.py:323
  16.2 13.4 %collective-permute-start.6 = (f32[8,4,1024]{2,1,0:T(4,128)S(1)}, f32[8,4,1024]{2,1,0:T(4,128)S(1)}, u32[]{:S(2)}, u32[]{:S(2)}) collective-permute-start(f32[8,4,1024]{2,1,0:T(4,128)S(1)} %get-tuple-element.47.refs_3_), channel_id=1, source_target_pairs={{0,16},{4,20},{8,24},{12,28},{16,0},{20,4},{24,8},{28,12},{1,17},{... | collective-permute-start | bytes 393224 | tf_op jit(solution)/shard_map/ppermute | solution.py:323
  18.4 12.0 %collective-permute-start.8 = (f32[8,4,1024]{2,1,0:T(4,128)S(1)}, f32[8,4,1024]{2,1,0:T(4,128)S(1)}, u32[]{:S(2)}, u32[]{:S(2)}) collective-permute-start(f32[8,4,1024]{2,1,0:T(4,128)S(1)} %get-tuple-element.47.refs_3_), channel_id=1, source_target_pairs={{0,24},{4,28},{8,16},{12,20},{16,8},{20,12},{24,0},{28,4},{1,25},{... | collective-permute-start | bytes 393224 | tf_op jit(solution)/shard_map/ppermute | solution.py:323
  21.3 9.8 %collective-permute-start.10 = (f32[8,4,1024]{2,1,0:T(4,128)S(1)}, f32[8,4,1024]{2,1,0:T(4,128)S(1)}, u32[]{:S(2)}, u32[]{:S(2)}) collective-permute-start(f32[8,4,1024]{2,1,0:T(4,128)S(1)} %get-tuple-element.46.refs_11_), channel_id=1, source_target_pairs={{16,20},{20,16},{24,28},{28,24},{17,21},{21,17},{25,29},{29,25},{1... | collective-permute-start | bytes 393224 | tf_op jit(solution)/shard_map/ppermute | solution.py:323
  25.3 9.3 %collective-permute-start.12 = (f32[8,4,1024]{2,1,0:T(4,128)S(1)}, f32[8,4,1024]{2,1,0:T(4,128)S(1)}, u32[]{:S(2)}, u32[]{:S(2)}) collective-permute-start(f32[8,4,1024]{2,1,0:T(4,128)S(1)} %collective-permute-done.11.refs_13_), channel_id=1, source_target_pairs={{16,20},{20,16},{24,28},{28,24},{17,21},{21,17},{25,29},{29,25},{1... | collective-permute-start | bytes 393224 | tf_op jit(solution)/shard_map/ppermute | solution.py:323
  29.7 10.7 %collective-permute-start.14 = (f32[8,4,1024]{2,1,0:T(4,128)S(1)}, f32[8,4,1024]{2,1,0:T(4,128)S(1)}, u32[]{:S(2)}, u32[]{:S(2)}) collective-permute-start(f32[8,4,1024]{2,1,0:T(4,128)S(1)} %collective-permute-done.13.refs_15_), channel_id=1, source_target_pairs={{0,4},{4,0},{8,12},{12,8},{1,5},{5,1},{9,13},{13,9},{2,6},{6,2},{1... | collective-permute-start | bytes 393224 | tf_op jit(solution)/shard_map/ppermute | solution.py:323
  30.4 10.0 %collective-permute-start.16 = (f32[8,4,1024]{2,1,0:T(4,128)S(1)}, f32[8,4,1024]{2,1,0:T(4,128)S(1)}, u32[]{:S(2)}, u32[]{:S(2)}) collective-permute-start(f32[8,4,1024]{2,1,0:T(4,128)S(1)} %collective-permute-done.15.refs_17_), channel_id=1, source_target_pairs={{0,4},{4,0},{8,12},{12,8},{1,5},{5,1},{9,13},{13,9},{2,6},{6,2},{1... | collective-permute-start | bytes 393224 | tf_op jit(solution)/shard_map/ppermute | solution.py:323
  64.4 11.6 %collective-permute-start.25 = (f32[8,4,1024]{2,1,0:T(4,128)S(1)}, f32[8,4,1024]{2,1,0:T(4,128)}, u32[]{:S(2)}, u32[]{:S(2)}) collective-permute-start(f32[8,4,1024]{2,1,0:T(4,128)S(1)} %get-tuple-element.37), channel_id=1, source_target_pairs={{0,4},{4,0},{8,12},{12,8},{16,20},{20,16},{24,28},{28,24},{1,5},{5... | collective-permute-start | bytes 393224 | tf_op jit(solution)/shard_map/ppermute | solution.py:323
  65.9 21.1 %collective-permute-start.28 = (f32[8,4,1024]{2,1,0:T(4,128)S(1)}, f32[8,4,1024]{2,1,0:T(4,128)S(1)}, u32[]{:S(2)}, u32[]{:S(2)}) collective-permute-start(f32[8,4,1024]{2,1,0:T(4,128)S(1)} %get-tuple-element.41), channel_id=1, source_target_pairs={{0,4},{4,0},{8,12},{12,8},{1,5},{5,1},{9,13},{13,9},{2,6},{6,2},{1... | collective-permute-start | bytes 393224 | tf_op jit(solution)/shard_map/ppermute | solution.py:323
  66.6 21.2 %collective-permute-start.30 = (f32[8,4,1024]{2,1,0:T(4,128)S(1)}, f32[8,4,1024]{2,1,0:T(4,128)S(1)}, u32[]{:S(2)}, u32[]{:S(2)}) collective-permute-start(f32[8,4,1024]{2,1,0:T(4,128)S(1)} %get-tuple-element.43), channel_id=1, source_target_pairs={{0,4},{4,0},{8,12},{12,8},{1,5},{5,1},{9,13},{13,9},{2,6},{6,2},{1... | collective-permute-start | bytes 393224 | tf_op jit(solution)/shard_map/ppermute | solution.py:323
  68.7 26.1 %collective-permute-start.20 = (f32[8,4,1024]{2,1,0:T(4,128)S(1)}, f32[8,4,1024]{2,1,0:T(4,128)S(1)}, u32[]{:S(2)}, u32[]{:S(2)}) collective-permute-start(f32[8,4,1024]{2,1,0:T(4,128)S(1)} %get-tuple-element.31), channel_id=1, source_target_pairs={{0,4},{4,0},{8,12},{12,8},{16,20},{20,16},{24,28},{28,24},{1,5},{5... | collective-permute-start | bytes 393224 | tf_op jit(solution)/shard_map/ppermute | solution.py:323
  71.6 19.7 %collective-permute-start.32 = (f32[8,4,1024]{2,1,0:T(4,128)S(1)}, f32[8,4,1024]{2,1,0:T(4,128)S(1)}, u32[]{:S(2)}, u32[]{:S(2)}) collective-permute-start(f32[8,4,1024]{2,1,0:T(4,128)S(1)} %get-tuple-element.45), channel_id=1, source_target_pairs={{16,20},{20,16},{24,28},{28,24},{17,21},{21,17},{25,29},{29,25},{1... | collective-permute-start | bytes 393224 | tf_op jit(solution)/shard_map/ppermute | solution.py:323
  76.0 20.1 %collective-permute-start.22 = (f32[8,4,1024]{2,1,0:T(4,128)S(1)}, f32[8,4,1024]{2,1,0:T(4,128)}, u32[]{:S(2)}, u32[]{:S(2)}) collective-permute-start(f32[8,4,1024]{2,1,0:T(4,128)S(1)} %add.103), channel_id=1, source_target_pairs={{0,24},{4,28},{8,16},{12,20},{16,8},{20,12},{24,0},{28,4},{1,25},{... | collective-permute-start | bytes 393224 | tf_op jit(solution)/shard_map/ppermute | solution.py:323
  87.1 10.4 %collective-permute-start.24 = (f32[8,4,1024]{2,1,0:T(4,128)S(1)}, f32[8,4,1024]{2,1,0:T(4,128)}, u32[]{:S(2)}, u32[]{:S(2)}) collective-permute-start(f32[8,4,1024]{2,1,0:T(4,128)S(1)} %add.105), channel_id=1, source_target_pairs={{0,16},{4,20},{8,24},{12,28},{16,0},{20,4},{24,8},{28,12},{1,17},{... | collective-permute-start | bytes 393224 | tf_op jit(solution)/shard_map/ppermute | solution.py:323
  87.7 12.1 %collective-permute-start.26 = (f32[8,4,1024]{2,1,0:T(4,128)S(1)}, f32[8,4,1024]{2,1,0:T(4,128)S(1)}, u32[]{:S(2)}, u32[]{:S(2)}) collective-permute-start(f32[8,4,1024]{2,1,0:T(4,128)S(1)} %add.107), channel_id=1, source_target_pairs={{0,8},{4,12},{8,0},{12,4},{16,24},{20,28},{24,16},{28,20},{1,9},{5... | collective-permute-start | bytes 393224 | tf_op jit(solution)/shard_map/ppermute | solution.py:323
  91.3 9.5 %collective-permute-start.27 = (f32[8,4,1024]{2,1,0:T(4,128)S(1)}, f32[8,4,1024]{2,1,0:T(4,128)S(1)}, u32[]{:S(2)}, u32[]{:S(2)}) collective-permute-start(f32[8,4,1024]{2,1,0:T(4,128)S(1)} %get-tuple-element.39), channel_id=1, source_target_pairs={{16,20},{20,16},{24,28},{28,24},{17,21},{21,17},{25,29},{29,25},{1... | collective-permute-start | bytes 393224 | tf_op jit(solution)/shard_map/ppermute | solution.py:323
  96.1 12.5 %collective-permute-start.31 = (f32[8,4,1024]{2,1,0:T(4,128)S(1)}, f32[8,4,1024]{2,1,0:T(4,128)S(1)}, u32[]{:S(2)}, u32[]{:S(2)}) collective-permute-start(f32[8,4,1024]{2,1,0:T(4,128)S(1)} %add.112), channel_id=1, source_target_pairs={{0,16},{4,20},{8,24},{12,28},{1,17},{5,21},{9,25},{13,29},{2,18},{... | collective-permute-start | bytes 393224 | tf_op jit(solution)/shard_map/ppermute | solution.py:323
  97.4 11.2 %collective-permute-start.33 = (f32[8,4,1024]{2,1,0:T(4,128)S(1)}, f32[8,4,1024]{2,1,0:T(4,128)S(1)}, u32[]{:S(2)}, u32[]{:S(2)}) collective-permute-start(f32[8,4,1024]{2,1,0:T(4,128)S(1)} %add.114), channel_id=1, source_target_pairs={{16,24},{20,28},{24,16},{28,20},{17,25},{21,29},{25,17},{29,21},{1... | collective-permute-start | bytes 393224 | tf_op jit(solution)/shard_map/ppermute | solution.py:323
  (17 other events, 181.9 us)

commit v2 on v0

v2 whole, which is shorter than its diff:
```python
import math

import jax
import jax.numpy as jnp
from jax import lax
from jax.experimental import pallas as pl
from jax.experimental.pallas import tpu as pltpu
from jax.sharding import PartitionSpec as P

HIGHEST = lax.Precision.HIGHEST
LANES = 128
VMEM = pltpu.VMEM
MIB = 1024 * 1024


def needed(block, first_slot, width, stratum):
    return (block + 1) * width > stratum * first_slot


def ring_of(blocks):
    return list(range(0, blocks, 2)) + list(range(blocks - 1, 0, -2))


def ring_place(block, blocks):
    return jnp.where(block % 2 == 0, block // 2, blocks - 1 - block // 2)


def block_at(place, blocks):
    place = lax.rem(place + 2 * blocks, blocks)
    return jnp.where(place < blocks // 2, 2 * place, 2 * (blocks - 1 - place) + 1)


def sin_pi(x):
    turns = jnp.round(x)
    y = (x - turns) * math.pi
    z = y * y
    value = -1.0 / 39916800
    for term in (1.0 / 362880, -1.0 / 5040, 1.0 / 120, -1.0 / 6, 1.0):
        value = value * z + term
    value = value * y
    return jnp.where(turns.astype(jnp.int32) % 2 != 0, -value, value)


def half_turns(order, step, length):
    total = order * step
    period = 2 * length
    scale = 0.5 / length.astype(jnp.float32)
    for _ in range(2):
        total = total - jnp.floor(total.astype(jnp.float32) * scale).astype(jnp.int32) * period
    return total.astype(jnp.float32) / length.astype(jnp.float32)


def pixel_mask(shape, length):
    pixel = lax.broadcasted_iota(jnp.int32, shape, 0) // 2 * shape[1]
    pixel = pixel + lax.broadcasted_iota(jnp.int32, shape, 1)
    return pixel < length


def meta_kernel(slots, cycles, ids, length, offset, weight, out_ref, *scratch):
    *held, sems = scratch
    copies = [
        pltpu.make_async_copy(source, target, sems.at[k])
        for k, (source, target) in enumerate(zip((ids, length, offset, weight), held))
    ]
    for copy in copies:
        copy.start()
    for copy in copies:
        copy.wait()
    lane = lax.broadcasted_iota(jnp.int32, (1, LANES), 1)
    out = jnp.zeros((1, LANES), jnp.float32)
    for m in range(slots):
        out = jnp.where(lane == m, held[0][m].astype(jnp.float32), out)
    for c in range(cycles):
        for k in range(3):
            value = held[1 + k][c].astype(jnp.float32)
            out = jnp.where(lane == slots + k * cycles + c, value, out)
    out_ref[...] = out


def entry(meta, at):
    return meta[:, at : at + 1]


def spread_ids(metas, slots, sources):
    per = LANES // slots
    lane = lax.broadcasted_iota(jnp.int32, (1, LANES), 1)
    pieces = []
    for start in range(0, len(sources), per):
        piece = jnp.zeros((1, LANES), jnp.float32)
        for k in range(per):
            value = metas[sources[start + k]]
            value = pltpu.roll(value, k * slots, 1) if k else value
            piece = jnp.where(lane // slots == k, value, piece)
        pieces.append(piece)
    return jnp.concatenate(pieces, axis=1)


def sky_kernel(normalise, groups, slots, cycles, *rest):
    metas = [ref[...] for ref in rest[:groups]]
    sky_ref, legendre = rest[groups : groups + 2]
    pieces_ref, gram_ref, acs_ref, asc_ref, fine_ref, tables, sems = rest[groups + 2 :]
    copies = table_copies(legendre, tables, sems)
    for copy in copies:
        copy.start()
    me = lax.axis_index("order")
    rows, both = acs_ref.shape[1:]
    every = both // 2
    ids = spread_ids(metas, slots, [d for _ in range(2) for d in range(groups)])
    ids = ids.astype(jnp.int32)
    row8 = lax.broadcasted_iota(jnp.int32, (8, both), 0)
    sums = [jnp.zeros((8, both), jnp.float32) for _ in range(4)]
    for c in range(cycles):
        length = entry(metas[0], slots + c).astype(jnp.int32)
        offset = entry(metas[0], slots + cycles + c).astype(jnp.int32)
        coarse = lax.broadcasted_iota(jnp.int32, (rows, both), 0) // 2 * (2 * LANES) + offset
        x = half_turns(ids, coarse, length)
        first = lax.broadcasted_iota(jnp.int32, (rows, both), 1) < every
        acs = sin_pi(x + jnp.where(first, 0.5, 1.0))
        asc = sin_pi(x + jnp.where(first, 0.0, 0.5))
        acs_ref[c] = acs
        asc_ref[c] = asc
        fine = 2 * lax.broadcasted_iota(jnp.int32, (LANES, both), 0)
        x = half_turns(ids, fine, length)
        first = lax.broadcasted_iota(jnp.int32, (LANES, both), 1) < every
        table = sin_pi(x + jnp.where(first, 0.5, 0.0))
        fine_ref[c] = table
        section = jnp.where(pixel_mask((rows, LANES), length), sky_ref[c], 0.0)
        spun = jnp.dot(section, table, precision=HIGHEST, preferred_element_type=jnp.float32)
        weight = entry(metas[0], slots + 2 * cycles + c) * normalise
        for k, value in enumerate((spun * acs, spun * asc)):
            value = sum(value[8 * i : 8 * i + 8] for i in range(rows // 8))
            for q in range(2):
                total = jnp.sum(jnp.where(row8 % 2 == q, value, 0.0), axis=0, keepdims=True)
                total = total * (-weight if k else weight)
                sums[2 * q + k] = jnp.where(row8 == c, total, sums[2 * q + k])
    source = lax.broadcasted_iota(jnp.int32, (both, LANES), 0) % every
    lane = lax.broadcasted_iota(jnp.int32, (both, LANES), 1)
    for d in range(groups):
        piece = jnp.zeros((8, LANES), jnp.float32)
        for a in range(4):
            place = ((lane - a * slots) == (source - d * slots)) & (lane // slots == a)
            piece = piece + jnp.dot(
                sums[a], place.astype(jnp.float32), precision=HIGHEST,
                preferred_element_type=jnp.float32,
            )
        pieces_ref[d] = piece
    count, wide = gram_ref.shape[1:]
    row = lax.broadcasted_iota(jnp.int32, (count, wide), 0)
    length = jnp.ones((count, wide), jnp.float32)
    offset = jnp.zeros((count, wide), jnp.float32)
    weight = jnp.zeros((count, wide), jnp.float32)
    for d in range(groups):
        for c in range(cycles):
            here = row == (me ^ d) * cycles + c
            length = jnp.where(here, entry(metas[d], slots + c), length)
            offset = jnp.where(here, entry(metas[d], slots + cycles + c), offset)
            weight = jnp.where(here, entry(metas[d], slots + 2 * cycles + c), weight)
    others = spread_ids(metas, slots, [d for d in range(groups) for _ in range(4)])
    lane = lax.broadcasted_iota(jnp.int32, (count, wide), 1)
    cosine = (lane // slots) % 2 == 0
    factor = jnp.where(others == 0.0, 0.5, 1.0) * normalise * weight * length
    inverse = 1.0 / length
    odd = offset > 0.5

    def response(n):
        turns = jnp.round(n * inverse)
        sign = jnp.where(odd & (turns.astype(jnp.int32) % 2 != 0), -1.0, 1.0)
        return jnp.where(turns * length == n, sign, 0.0)

    for m in range(slots):
        mine = entry(metas[0], m)
        near = response(mine - others)
        far = response(mine + others)
        gram_ref[m] = factor * (near + jnp.where(cosine, far, -far))
    for copy in copies:
        copy.wait()


def table_copies(legendre, tables, sems):
    slots, _, _, degrees = tables.shape
    copies = []
    for m in range(slots):
        first = m * (degrees // slots)
        part = (m, slice(None), slice(None), pl.ds(first, degrees - first))
        copies.append(pltpu.make_async_copy(legendre.at[part], tables.at[part], sems.at[m]))
    return copies


def forward_kernel(layout, groups, meta_ref, tables, pieces_ref, *rest):
    parts = rest[: len(layout)]
    phases_ref, *messages, coefs = rest[len(layout) :]
    slots, _, count, degrees = tables.shape
    width = parts[0].shape[2]
    blocks = degrees // width
    stratum = degrees // slots
    meta = meta_ref[...]
    place = ring_place(lax.axis_index("blk"), blocks)
    for part, (low, step) in zip(parts, layout):
        first = pl.multiple_of(block_at(place + step, blocks) * width, LANES)
        for m in range(part.shape[0]):
            coefs[low + m, :, pl.ds(first, width)] = part[m]
    lane = lax.broadcasted_iota(jnp.int32, (count, LANES), 1)
    phases = jnp.zeros((count, LANES), jnp.float32)
    for m in range(slots):
        floor = jnp.maximum(entry(meta, m).astype(jnp.int32), 2)
        first = stratum * m // LANES
        p = [jnp.zeros((count, LANES), jnp.float32)] * 4
        n = [jnp.zeros((count, LANES), jnp.float32)] * 4
        for t in range(first, degrees // LANES):
            span = slice(t * LANES, (t + 1) * LANES)
            plus = tables[m, 0, :, span]
            minus = tables[m, 1, :, span]
            if t * LANES < stratum * (m + 1):
                keep = lane >= floor - t * LANES
                plus = jnp.where(keep, plus, 0.0)
                minus = jnp.where(keep, minus, 0.0)
            for a in range(4):
                c = coefs[m, a : a + 1, span]
                if t * LANES < stratum * (m + 1):
                    c = jnp.where(keep[:1], c, 0.0)
                p[a] = p[a] + plus * c
                n[a] = n[a] + minus * c
        for a, total in enumerate([n[3] - p[0], -p[1] - n[2], -p[2] - n[1], n[0] - p[3]]):
            value = jnp.sum(total, axis=1, keepdims=True)
            phases = jnp.where(lane == a * slots + m, value, phases)
    phases_ref[...] = phases
    for d in range(1, groups):
        messages[d - 1][:count] = phases
        messages[d - 1][count:] = pieces_ref[d]


def fold_rows(values, row):
    for step in (1, 2, 4):
        low = (row & step) == 0
        values = [
            jnp.where(low, values[i], values[i + 1])
            + pltpu.roll(jnp.where(low, values[i + 1], values[i]), step, 0)
            for i in range(0, len(values), 2)
        ]
    return values[0]


def backward_kernel(groups, cycles, tables, gram_ref, pieces_ref, phases_ref, *rest):
    messages = rest[: groups - 1]
    out, low_ref, high_ref, sky = rest[groups - 1 :]
    slots, _, count, degrees = tables.shape
    blocks, _, _, width = out.shape
    stratum = degrees // slots
    place = ring_place(lax.axis_index("blk"), blocks)
    owner = lax.axis_index("order")
    ring = ring_of(blocks)
    step_of = [lax.rem(ring.index(b) - place + blocks, blocks) for b in range(blocks)]
    wide = 4 * slots
    pairs = []
    for d in range(groups):
        phases = phases_ref[...] if d == 0 else messages[d - 1][:count]
        piece = pieces_ref[0] if d == 0 else messages[d - 1][count:]
        sky[pl.ds((owner ^ d) * cycles, cycles)] = piece[:cycles]
        pairs.append(phases)
    lane = lax.broadcasted_iota(jnp.int32, (count, LANES), 1)
    row8 = lax.broadcasted_iota(jnp.int32, (8, LANES), 0)
    per = LANES // wide
    packed = []
    for start in range(0, groups, per):
        value = pairs[start]
        for k in range(1, per):
            value = jnp.where(
                lane // wide == k, pltpu.roll(pairs[start + k], k * wide, 1), value
            )
        packed.append(value)
    observed = sky[...]
    for m in range(slots):
        total = jnp.where((lane < wide) & (lane % slots == m), observed, 0.0)
        for k, value in enumerate(packed):
            total = total - gram_ref[m, :, k * LANES : (k + 1) * LANES] * value
        an = []
        for a in range(4):
            value = jnp.where((lane % wide) // slots == a, total, 0.0)
            value = jnp.sum(value, axis=1, keepdims=True)
            an.append(jnp.broadcast_to(value, (count, LANES)))
        ng = [-value for value in an]
        for t in range(stratum * m // LANES, degrees // LANES, 2):
            values = []
            for u in (t, t + 1):
                span = slice(u * LANES, (u + 1) * LANES)
                plus = tables[m, 0, :, span]
                minus = tables[m, 1, :, span]
                four = [
                    plus * ng[0] + minus * an[3],
                    plus * ng[1] + minus * ng[2],
                    plus * ng[2] + minus * ng[1],
                    plus * ng[3] + minus * an[0],
                ]
                values += [
                    sum(v[8 * k : 8 * k + 8] for k in range(count // 8)) for v in four
                ]
            folded = fold_rows(values, row8)
            for k, u in enumerate((t, t + 1)):
                step = step_of[u * LANES // width]
                inner = u * LANES % width
                out[step, m, :, inner : inner + LANES] = folded[4 * k : 4 * k + 4]
    middle = low_ref.shape[0]
    low_ref[...] = out[blocks // 2, :middle]
    high_ref[...] = out[blocks // 2, middle:]


def residual_kernel(groups, slots, cycles, *rest):
    metas = [ref[...] for ref in rest[:groups]]
    sky_ref, acs_ref, asc_ref, fine_ref, phases_ref = rest[groups : groups + 5]
    messages = rest[groups + 5 : 2 * groups + 4]
    out_ref, spread = rest[2 * groups + 4 :]
    owner = lax.axis_index("order")
    rows, both = acs_ref.shape[1:]
    every = both // 2
    count = phases_ref.shape[0]
    source = lax.broadcasted_iota(jnp.int32, (LANES, both), 0)
    lane = lax.broadcasted_iota(jnp.int32, (LANES, both), 1) % every
    ids = spread_ids(metas, slots, [d for _ in range(2) for d in range(groups)])
    factor = jnp.where(ids == 0.0, 1.0, 2.0)
    for a in range(4):
        total = jnp.zeros((count, both), jnp.float32)
        for d in range(groups):
            phases = phases_ref[...] if d == 0 else messages[d - 1][:count]
            place = (lane - d * slots == source - a * slots) & (lane // slots == d)
            total = total + jnp.dot(
                phases, place.astype(jnp.float32), precision=HIGHEST,
                preferred_element_type=jnp.float32,
            )
        spread[a] = total * factor
    even = lax.broadcasted_iota(jnp.int32, (rows, both), 0) % 2 == 0
    for c in range(cycles):
        q_re, q_im, u_re, u_im = [spread[a, pl.ds(owner * cycles + c, 1)] for a in range(4)]
        weights = jnp.where(even, q_re, u_re) * acs_ref[c]
        weights = weights - jnp.where(even, q_im, u_im) * asc_ref[c]
        model = lax.dot_general(
            weights, fine_ref[c], (((1,), (1,)), ((), ())), precision=HIGHEST,
            preferred_element_type=jnp.float32,
        )
        inside = pixel_mask((rows, LANES), entry(metas[0], slots + c).astype(jnp.int32))
        out_ref[c] = jnp.where(inside, sky_ref[c] - model, 0.0)


def add_kernel(index, piece_ref, value_ref, out_ref, first=0):
    size = value_ref.shape[0]
    slots = out_ref.shape[0]
    out_ref[first : first + size] = piece_ref[index, first : first + size] + value_ref[...]
    if first:
        out_ref[:first] = piece_ref[index, :first]
    if first + size < slots:
        out_ref[first + size :] = piece_ref[index, first + size :]


def final_kernel(meta_ref, harmonics_ref, piece_ref, ahead_ref, behind_ref, out_ref):
    slots, parts, width = out_ref.shape
    start = lax.axis_index("blk") * width
    degree = start + lax.broadcasted_iota(jnp.int32, (parts, width), 1)
    meta = meta_ref[...]
    for m in range(slots):
        update = piece_ref[0, m] + ahead_ref[m] + behind_ref[m]
        valid = degree >= jnp.maximum(entry(meta, m).astype(jnp.int32), 2)
        out_ref[m] = jnp.where(valid, harmonics_ref[m] + update, 0.0)


def vmem():
    return pl.BlockSpec(memory_space=VMEM)


def shape(*dims):
    return jax.ShapeDtypeStruct(dims, jnp.float32)


def body(harmonics, legendre, sky_map, cycle_length, cycle_offset, cycle_weight, order_ids):
    groups = lax.axis_size("order")
    blocks = lax.axis_size("blk")
    slots, _, width = harmonics.shape
    count, degrees = legendre.shape[2:]
    cycles, _, pixels = sky_map.shape
    rows = pixels // LANES
    stratum = degrees // slots
    every = slots * groups
    normalise = math.sqrt(degrees * every / (cycles * groups * blocks * pixels))

    def swap(value, axis, step):
        size = lax.axis_size(axis)
        return lax.ppermute(value, axis, [(i, i ^ step) for i in range(size)])

    ring = ring_of(blocks)

    def turn(value, way, step, first=0):
        pairs = [
            (ring[p], ring[(p + way) % blocks])
            for p in range(blocks)
            if needed(ring[(p + step) % blocks], first, width, stratum)
        ]
        return lax.ppermute(value, "blk", pairs)

    hbm = pl.BlockSpec(memory_space=pl.ANY)
    small = (order_ids, cycle_length, cycle_offset, cycle_weight)
    meta = pl.pallas_call(
        lambda *refs: meta_kernel(slots, cycles, *refs),
        out_shape=pltpu.VMEM((1, LANES), jnp.float32),
        in_specs=[hbm] * 4,
        out_specs=vmem(),
        scratch_shapes=[pltpu.SMEM(v.shape, v.dtype) for v in small]
        + [pltpu.SemaphoreType.DMA((len(small),))],
        compiler_params=pltpu.CompilerParams(vmem_limit_bytes=2 * MIB),
        name="meta",
    )(*[pltpu.with_memory_space_constraint(v, pltpu.HBM) for v in small])
    harmonics, meta = lax.optimization_barrier((harmonics, meta))
    metas = [meta] + [swap(meta, "order", d) for d in range(1, groups)]

    far = blocks // 2
    middle = slots // 2
    ahead, behind = turn(harmonics, 1, 0), turn(harmonics, -1, 0)
    parts, layout = [harmonics, ahead, behind], [(0, 0), (0, -1), (0, 1)]
    ahead, behind, *metas = lax.optimization_barrier((ahead, behind, *metas))

    sky = sky_map.reshape(cycles, 2, rows, LANES).transpose(0, 2, 1, 3)
    sky = sky.reshape(cycles, 2 * rows, LANES)
    pieces, gram, acs, asc, fine, tables = pl.pallas_call(
        lambda *refs: sky_kernel(normalise, groups, slots, cycles, *refs),
        out_shape=(
            shape(groups, 8, LANES),
            shape(slots, count, 4 * every),
            shape(cycles, 2 * rows, 2 * every),
            shape(cycles, 2 * rows, 2 * every),
            shape(cycles, LANES, 2 * every),
            pltpu.VMEM(legendre.shape, jnp.float32),
        ),
        in_specs=[vmem()] * (groups + 1) + [hbm],
        out_specs=(vmem(), vmem(), vmem(), vmem(), vmem(), hbm),
        scratch_shapes=[pltpu.SemaphoreType.DMA((slots,))],
        compiler_params=pltpu.CompilerParams(vmem_limit_bytes=16 * MIB),
        cost_estimate=pl.CostEstimate(flops=10**8, bytes_accessed=12 * MIB, transcendentals=0),
        name="sky_analysis",
    )(
        *metas, sky,
        pltpu.with_memory_space_constraint(legendre, pltpu.HBM),
    )

    for k in range(2, far):
        ahead, behind = turn(ahead, 1, 1 - k), turn(behind, -1, k - 1)
        parts += [ahead, behind]
        layout += [(0, -k), (0, k)]
        if k == 2:
            ahead, behind, pieces = lax.optimization_barrier((ahead, behind, pieces))
    parts += [turn(ahead[:middle], 1, 1 - far), turn(behind[middle:], -1, far - 1, middle)]
    layout += [(0, far), (middle, far)]

    outs = pl.pallas_call(
        lambda *refs: forward_kernel(layout, groups, *refs),
        out_shape=[shape(count, LANES)] + [shape(count + 8, LANES)] * (groups - 1),
        in_specs=[vmem()] * (3 + len(parts)),
        out_specs=[vmem()] * groups,
        scratch_shapes=[pltpu.VMEM((slots, 4, degrees), jnp.float32)],
        compiler_params=pltpu.CompilerParams(vmem_limit_bytes=24 * MIB),
        cost_estimate=pl.CostEstimate(flops=10**8, bytes_accessed=8 * MIB, transcendentals=0),
        name="forward",
    )(meta, tables, pieces, *parts)
    phases = outs[0]
    messages = [swap(outs[d], "order", d) for d in range(1, groups)]

    half = pltpu.VMEM((middle, 4, width), jnp.float32)
    block = pltpu.VMEM((slots, 4, width), jnp.float32)
    piece, low_part, high_part = pl.pallas_call(
        lambda *refs: backward_kernel(groups, cycles, *refs),
        out_shape=[pltpu.VMEM((blocks, slots, 4, width), jnp.float32), half, half],
        in_specs=[vmem()] * (3 + groups),
        out_specs=[vmem()] * 3,
        scratch_shapes=[pltpu.VMEM((count, LANES), jnp.float32)],
        compiler_params=pltpu.CompilerParams(vmem_limit_bytes=24 * MIB),
        cost_estimate=pl.CostEstimate(flops=10**8, bytes_accessed=8 * MIB, transcendentals=0),
        name="backward",
    )(tables, gram, pieces, phases, *messages)

    def add(index, value, first=0):
        return pl.pallas_call(
            lambda *refs: add_kernel(index, *refs, first=first),
            out_shape=block,
            in_specs=[vmem()] * 2,
            out_specs=vmem(),
            compiler_params=pltpu.CompilerParams(vmem_limit_bytes=4 * MIB),
            cost_estimate=pl.CostEstimate(flops=10**5, bytes_accessed=10**6, transcendentals=0),
            name="add",
        )(piece, pltpu.with_memory_space_constraint(value, pltpu.VMEM))

    ahead, behind = turn(low_part, 1, far), turn(high_part, -1, -far, middle)
    ahead, behind = add(far - 1, ahead), add(far + 1, behind, middle)
    for k in reversed(range(1, far)):
        ahead, behind = turn(ahead, 1, k), turn(behind, -1, -k)
        if k > 1:
            ahead, behind = add(k - 1, ahead), add(blocks - k + 1, behind)
    refined = pl.pallas_call(
        final_kernel,
        out_shape=shape(*harmonics.shape),
        in_specs=[vmem()] * 5,
        out_specs=vmem(),
        compiler_params=pltpu.CompilerParams(vmem_limit_bytes=8 * MIB),
        cost_estimate=pl.CostEstimate(flops=10**5, bytes_accessed=10**6, transcendentals=0),
        name="refine",
    )(
        meta, harmonics, piece,
        pltpu.with_memory_space_constraint(ahead, pltpu.VMEM),
        pltpu.with_memory_space_constraint(behind, pltpu.VMEM),
    )

    residual = pl.pallas_call(
        lambda *refs: residual_kernel(groups, slots, cycles, *refs),
        out_shape=shape(cycles, 2 * rows, LANES),
        in_specs=[vmem()] * (4 + 2 * groups),
        out_specs=vmem(),
        scratch_shapes=[pltpu.VMEM((4, count, 2 * every), jnp.float32)],
        compiler_params=pltpu.CompilerParams(vmem_limit_bytes=16 * MIB),
        cost_estimate=pl.CostEstimate(flops=10**8, bytes_accessed=2 * MIB, transcendentals=0),
        name="residual",
    )(*metas, sky, acs, asc, fine, phases, *messages)
    residual = residual.reshape(cycles, rows, 2, LANES).transpose(0, 2, 1, 3)
    return (refined, residual.reshape(sky_map.shape))


def solution(mesh):
    return jax.shard_map(
        body,
        mesh=mesh,
        in_specs=(
            P("order", None, "blk"),
            P("order", None, "blk", None),
            P(("blk", "order"), None, None),
            P(("blk", "order")),
            P(("blk", "order")),
            P(("blk", "order")),
            P("order"),
        ),
        out_specs=(P("order", None, "blk"), P(("blk", "order"), None, None)),
        check_vma=False,
    )
```

time: 494 us -> 73.6 us (0.15)
  other arithmetic: 134 us -> 0 us
  waiting for transfers between devices: 134 us -> 34.5 us
  local copies, waits for them, and re-layouts: 98.1 us -> 0.98 us
  matrix products: 90.6 us -> 0 us
  starting transfers between devices: 3.3 us -> 25.6 us
  between operations: 14.9 us -> 0.74 us
  blocking collectives: 12.4 us -> 0 us
  Pallas kernels: 0 us -> 11.5 us
  loops' own time: 5.14 us -> 0 us
    cos x16 -> x0, other arithmetic: 111 us -> none  [cycle_tables(): return (jnp.concatenate([jnp.cos(angles), jnp.sin(angles)], axis=0), inside)]
    unnamed x28 -> x6, local copies, waits for them, and re-layouts: 93.2 us -> 0.96 us
    dot_general x34 -> x0, matrix products: 90.6 us -> none  [the longest x1 57.8 us: body(): jnp.einsum('mtrl,mcl->mtcr', legendre, section * keep_mask[:, None, :], p...]
    unnamed x3 -> x0, waiting for transfers between devices: 86.4 us -> none
    all_gather x1 -> x0, waiting for transfers between devices: 44.4 us -> none  [body(): section = lax.all_gather(harmonics, 'blk', axis=2, tiled=True)]
    ppermute x0 -> x22, waiting for transfers between devices: none -> 34.5 us  [the longest x16 29 us: turn(): return lax.ppermute(value, 'blk', pairs)]
    ppermute x0 -> x22, starting transfers between devices: none -> 25.6 us  [the longest x16 21.6 us: turn(): return lax.ppermute(value, 'blk', pairs)]
    pallas_call x0 -> x12, Pallas kernels: none -> 11.5 us  [the longest x1 3.58 us: body(): pl.pallas_call(lambda *refs: sky_kernel(normalise, groups, slots, cycles,...]
  transfers between devices with their start and end apart: 3 -> 22, of which waited for: 3 -> 16; matrix products, arithmetic and copies ran while one was open for 1% -> 0% of each run, Pallas kernels for 0% -> 8%
where the time goes in v2:
time: 73.6 us; the launch traced here: 73.4 us
  waiting for transfers between devices  34.5 us (47%)
  starting transfers between devices  25.6 us (35%)
  Pallas kernels  11.5 us (16%)
  local copies, waits for them, and re-layouts  0.98 us (1%)
  between operations  0.74 us (1%)
    ppermute x16, waiting for transfers between devices, turn(): return lax.ppermute(value, 'blk', pairs)  29 us
    ppermute x16, starting transfers between devices, turn(): return lax.ppermute(value, 'blk', pairs)  21.6 us
    ppermute x6, waiting for transfers between devices, swap(): return lax.ppermute(value, axis, [(i, i ^ step) for i in range(size)])  5.59 us
    ppermute x6, starting transfers between devices, swap(): return lax.ppermute(value, axis, [(i, i ^ step) for i in range(size)])  3.98 us
    pallas_call x1, Pallas kernels, body(): pl.pallas_call(lambda *refs: sky_kernel(normalise, groups, slots, cycles,...  3.58 us
    pallas_call x1, Pallas kernels, body(): pl.pallas_call(lambda *refs: forward_kernel(layout, groups, *refs), out_s...  2.37 us
    pallas_call x1, Pallas kernels, body(): pl.pallas_call(lambda *refs: backward_kernel(groups, cycles, *refs), out_...  2.07 us
    pallas_call x1, Pallas kernels, body(): pl.pallas_call(lambda *refs: residual_kernel(groups, slots, cycles, *refs...  1.72 us
  transfers between devices with their start and end apart: 22, of which 16 were waited for; matrix products, arithmetic and copies ran while one was open for 0% of the time, Pallas kernels for 8%

profile of v2, /device:TPU:0, one launch (start us, length us, event | category | flops | bytes accessed | tf_op | source)
XLA Modules:
  0.0 73.4 jit_solution(14228768975561170443)
XLA Ops:
  1.4 3.1 %collective-permute-start = (f32[16,4,1024]{2,1,0:T(4,128)}, f32[16,4,1024]{2,1,0:T(4,128)S(1)}, u32[]{:S(2)}, u32[]{:S(2)}) collective-permute-start(f32[16,4,1024]{2,1,0:T(4,128)} %harmonics_ref), channel_id=1, source_target_pairs={{0,8},{8,16},{16,24},{24,28},{28,20},{20,12},{12,4},{4,0},{1,9},{9... | collective-permute-start | bytes 786440 | tf_op jit(solution)/shard_map/ppermute | solution.py:395
  4.5 1.9 %collective-permute-start.3 = (f32[1,128]{1,0:T(1,128)S(1)}, f32[1,128]{1,0:T(1,128)S(1)}, u32[]{:S(2)}, u32[]{:S(2)}) collective-permute-start(f32[1,128]{1,0:T(1,128)S(1)} %meta.1.refs_0_.meta_ref), channel_id=1, source_target_pairs={{0,2},{1,3},{2,0},{3,1},{4,6},{5,7},{6,4},{7,5},{8,10},{9,11},{10,... | collective-permute-start | bytes 1544 | tf_op jit(solution)/shard_map/ppermute | solution.py:385
  9.4 1.6 %collective-permute-done.refs_4_ = f32[16,4,1024]{2,1,0:T(4,128)S(1)} collective-permute-done((f32[16,4,1024]{2,1,0:T(4,128)}, f32[16,4,1024]{2,1,0:T(4,128)S(1)}, u32[]{:S(2)}, u32[]{:S(2)}) %collective-permute-start) | collective-permute-done | bytes 262176 | tf_op jit(solution)/shard_map/ppermute | solution.py:395
  12.4 1.6 %collective-permute-start.5 = (f32[16,4,1024]{2,1,0:T(4,128)S(1)}, f32[16,4,1024]{2,1,0:T(4,128)S(1)}, u32[]{:S(2)}, u32[]{:S(2)}) collective-permute-start(f32[16,4,1024]{2,1,0:T(4,128)S(1)} %collective-permute-done.refs_4_), channel_id=1, source_target_pairs={{0,8},{8,16},{16,24},{24,28},{28,20},{20,12},{12,4},{4,0},{1,9},{9... | collective-permute-start | bytes 786440 | tf_op jit(solution)/shard_map/ppermute | solution.py:395
  15.4 3.6 %sky_analysis.1 = (f32[4,8,128]{2,1,0:T(8,128)S(1)}, f32[16,8,256]{2,1,0:T(8,128)S(1)}, f32[2,256,128]{2,1,0:T(8,128)S(1)}, f32[2,256,128]{2,1,0:T(8,128)S(1)}, ...) custom-call(f32[1,128]{1,0:T(1,128)S(1)} %meta.1.refs_0_.meta_ref, ...), custom_call_target="tpu_custom_call" | custom-call | flops 100000000 | bytes 12582912 | tf_op jit(solution)/shard_map/sky_analysis/pallas_call | solution.py:420
  21.0 1.6 %collective-permute-start.7 = (f32[16,4,1024]{2,1,0:T(4,128)S(1)}, f32[16,4,1024]{2,1,0:T(4,128)S(1)}, u32[]{:S(2)}, u32[]{:S(2)}) collective-permute-start(f32[16,4,1024]{2,1,0:T(4,128)S(1)} %collective-permute-done.5.refs_6_), channel_id=1, source_target_pairs={{0,8},{8,16},{16,24},{24,28},{28,20},{20,12},{12,4},{4,0},{1,9},{9... | collective-permute-start | bytes 786440 | tf_op jit(solution)/shard_map/ppermute | solution.py:395
  22.6 4.3 %collective-permute-done.8.refs_9_ = f32[16,4,1024]{2,1,0:T(4,128)S(1)} collective-permute-done((f32[16,4,1024]{2,1,0:T(4,128)S(1)}, f32[16,4,1024]{2,1,0:T(4,128)S(1)}, u32[]{:S(2)}, u32[]{:S(2)}) %collective-permute-start.8) | collective-permute-done | bytes 262176 | tf_op jit(solution)/shard_map/ppermute | solution.py:395
  27.0 2.4 %collective-permute-start.10 = (f32[8,4,1024]{2,1,0:T(4,128)S(1)}, f32[8,4,1024]{2,1,0:T(4,128)S(1)}, u32[]{:S(2)}, u32[]{:S(2)}) collective-permute-start(f32[8,4,1024]{2,1,0:T(4,128)S(1)} %slice.9), channel_id=1, source_target_pairs={{0,4},{8,0},{16,8},{4,12},{1,5},{9,1},{17,9},{5,13},{2,6},{10,2},{... | collective-permute-start | bytes 393224 | tf_op jit(solution)/shard_map/ppermute | solution.py:395
  29.4 1.6 %collective-permute-start.9 = (f32[8,4,1024]{2,1,0:T(4,128)S(1)}, f32[8,4,1024]{2,1,0:T(4,128)S(1)}, u32[]{:S(2)}, u32[]{:S(2)}) collective-permute-start(f32[8,4,1024]{2,1,0:T(4,128)S(1)} %slice.8), channel_id=1, source_target_pairs={{0,8},{8,16},{16,24},{24,28},{28,20},{20,12},{12,4},{4,0},{1,9},{9... | collective-permute-start | bytes 393224 | tf_op jit(solution)/shard_map/ppermute | solution.py:395
  31.0 2.8 %collective-permute-done.10.refs_11_ = f32[8,4,1024]{2,1,0:T(4,128)S(1)} collective-permute-done((f32[8,4,1024]{2,1,0:T(4,128)S(1)}, f32[8,4,1024]{2,1,0:T(4,128)S(1)}, u32[]{:S(2)}, u32[]{:S(2)}) %collective-permute-start.10) | collective-permute-done | bytes 131104 | tf_op jit(solution)/shard_map/ppermute | solution.py:395
  34.4 2.4 %forward.1 = (f32[8,128]{1,0:T(8,128)S(1)}, f32[16,128]{1,0:T(8,128)S(1)}, f32[16,128]{1,0:T(8,128)S(1)}, f32[16,128]{1,0:T(8,128)S(1)}) custom-call(f32[1,128]{1,0:T(1,128)S(1)} %meta.1.refs_0_.meta_ref, f32[16,2,8,8192]{3,2,1,0:T(8,128)S(1)} %get-tuple-element.32.refs_1_.refs_0_, f32[4,8,128]{2,1,0:T(8,128)S(1)} %get-tuple-element.37.refs_2_, ...), custom_call_target="tpu_custom_call" | custom-call | flops 100000000 | bytes 8388608 | tf_op jit(solution)/shard_map/forward/pallas_call | solution.py:450
  36.8 1.6 %collective-permute-start.12 = (f32[16,128]{1,0:T(8,128)S(1)}, f32[16,128]{1,0:T(8,128)S(1)}, u32[]{:S(2)}, u32[]{:S(2)}) collective-permute-start(f32[16,128]{1,0:T(8,128)S(1)} %get-tuple-element.42), channel_id=1, source_target_pairs={{0,2},{1,3},{2,0},{3,1},{4,6},{5,7},{6,4},{7,5},{8,10},{9,11},{10,... | collective-permute-start | bytes 24584 | tf_op jit(solution)/shard_map/ppermute | solution.py:385
  38.7 1.9 %collective-permute-done.12.refs_5_.refs_10_ = f32[16,128]{1,0:T(8,128)S(1)} collective-permute-done((f32[16,128]{1,0:T(8,128)S(1)}, f32[16,128]{1,0:T(8,128)S(1)}, u32[]{:S(2)}, u32[]{:S(2)}) %collective-permute-start.12) | collective-permute-done | bytes 8224 | tf_op jit(solution)/shard_map/ppermute | solution.py:385
  41.4 2.1 %backward.1 = (f32[8,16,4,1024]{3,2,1,0:T(4,128)S(1)}, f32[8,4,1024]{2,1,0:T(4,128)S(1)}, f32[8,4,1024]{2,1,0:T(4,128)S(1)}) custom-call(f32[16,2,8,8192]{3,2,1,0:T(8,128)S(1)} %get-tuple-element.32.refs_1_.refs_0_, f32[16,8,256]{2,1,0:T(8,128)S(1)} %get-tuple-element.33.refs_1_, f32[4,8,128]{2,1,0:T(8,128)S(1)} %get-tuple-element.37.refs_2_, ...), custom_call_target="tpu_custom_call" | custom-call | flops 100000000 | bytes 8388608 | tf_op jit(solution)/shard_map/backward/pallas_call | solution.py:465
  43.5 2.6 %collective-permute-start.18 = (f32[8,4,1024]{2,1,0:T(4,128)S(1)}, f32[8,4,1024]{2,1,0:T(4,128)S(1)}, u32[]{:S(2)}, u32[]{:S(2)}) collective-permute-start(f32[8,4,1024]{2,1,0:T(4,128)S(1)} %get-tuple-element.46), channel_id=1, source_target_pairs={{0,4},{8,0},{12,20},{4,12},{1,5},{9,1},{13,21},{5,13},{2,6},{10,2}... | collective-permute-start | bytes 393224 | tf_op jit(solution)/shard_map/ppermute | solution.py:395
  46.1 1.5 %collective-permute-start.14 = (f32[8,4,1024]{2,1,0:T(4,128)S(1)}, f32[8,4,1024]{2,1,0:T(4,128)S(1)}, u32[]{:S(2)}, u32[]{:S(2)}) collective-permute-start(f32[8,4,1024]{2,1,0:T(4,128)S(1)} %get-tuple-element.45), channel_id=1, source_target_pairs={{0,8},{8,16},{16,24},{24,28},{28,20},{20,12},{12,4},{4,0},{1,9},{9... | collective-permute-start | bytes 393224 | tf_op jit(solution)/shard_map/ppermute | solution.py:395
  47.7 3.5 %collective-permute-done.18.refs_1_ = f32[8,4,1024]{2,1,0:T(4,128)S(1)} collective-permute-done((f32[8,4,1024]{2,1,0:T(4,128)S(1)}, f32[8,4,1024]{2,1,0:T(4,128)S(1)}, u32[]{:S(2)}, u32[]{:S(2)}) %collective-permute-start.18) | collective-permute-done | bytes 131104 | tf_op jit(solution)/shard_map/ppermute | solution.py:395
  51.8 1.5 %collective-permute-start.15 = (f32[16,4,1024]{2,1,0:T(4,128)S(1)}, f32[16,4,1024]{2,1,0:T(4,128)S(1)}, u32[]{:S(2)}, u32[]{:S(2)}) collective-permute-start(f32[16,4,1024]{2,1,0:T(4,128)S(1)} %add.6), channel_id=1, source_target_pairs={{0,8},{8,16},{16,24},{24,28},{28,20},{20,12},{12,4},{4,0},{1,9},{9... | collective-permute-start | bytes 786440 | tf_op jit(solution)/shard_map/ppermute | solution.py:395
  53.3 5.4 %collective-permute-done.19.refs_1_ = f32[16,4,1024]{2,1,0:T(4,128)S(1)} collective-permute-done((f32[16,4,1024]{2,1,0:T(4,128)S(1)}, f32[16,4,1024]{2,1,0:T(4,128)S(1)}, u32[]{:S(2)}, u32[]{:S(2)}) %collective-permute-start.19) | collective-permute-done | bytes 262176 | tf_op jit(solution)/shard_map/ppermute | solution.py:395
  59.4 1.5 %collective-permute-start.16 = (f32[16,4,1024]{2,1,0:T(4,128)S(1)}, f32[16,4,1024]{2,1,0:T(4,128)S(1)}, u32[]{:S(2)}, u32[]{:S(2)}) collective-permute-start(f32[16,4,1024]{2,1,0:T(4,128)S(1)} %add.7), channel_id=1, source_target_pairs={{0,8},{8,16},{16,24},{24,28},{28,20},{20,12},{12,4},{4,0},{1,9},{9... | collective-permute-start | bytes 786440 | tf_op jit(solution)/shard_map/ppermute | solution.py:395
  61.0 4.5 %collective-permute-done.20.refs_1_ = f32[16,4,1024]{2,1,0:T(4,128)S(1)} collective-permute-done((f32[16,4,1024]{2,1,0:T(4,128)S(1)}, f32[16,4,1024]{2,1,0:T(4,128)S(1)}, u32[]{:S(2)}, u32[]{:S(2)}) %collective-permute-start.20) | collective-permute-done | bytes 262176 | tf_op jit(solution)/shard_map/ppermute | solution.py:395
  66.2 1.5 %collective-permute-start.17 = (f32[16,4,1024]{2,1,0:T(4,128)S(1)}, f32[16,4,1024]{2,1,0:T(4,128)S(1)}, u32[]{:S(2)}, u32[]{:S(2)}) collective-permute-start(f32[16,4,1024]{2,1,0:T(4,128)S(1)} %add.8), channel_id=1, source_target_pairs={{0,8},{8,16},{16,24},{24,28},{28,20},{20,12},{12,4},{4,0},{1,9},{9... | collective-permute-start | bytes 786440 | tf_op jit(solution)/shard_map/ppermute | solution.py:395
  67.7 1.7 %residual.1 = f32[2,256,128]{2,1,0:T(8,128)} custom-call(f32[1,128]{1,0:T(1,128)S(1)} %meta.1.refs_0_.meta_ref, f32[1,128]{1,0:T(1,128)S(1)} %collective-permute-done.2.refs_1_, f32[1,128]{1,0:T(1,128)S(1)} %collective-permute-done.3.refs_2_, f32[1,128]{1,0:T(1,128)S(1)} %collective-permute-done.4.refs_3_, f32[2,256,128]{2,1,0:T(8,128)S(1)} %bitcast.11, ...), custom_call_target="tpu_custom_call" | custom-call | flops 100000000 | bytes 2097152 | tf_op jit(solution)/shard_map/residual/pallas_call | solution.py:507
  69.4 2.5 %collective-permute-done.21.behind_ref = f32[16,4,1024]{2,1,0:T(4,128)S(1)} collective-permute-done((f32[16,4,1024]{2,1,0:T(4,128)S(1)}, f32[16,4,1024]{2,1,0:T(4,128)S(1)}, u32[]{:S(2)}, u32[]{:S(2)}) %collective-permute-start.21) | collective-permute-done | bytes 262176 | tf_op jit(solution)/shard_map/ppermute | solution.py:395
  (40 shorter events, 14.0 us)
Async XLA Ops:
  1.4 9.5 %collective-permute-start = (f32[16,4,1024]{2,1,0:T(4,128)}, f32[16,4,1024]{2,1,0:T(4,128)S(1)}, u32[]{:S(2)}, u32[]{:S(2)}) collective-permute-start(f32[16,4,1024]{2,1,0:T(4,128)} %harmonics_ref), channel_id=1, source_target_pairs={{0,8},{8,16},{16,24},{24,28},{28,20},{20,12},{12,4},{4,0},{1,9},{9... | collective-permute-start | bytes 786440 | tf_op jit(solution)/shard_map/ppermute | solution.py:395
  4.5 8.0 %collective-permute-start.1 = (f32[16,4,1024]{2,1,0:T(4,128)}, f32[16,4,1024]{2,1,0:T(4,128)S(1)}, u32[]{:S(2)}, u32[]{:S(2)}) collective-permute-start(f32[16,4,1024]{2,1,0:T(4,128)} %harmonics_ref), channel_id=1, source_target_pairs={{0,4},{8,0},{16,8},{24,16},{28,24},{20,28},{12,20},{4,12},{1,5},{9... | collective-permute-start | bytes 786440 | tf_op jit(solution)/shard_map/ppermute | solution.py:395
  4.5 2.1 %collective-permute-start.2 = (f32[1,128]{1,0:T(1,128)S(1)}, f32[1,128]{1,0:T(1,128)S(1)}, u32[]{:S(2)}, u32[]{:S(2)}) collective-permute-start(f32[1,128]{1,0:T(1,128)S(1)} %meta.1.refs_0_.meta_ref), channel_id=1, source_target_pairs={{0,1},{1,0},{2,3},{3,2},{4,5},{5,4},{6,7},{7,6},{8,9},{9,8},{10,11... | collective-permute-start | bytes 1544 | tf_op jit(solution)/shard_map/ppermute | solution.py:385
  4.5 3.5 %collective-permute-start.3 = (f32[1,128]{1,0:T(1,128)S(1)}, f32[1,128]{1,0:T(1,128)S(1)}, u32[]{:S(2)}, u32[]{:S(2)}) collective-permute-start(f32[1,128]{1,0:T(1,128)S(1)} %meta.1.refs_0_.meta_ref), channel_id=1, source_target_pairs={{0,2},{1,3},{2,0},{3,1},{4,6},{5,7},{6,4},{7,5},{8,10},{9,11},{10,... | collective-permute-start | bytes 1544 | tf_op jit(solution)/shard_map/ppermute | solution.py:385
  6.4 3.0 %collective-permute-start.4 = (f32[1,128]{1,0:T(1,128)S(1)}, f32[1,128]{1,0:T(1,128)S(1)}, u32[]{:S(2)}, u32[]{:S(2)}) collective-permute-start(f32[1,128]{1,0:T(1,128)S(1)} %meta.1.refs_0_.meta_ref), channel_id=1, source_target_pairs={{0,3},{1,2},{2,1},{3,0},{4,7},{5,6},{6,5},{7,4},{8,11},{9,10},{10,... | collective-permute-start | bytes 1544 | tf_op jit(solution)/shard_map/ppermute | solution.py:385
  12.4 6.9 %collective-permute-start.5 = (f32[16,4,1024]{2,1,0:T(4,128)S(1)}, f32[16,4,1024]{2,1,0:T(4,128)S(1)}, u32[]{:S(2)}, u32[]{:S(2)}) collective-permute-start(f32[16,4,1024]{2,1,0:T(4,128)S(1)} %collective-permute-done.refs_4_), channel_id=1, source_target_pairs={{0,8},{8,16},{16,24},{24,28},{28,20},{20,12},{12,4},{4,0},{1,9},{9... | collective-permute-start | bytes 786440 | tf_op jit(solution)/shard_map/ppermute | solution.py:395
  14.0 6.6 %collective-permute-start.6 = (f32[16,4,1024]{2,1,0:T(4,128)S(1)}, f32[16,4,1024]{2,1,0:T(4,128)S(1)}, u32[]{:S(2)}, u32[]{:S(2)}) collective-permute-start(f32[16,4,1024]{2,1,0:T(4,128)S(1)} %collective-permute-done.1.refs_5_), channel_id=1, source_target_pairs={{0,4},{8,0},{16,8},{24,16},{28,24},{20,28},{12,20},{4,12},{1,5},{9... | collective-permute-start | bytes 786440 | tf_op jit(solution)/shard_map/ppermute | solution.py:395
  15.4 19.0 %copy-start.2 = (f32[16,4,1024]{2,1,0:T(4,128)S(1)}, f32[16,4,1024]{2,1,0:T(4,128)}, u32[]{:S(2)}) copy-start(f32[16,4,1024]{2,1,0:T(4,128)} %harmonics_ref) | copy-start | bytes 786436
  20.6 6.4 %collective-permute-start.8 = (f32[16,4,1024]{2,1,0:T(4,128)S(1)}, f32[16,4,1024]{2,1,0:T(4,128)S(1)}, u32[]{:S(2)}, u32[]{:S(2)}) collective-permute-start(f32[16,4,1024]{2,1,0:T(4,128)S(1)} %collective-permute-done.6.refs_7_), channel_id=1, source_target_pairs={{0,4},{8,0},{16,8},{24,16},{28,24},{20,28},{12,20},{4,12},{1,5},{9... | collective-permute-start | bytes 786440 | tf_op jit(solution)/shard_map/ppermute | solution.py:395
  21.0 8.3 %collective-permute-start.7 = (f32[16,4,1024]{2,1,0:T(4,128)S(1)}, f32[16,4,1024]{2,1,0:T(4,128)S(1)}, u32[]{:S(2)}, u32[]{:S(2)}) collective-permute-start(f32[16,4,1024]{2,1,0:T(4,128)S(1)} %collective-permute-done.5.refs_6_), channel_id=1, source_target_pairs={{0,8},{8,16},{16,24},{24,28},{28,20},{20,12},{12,4},{4,0},{1,9},{9... | collective-permute-start | bytes 786440 | tf_op jit(solution)/shard_map/ppermute | solution.py:395
  27.0 6.9 %collective-permute-start.10 = (f32[8,4,1024]{2,1,0:T(4,128)S(1)}, f32[8,4,1024]{2,1,0:T(4,128)S(1)}, u32[]{:S(2)}, u32[]{:S(2)}) collective-permute-start(f32[8,4,1024]{2,1,0:T(4,128)S(1)} %slice.9), channel_id=1, source_target_pairs={{0,4},{8,0},{16,8},{4,12},{1,5},{9,1},{17,9},{5,13},{2,6},{10,2},{... | collective-permute-start | bytes 393224 | tf_op jit(solution)/shard_map/ppermute | solution.py:395
  29.4 5.0 %collective-permute-start.9 = (f32[8,4,1024]{2,1,0:T(4,128)S(1)}, f32[8,4,1024]{2,1,0:T(4,128)S(1)}, u32[]{:S(2)}, u32[]{:S(2)}) collective-permute-start(f32[8,4,1024]{2,1,0:T(4,128)S(1)} %slice.8), channel_id=1, source_target_pairs={{0,8},{8,16},{16,24},{24,28},{28,20},{20,12},{12,4},{4,0},{1,9},{9... | collective-permute-start | bytes 393224 | tf_op jit(solution)/shard_map/ppermute | solution.py:395
  36.8 1.9 %collective-permute-start.11 = (f32[16,128]{1,0:T(8,128)S(1)}, f32[16,128]{1,0:T(8,128)S(1)}, u32[]{:S(2)}, u32[]{:S(2)}) collective-permute-start(f32[16,128]{1,0:T(8,128)S(1)} %get-tuple-element.41), channel_id=1, source_target_pairs={{0,1},{1,0},{2,3},{3,2},{4,5},{5,4},{6,7},{7,6},{8,9},{9,8},{10,11... | collective-permute-start | bytes 24584 | tf_op jit(solution)/shard_map/ppermute | solution.py:385
  36.8 3.7 %collective-permute-start.12 = (f32[16,128]{1,0:T(8,128)S(1)}, f32[16,128]{1,0:T(8,128)S(1)}, u32[]{:S(2)}, u32[]{:S(2)}) collective-permute-start(f32[16,128]{1,0:T(8,128)S(1)} %get-tuple-element.42), channel_id=1, source_target_pairs={{0,2},{1,3},{2,0},{3,1},{4,6},{5,7},{6,4},{7,5},{8,10},{9,11},{10,... | collective-permute-start | bytes 24584 | tf_op jit(solution)/shard_map/ppermute | solution.py:385
  38.4 3.1 %collective-permute-start.13 = (f32[16,128]{1,0:T(8,128)S(1)}, f32[16,128]{1,0:T(8,128)S(1)}, u32[]{:S(2)}, u32[]{:S(2)}) collective-permute-start(f32[16,128]{1,0:T(8,128)S(1)} %get-tuple-element.43), channel_id=1, source_target_pairs={{0,3},{1,2},{2,1},{3,0},{4,7},{5,6},{6,5},{7,4},{8,11},{9,10},{10,... | collective-permute-start | bytes 24584 | tf_op jit(solution)/shard_map/ppermute | solution.py:385
  43.5 24.2 %copy-start.1 = (f32[2,2,16384]{2,1,0:T(2,128)S(1)}, f32[2,2,16384]{2,1,0:T(2,128)}, u32[]{:S(2)}) copy-start(f32[2,2,16384]{2,1,0:T(2,128)} %param.9) | copy-start | bytes 786436
  43.5 7.6 %collective-permute-start.18 = (f32[8,4,1024]{2,1,0:T(4,128)S(1)}, f32[8,4,1024]{2,1,0:T(4,128)S(1)}, u32[]{:S(2)}, u32[]{:S(2)}) collective-permute-start(f32[8,4,1024]{2,1,0:T(4,128)S(1)} %get-tuple-element.46), channel_id=1, source_target_pairs={{0,4},{8,0},{12,20},{4,12},{1,5},{9,1},{13,21},{5,13},{2,6},{10,2}... | collective-permute-start | bytes 393224 | tf_op jit(solution)/shard_map/ppermute | solution.py:395
  46.1 5.6 %collective-permute-start.14 = (f32[8,4,1024]{2,1,0:T(4,128)S(1)}, f32[8,4,1024]{2,1,0:T(4,128)S(1)}, u32[]{:S(2)}, u32[]{:S(2)}) collective-permute-start(f32[8,4,1024]{2,1,0:T(4,128)S(1)} %get-tuple-element.45), channel_id=1, source_target_pairs={{0,8},{8,16},{16,24},{24,28},{28,20},{20,12},{12,4},{4,0},{1,9},{9... | collective-permute-start | bytes 393224 | tf_op jit(solution)/shard_map/ppermute | solution.py:395
  51.2 7.6 %collective-permute-start.19 = (f32[16,4,1024]{2,1,0:T(4,128)S(1)}, f32[16,4,1024]{2,1,0:T(4,128)S(1)}, u32[]{:S(2)}, u32[]{:S(2)}) collective-permute-start(f32[16,4,1024]{2,1,0:T(4,128)S(1)} %add.9), channel_id=1, source_target_pairs={{0,4},{8,0},{16,8},{24,16},{28,24},{20,28},{12,20},{4,12},{1,5},{9... | collective-permute-start | bytes 786440 | tf_op jit(solution)/shard_map/ppermute | solution.py:395
  51.8 7.6 %collective-permute-start.15 = (f32[16,4,1024]{2,1,0:T(4,128)S(1)}, f32[16,4,1024]{2,1,0:T(4,128)S(1)}, u32[]{:S(2)}, u32[]{:S(2)}) collective-permute-start(f32[16,4,1024]{2,1,0:T(4,128)S(1)} %add.6), channel_id=1, source_target_pairs={{0,8},{8,16},{16,24},{24,28},{28,20},{20,12},{12,4},{4,0},{1,9},{9... | collective-permute-start | bytes 786440 | tf_op jit(solution)/shard_map/ppermute | solution.py:395
  58.8 6.7 %collective-permute-start.20 = (f32[16,4,1024]{2,1,0:T(4,128)S(1)}, f32[16,4,1024]{2,1,0:T(4,128)S(1)}, u32[]{:S(2)}, u32[]{:S(2)}) collective-permute-start(f32[16,4,1024]{2,1,0:T(4,128)S(1)} %add.10), channel_id=1, source_target_pairs={{0,4},{8,0},{16,8},{24,16},{28,24},{20,28},{12,20},{4,12},{1,5},{9... | collective-permute-start | bytes 786440 | tf_op jit(solution)/shard_map/ppermute | solution.py:395
  59.4 6.7 %collective-permute-start.16 = (f32[16,4,1024]{2,1,0:T(4,128)S(1)}, f32[16,4,1024]{2,1,0:T(4,128)S(1)}, u32[]{:S(2)}, u32[]{:S(2)}) collective-permute-start(f32[16,4,1024]{2,1,0:T(4,128)S(1)} %add.7), channel_id=1, source_target_pairs={{0,8},{8,16},{16,24},{24,28},{28,20},{20,12},{12,4},{4,0},{1,9},{9... | collective-permute-start | bytes 786440 | tf_op jit(solution)/shard_map/ppermute | solution.py:395
  65.5 6.4 %collective-permute-start.21 = (f32[16,4,1024]{2,1,0:T(4,128)S(1)}, f32[16,4,1024]{2,1,0:T(4,128)S(1)}, u32[]{:S(2)}, u32[]{:S(2)}) collective-permute-start(f32[16,4,1024]{2,1,0:T(4,128)S(1)} %add.11), channel_id=1, source_target_pairs={{0,4},{8,0},{16,8},{24,16},{28,24},{20,28},{12,20},{4,12},{1,5},{9... | collective-permute-start | bytes 786440 | tf_op jit(solution)/shard_map/ppermute | solution.py:395
  66.2 6.4 %collective-permute-start.17 = (f32[16,4,1024]{2,1,0:T(4,128)S(1)}, f32[16,4,1024]{2,1,0:T(4,128)S(1)}, u32[]{:S(2)}, u32[]{:S(2)}) collective-permute-start(f32[16,4,1024]{2,1,0:T(4,128)S(1)} %add.8), channel_id=1, source_target_pairs={{0,8},{8,16},{16,24},{24,28},{28,20},{20,12},{12,4},{4,0},{1,9},{9... | collective-permute-start | bytes 786440 | tf_op jit(solution)/shard_map/ppermute | solution.py:395
  (1 other events, 0.9 us)

commit v3 on v2

v3 whole, which is shorter than its diff:
```python
import math

import jax
import jax.numpy as jnp
from jax import lax
from jax.experimental import pallas as pl
from jax.experimental.pallas import tpu as pltpu
from jax.sharding import PartitionSpec as P

HIGHEST = lax.Precision.HIGHEST
LANES = 128
VMEM = pltpu.VMEM
MIB = 1024 * 1024


def ring_of(blocks):
    return list(range(0, blocks, 2)) + list(range(blocks - 1, 0, -2))


def ring_place(block, blocks):
    return jnp.where(block % 2 == 0, block // 2, blocks - 1 - block // 2)


def block_at(place, blocks):
    place = lax.rem(place + 2 * blocks, blocks)
    return jnp.where(place < blocks // 2, 2 * place, 2 * (blocks - 1 - place) + 1)


def sin_pi(x):
    turns = jnp.round(x)
    y = (x - turns) * math.pi
    z = y * y
    value = -1.0 / 39916800
    for term in (1.0 / 362880, -1.0 / 5040, 1.0 / 120, -1.0 / 6, 1.0):
        value = value * z + term
    value = value * y
    return jnp.where(turns.astype(jnp.int32) % 2 != 0, -value, value)


def half_turns(order, step, length):
    total = order * step
    period = 2 * length
    scale = 0.5 / length.astype(jnp.float32)
    for _ in range(2):
        total = total - jnp.floor(total.astype(jnp.float32) * scale).astype(jnp.int32) * period
    return total.astype(jnp.float32) / length.astype(jnp.float32)


def pixel_mask(shape, length):
    pixel = lax.broadcasted_iota(jnp.int32, shape, 0) // 2 * shape[1]
    pixel = pixel + lax.broadcasted_iota(jnp.int32, shape, 1)
    return pixel < length


def meta_kernel(slots, cycles, ids, length, offset, weight, out_ref, *scratch):
    *held, sems = scratch
    copies = [
        pltpu.make_async_copy(source, target, sems.at[k])
        for k, (source, target) in enumerate(zip((ids, length, offset, weight), held))
    ]
    for copy in copies:
        copy.start()
    for copy in copies:
        copy.wait()
    lane = lax.broadcasted_iota(jnp.int32, (1, LANES), 1)
    out = jnp.zeros((1, LANES), jnp.float32)
    for m in range(slots):
        out = jnp.where(lane == m, held[0][m].astype(jnp.float32), out)
    for c in range(cycles):
        for k in range(3):
            value = held[1 + k][c].astype(jnp.float32)
            out = jnp.where(lane == slots + k * cycles + c, value, out)
    out_ref[...] = out


def entry(meta, at):
    return meta[:, at : at + 1]


def spread_ids(metas, slots, sources):
    per = LANES // slots
    lane = lax.broadcasted_iota(jnp.int32, (1, LANES), 1)
    pieces = []
    for start in range(0, len(sources), per):
        piece = jnp.zeros((1, LANES), jnp.float32)
        for k in range(per):
            value = metas[sources[start + k]]
            value = pltpu.roll(value, k * slots, 1) if k else value
            piece = jnp.where(lane // slots == k, value, piece)
        pieces.append(piece)
    return jnp.concatenate(pieces, axis=1)


def sky_kernel(normalise, groups, slots, cycles, *rest):
    metas = [ref[...] for ref in rest[:groups]]
    sky_hbm, pieces_ref, acs_ref, asc_ref, fine_ref, section_ref, sky_ref, sky_sem = rest[groups:]
    sky_copy = pltpu.make_async_copy(sky_hbm, sky_ref, sky_sem)
    sky_copy.start()
    rows, both = acs_ref.shape[1:]
    every = both // 2
    ids = spread_ids(metas, slots, [d for _ in range(2) for d in range(groups)])
    ids = ids.astype(jnp.int32)
    row8 = lax.broadcasted_iota(jnp.int32, (8, both), 0)
    sums = [jnp.zeros((8, both), jnp.float32) for _ in range(4)]
    for c in range(cycles):
        length = entry(metas[0], slots + c).astype(jnp.int32)
        offset = entry(metas[0], slots + cycles + c).astype(jnp.int32)
        coarse = lax.broadcasted_iota(jnp.int32, (rows, both), 0) // 2 * (2 * LANES) + offset
        x = half_turns(ids, coarse, length)
        first = lax.broadcasted_iota(jnp.int32, (rows, both), 1) < every
        acs = sin_pi(x + jnp.where(first, 0.5, 1.0))
        asc = sin_pi(x + jnp.where(first, 0.0, 0.5))
        acs_ref[c] = acs
        asc_ref[c] = asc
        fine = 2 * lax.broadcasted_iota(jnp.int32, (LANES, both), 0)
        x = half_turns(ids, fine, length)
        first = lax.broadcasted_iota(jnp.int32, (LANES, both), 1) < every
        table = sin_pi(x + jnp.where(first, 0.5, 0.0))
        fine_ref[c] = table
        if c == 0:
            sky_copy.wait()
        section = jnp.where(pixel_mask((rows, LANES), length), sky_ref[c], 0.0)
        section_ref[c] = section
        spun = jnp.dot(section, table, precision=HIGHEST, preferred_element_type=jnp.float32)
        weight = entry(metas[0], slots + 2 * cycles + c) * normalise
        for k, value in enumerate((spun * acs, spun * asc)):
            value = sum(value[8 * i : 8 * i + 8] for i in range(rows // 8))
            for q in range(2):
                total = jnp.sum(jnp.where(row8 % 2 == q, value, 0.0), axis=0, keepdims=True)
                total = total * (-weight if k else weight)
                sums[2 * q + k] = jnp.where(row8 == c, total, sums[2 * q + k])
    lane = lax.broadcasted_iota(jnp.int32, (8, LANES), 1)
    totals = []
    for value in sums:
        tiles = [value[:, i : i + LANES] for i in range(0, both, LANES)]
        if every < LANES:
            shift = every
            while shift < LANES:
                tiles[0] = tiles[0] + pltpu.roll(tiles[0], shift, 1)
                shift *= 2
            totals.append(tiles)
        else:
            half = len(tiles) // 2
            totals.append([tiles[i] + tiles[half + i] for i in range(half)])
    for d in range(groups):
        piece = jnp.zeros((8, LANES), jnp.float32)
        tile, at = divmod(d * slots, LANES)
        for a in range(4):
            shift = (a * slots - at) % LANES
            value = totals[a][tile]
            value = pltpu.roll(value, shift, 1) if shift else value
            piece = jnp.where(lane // slots == a, value, piece)
        pieces_ref[d] = piece


def gram_kernel(normalise, groups, slots, cycles, *rest):
    metas = [ref[...] for ref in rest[:groups]]
    (gram_ref,) = rest[groups:]
    me = lax.axis_index("order")
    count, wide = gram_ref.shape[1:]
    row = lax.broadcasted_iota(jnp.int32, (count, wide), 0)
    length = jnp.ones((count, wide), jnp.float32)
    offset = jnp.zeros((count, wide), jnp.float32)
    weight = jnp.zeros((count, wide), jnp.float32)
    for d in range(groups):
        for c in range(cycles):
            here = row == (me ^ d) * cycles + c
            length = jnp.where(here, entry(metas[d], slots + c), length)
            offset = jnp.where(here, entry(metas[d], slots + cycles + c), offset)
            weight = jnp.where(here, entry(metas[d], slots + 2 * cycles + c), weight)
    others = spread_ids(metas, slots, [d for d in range(groups) for _ in range(4)])
    lane = lax.broadcasted_iota(jnp.int32, (count, wide), 1)
    cosine = (lane // slots) % 2 == 0
    factor = jnp.where(others == 0.0, 0.5, 1.0) * normalise * weight * length
    inverse = 1.0 / length
    odd = offset > 0.5

    def response(n):
        turns = jnp.round(n * inverse)
        sign = jnp.where(odd & (turns.astype(jnp.int32) % 2 != 0), -1.0, 1.0)
        return jnp.where(turns * length == n, sign, 0.0)

    for m in range(slots):
        mine = entry(metas[0], m)
        near = response(mine - others)
        far = response(mine + others)
        gram_ref[m] = factor * (near + jnp.where(cosine, far, -far))


def table_copies(legendre, tables, sems):
    slots, _, _, degrees = tables.shape
    copies = []
    for m in range(slots):
        first = m * (degrees // slots)
        part = (m, slice(None), slice(None), pl.ds(first, degrees - first))
        copies.append(pltpu.make_async_copy(legendre.at[part], tables.at[part], sems.at[m]))
    return copies


def use_tile(tables, m, span, keep, coefs, p, n):
    plus = tables[m, 0, :, span]
    minus = tables[m, 1, :, span]
    if keep is not None:
        plus = jnp.where(keep, plus, 0.0)
        minus = jnp.where(keep, minus, 0.0)
    for a in range(4):
        c = coefs(a)
        if keep is not None:
            c = jnp.where(keep[:1], c, 0.0)
        p[a] = p[a] + plus * c
        n[a] = n[a] + minus * c


def combine(p, n):
    return [n[3] - p[0], -p[1] - n[2], -p[2] - n[1], n[0] - p[3]]


def tables_kernel(legendre, tables, sems):
    copies = table_copies(legendre, tables, sems)
    for copy in copies:
        copy.start()
    for copy in copies:
        copy.wait()


def forward_kernel(steps, firsts, meta_ref, tables, *rest):
    parts = rest[: len(steps)]
    sums_ref, coefs = rest[len(steps) :]
    slots, _, count, degrees = tables.shape
    width = parts[0].shape[2]
    blocks = degrees // width
    stratum = degrees // slots
    meta = meta_ref[...]
    place = ring_place(lax.axis_index("blk"), blocks)
    for part, step, low in zip(parts, steps, firsts):
        first = pl.multiple_of(block_at(place + step, blocks) * width, LANES)
        for m in range(part.shape[0]):
            coefs[low + m, :, pl.ds(first, width)] = part[m]
    first = pl.multiple_of(block_at(place + blocks // 2, blocks) * width, LANES)
    for m in range(slots):
        coefs[m, :, pl.ds(first, width)] = jnp.zeros((4, width), jnp.float32)
    lane = lax.broadcasted_iota(jnp.int32, (count, LANES), 1)
    for m in range(slots):
        floor = jnp.maximum(entry(meta, m).astype(jnp.int32), 2)
        p = [jnp.zeros((count, LANES), jnp.float32)] * 4
        n = [jnp.zeros((count, LANES), jnp.float32)] * 4
        for t in range(stratum * m // LANES, degrees // LANES):
            span = slice(t * LANES, (t + 1) * LANES)
            keep = lane >= floor - t * LANES if t * LANES < stratum * (m + 1) else None
            use_tile(tables, m, span, keep, lambda a: coefs[m, a : a + 1, span], p, n)
        for a, total in enumerate(combine(p, n)):
            sums_ref[m, a] = total


def phases_kernel(groups, meta_ref, tables, pieces_ref, sums_ref, low_ref, high_ref, *rest):
    phases_ref, *messages = rest
    slots, _, count, degrees = tables.shape
    middle, _, width = low_ref.shape
    blocks = degrees // width
    meta = meta_ref[...]
    place = ring_place(lax.axis_index("blk"), blocks)
    first = pl.multiple_of(block_at(place + blocks // 2, blocks) * width, LANES)
    lane = lax.broadcasted_iota(jnp.int32, (count, LANES), 1)
    phases = jnp.zeros((count, LANES), jnp.float32)
    for m in range(slots):
        floor = jnp.maximum(entry(meta, m).astype(jnp.int32), 2) - first
        part, at = (low_ref, m) if m < middle else (high_ref, m - middle)
        p = [jnp.zeros((count, LANES), jnp.float32)] * 4
        n = [jnp.zeros((count, LANES), jnp.float32)] * 4
        for t in range(width // LANES):
            here = slice(t * LANES, (t + 1) * LANES)
            keep = lane >= floor - t * LANES
            span = pl.ds(first + t * LANES, LANES)
            use_tile(tables, m, span, keep, lambda a: part[at, a : a + 1, here], p, n)
        for a, total in enumerate(combine(p, n)):
            value = jnp.sum(total + sums_ref[m, a], axis=1, keepdims=True)
            phases = jnp.where(lane == a * slots + m, value, phases)
    phases_ref[...] = phases
    for d in range(1, groups):
        messages[d - 1][:count] = phases
        messages[d - 1][count:] = pieces_ref[d]


def fold_rows(values, row):
    for step in (1, 2, 4):
        low = (row & step) == 0
        values = [
            jnp.where(low, values[i], values[i + 1])
            + pltpu.roll(jnp.where(low, values[i + 1], values[i]), step, 0)
            for i in range(0, len(values), 2)
        ]
    return values[0]


def update_tiles(tables, m, spans, an, ng, row8):
    count = tables.shape[2]
    values = []
    for span in spans:
        plus = tables[m, 0, :, span]
        minus = tables[m, 1, :, span]
        four = [
            plus * ng[0] + minus * an[3],
            plus * ng[1] + minus * ng[2],
            plus * ng[2] + minus * ng[1],
            plus * ng[3] + minus * an[0],
        ]
        values += [sum(v[8 * k : 8 * k + 8] for k in range(count // 8)) for v in four]
    return fold_rows(values, row8)


def analysed_kernel(groups, cycles, tables, gram_ref, pieces_ref, phases_ref, *rest):
    messages = rest[: groups - 1]
    *sends, analysed_ref, sky = rest[groups - 1 :]
    slots, _, count, degrees = tables.shape
    middle, _, width = sends[0].shape
    blocks = degrees // width
    far = blocks // 2
    place = ring_place(lax.axis_index("blk"), blocks)
    firsts = [
        pl.multiple_of(block_at(place + step, blocks) * width, LANES)
        for step in (far, -far, 1 - far, far - 1)
    ]
    owner = lax.axis_index("order")
    wide = 4 * slots
    pairs = []
    for d in range(groups):
        phases = phases_ref[...] if d == 0 else messages[d - 1][:count]
        piece = pieces_ref[0] if d == 0 else messages[d - 1][count:]
        sky[pl.ds((owner ^ d) * cycles, cycles)] = piece[:cycles]
        pairs.append(phases)
    lane = lax.broadcasted_iota(jnp.int32, (count, LANES), 1)
    row8 = lax.broadcasted_iota(jnp.int32, (8, LANES), 0)
    per = LANES // wide
    packed = []
    for start in range(0, groups, per):
        value = pairs[start]
        for k in range(1, per):
            value = jnp.where(
                lane // wide == k, pltpu.roll(pairs[start + k], k * wide, 1), value
            )
        packed.append(value)
    observed = sky[...]
    for m in range(slots):
        total = jnp.where((lane < wide) & (lane % slots == m), observed, 0.0)
        for k, value in enumerate(packed):
            total = total - gram_ref[m, :, k * LANES : (k + 1) * LANES] * value
        an = []
        for a in range(4):
            value = jnp.where((lane % wide) // slots == a, total, 0.0)
            value = jnp.sum(value, axis=1, keepdims=True)
            an.append(jnp.broadcast_to(value, (count, LANES)))
            analysed_ref[m, a] = an[a]
        ng = [-value for value in an]
        half, at = divmod(m, middle)
        for part, first in zip(sends[half::2], firsts[half::2]):
            for t in range(0, width // LANES, 2):
                spans = [pl.ds(first + u * LANES, LANES) for u in (t, t + 1)]
                folded = update_tiles(tables, m, spans, an, ng, row8)
                for k, u in enumerate((t, t + 1)):
                    part[at, :, u * LANES : (u + 1) * LANES] = folded[4 * k : 4 * k + 4]


def backward_kernel(tables, analysed_ref, out):
    slots, _, _, degrees = tables.shape
    blocks, _, _, width = out.shape
    stratum = degrees // slots
    place = ring_place(lax.axis_index("blk"), blocks)
    ring = ring_of(blocks)
    step_of = [lax.rem(ring.index(b) - place + blocks, blocks) for b in range(blocks)]
    row8 = lax.broadcasted_iota(jnp.int32, (8, LANES), 0)
    for m in range(slots):
        an = [analysed_ref[m, a] for a in range(4)]
        ng = [-value for value in an]
        for t in range(stratum * m // LANES, degrees // LANES, 2):
            spans = [slice(u * LANES, (u + 1) * LANES) for u in (t, t + 1)]
            folded = update_tiles(tables, m, spans, an, ng, row8)
            for k, u in enumerate((t, t + 1)):
                inner = u * LANES % width
                out[step_of[u * LANES // width], m, :, inner : inner + LANES] = folded[
                    4 * k : 4 * k + 4
                ]


def residual_kernel(groups, slots, cycles, *rest):
    metas = [ref[...] for ref in rest[:groups]]
    section_ref, acs_ref, asc_ref, fine_ref, phases_ref = rest[groups : groups + 5]
    messages = rest[groups + 5 : 2 * groups + 4]
    out_ref, spread = rest[2 * groups + 4 :]
    owner = lax.axis_index("order")
    rows, both = acs_ref.shape[1:]
    every = both // 2
    count = phases_ref.shape[0]
    lane = lax.broadcasted_iota(jnp.int32, (count, LANES), 1)
    ids = spread_ids(metas, slots, [d for _ in range(2) for d in range(groups)])
    factor = jnp.where(ids == 0.0, 1.0, 2.0)
    per = LANES // slots
    values = [phases_ref[...]] + [ref[:count] for ref in messages]
    for a in range(4):
        tiles = []
        for start in range(0, 2 * groups, per):
            tile = jnp.zeros((count, LANES), jnp.float32)
            for k in range(per):
                shift = (k - a) * slots % LANES
                value = values[(start + k) % groups]
                value = pltpu.roll(value, shift, 1) if shift else value
                tile = jnp.where(lane // slots == k, value, tile)
            tiles.append(tile)
        spread[a] = jnp.concatenate(tiles, axis=1) * factor
    even = lax.broadcasted_iota(jnp.int32, (rows, both), 0) % 2 == 0
    for c in range(cycles):
        q_re, q_im, u_re, u_im = [spread[a, pl.ds(owner * cycles + c, 1)] for a in range(4)]
        weights = jnp.where(even, q_re, u_re) * acs_ref[c]
        weights = weights - jnp.where(even, q_im, u_im) * asc_ref[c]
        model = lax.dot_general(
            weights, fine_ref[c], (((1,), (1,)), ((), ())), precision=HIGHEST,
            preferred_element_type=jnp.float32,
        )
        inside = pixel_mask((rows, LANES), entry(metas[0], slots + c).astype(jnp.int32))
        out_ref[c] = section_ref[c] - jnp.where(inside, model, 0.0)


def add_kernel(index, first, piece_ref, value_ref, out_ref):
    out_ref[...] = piece_ref[index, first : first + out_ref.shape[0]] + value_ref[...]


def final_kernel(meta_ref, harmonics_ref, piece_ref, *rest):
    *received, out_ref = rest
    slots, parts, width = out_ref.shape
    middle = slots // 2
    start = lax.axis_index("blk") * width
    degree = start + lax.broadcasted_iota(jnp.int32, (parts, width), 1)
    meta = meta_ref[...]
    for m in range(slots):
        h, at = divmod(m, middle)
        update = piece_ref[0, m] + (received[h][at] + received[2 + h][at])
        valid = degree >= jnp.maximum(entry(meta, m).astype(jnp.int32), 2)
        out_ref[m] = jnp.where(valid, harmonics_ref[m] + update, 0.0)


def vmem():
    return pl.BlockSpec(memory_space=VMEM)


def shape(*dims):
    return jax.ShapeDtypeStruct(dims, jnp.float32)


def body(harmonics, legendre, sky_map, cycle_length, cycle_offset, cycle_weight, order_ids):
    groups = lax.axis_size("order")
    blocks = lax.axis_size("blk")
    slots, _, width = harmonics.shape
    count, degrees = legendre.shape[2:]
    cycles, _, pixels = sky_map.shape
    rows = pixels // LANES
    every = slots * groups
    normalise = math.sqrt(degrees * every / (cycles * groups * blocks * pixels))

    def swap(value, axis, step):
        size = lax.axis_size(axis)
        return lax.ppermute(value, axis, [(i, i ^ step) for i in range(size)])

    ring = ring_of(blocks)

    def turn(value, way):
        pairs = [(ring[p], ring[(p + way) % blocks]) for p in range(blocks)]
        return lax.ppermute(value, "blk", pairs)

    def estimate(micros):
        return pl.CostEstimate(flops=0, bytes_accessed=int(micros * 3.0e6), transcendentals=0)

    hbm = pl.BlockSpec(memory_space=pl.ANY)
    small = (order_ids, cycle_length, cycle_offset, cycle_weight)
    meta = pl.pallas_call(
        lambda *refs: meta_kernel(slots, cycles, *refs),
        out_shape=pltpu.VMEM((1, LANES), jnp.float32),
        in_specs=[hbm] * 4,
        out_specs=vmem(),
        scratch_shapes=[pltpu.SMEM(v.shape, v.dtype) for v in small]
        + [pltpu.SemaphoreType.DMA((len(small),))],
        compiler_params=pltpu.CompilerParams(vmem_limit_bytes=2 * MIB),
        name="meta",
    )(*[pltpu.with_memory_space_constraint(v, pltpu.HBM) for v in small])
    metas = [meta] + [swap(meta, "order", d) for d in range(1, groups)]

    far = blocks // 2
    middle = slots // 2
    ahead, behind = turn(harmonics, 1), turn(harmonics, -1)
    parts, steps, firsts = [harmonics, ahead, behind], [0, -1, 1], [0, 0, 0]
    tables = pl.pallas_call(
        tables_kernel,
        out_shape=pltpu.VMEM(legendre.shape, jnp.float32),
        in_specs=[hbm],
        out_specs=hbm,
        scratch_shapes=[pltpu.SemaphoreType.DMA((slots,))],
        compiler_params=pltpu.CompilerParams(vmem_limit_bytes=2 * MIB),
        cost_estimate=estimate(1.5),
        name="tables",
    )(pltpu.with_memory_space_constraint(legendre, pltpu.HBM))
    behind, tables, *metas = lax.optimization_barrier((behind, tables, *metas))
    ahead = [ahead[:middle], ahead[middle:]]
    behind = [behind[:middle], behind[middle:]]

    sky = sky_map.reshape(cycles, 2, rows, LANES).transpose(0, 2, 1, 3)
    sky = sky.reshape(cycles, 2 * rows, LANES)
    pieces, acs, asc, fine, section = pl.pallas_call(
        lambda *refs: sky_kernel(normalise, groups, slots, cycles, *refs),
        out_shape=(
            shape(groups, 8, LANES),
            shape(cycles, 2 * rows, 2 * every),
            shape(cycles, 2 * rows, 2 * every),
            shape(cycles, LANES, 2 * every),
            shape(cycles, 2 * rows, LANES),
        ),
        in_specs=[vmem()] * groups + [hbm],
        out_specs=(vmem(),) * 5,
        scratch_shapes=[
            pltpu.VMEM((cycles, 2 * rows, LANES), jnp.float32),
            pltpu.SemaphoreType.DMA,
        ],
        compiler_params=pltpu.CompilerParams(vmem_limit_bytes=16 * MIB),
        cost_estimate=estimate(3),
        name="sky_analysis",
    )(*metas, pltpu.with_memory_space_constraint(sky, pltpu.HBM))
    gram = pl.pallas_call(
        lambda *refs: gram_kernel(normalise, groups, slots, cycles, *refs),
        out_shape=shape(slots, count, 4 * every),
        in_specs=[vmem()] * groups,
        out_specs=vmem(),
        compiler_params=pltpu.CompilerParams(vmem_limit_bytes=8 * MIB),
        cost_estimate=estimate(1),
        name="response",
    )(*metas)

    for k in range(2, far):
        ahead = [turn(value, 1) for value in ahead]
        behind = [turn(value, -1) for value in behind[::-1]][::-1]
        parts += ahead + behind
        steps += [-k, -k, k, k]
        firsts += [0, middle] * 2
        if k == 2:
            behind[0], pieces = lax.optimization_barrier((behind[0], pieces))
        if k == 3:
            behind[0], gram = lax.optimization_barrier((behind[0], gram))
    ends = [turn(ahead[0], 1), turn(behind[1], -1)]

    whole = pltpu.VMEM((slots, 4, count, LANES), jnp.float32)
    sums = pl.pallas_call(
        lambda *refs: forward_kernel(steps, firsts, *refs),
        out_shape=whole,
        in_specs=[vmem()] * (2 + len(parts)),
        out_specs=vmem(),
        scratch_shapes=[pltpu.VMEM((slots, 4, degrees), jnp.float32)],
        compiler_params=pltpu.CompilerParams(vmem_limit_bytes=24 * MIB),
        cost_estimate=estimate(2),
        name="forward",
    )(meta, tables, *parts)
    phases, *outs = pl.pallas_call(
        lambda *refs: phases_kernel(groups, *refs),
        out_shape=[shape(count, LANES)] + [shape(count + 8, LANES)] * (groups - 1),
        in_specs=[vmem()] * 6,
        out_specs=[vmem()] * groups,
        compiler_params=pltpu.CompilerParams(vmem_limit_bytes=16 * MIB),
        cost_estimate=estimate(1),
        name="phases",
    )(meta, tables, pieces, sums, *ends)
    messages = [swap(outs[d - 1], "order", d) for d in range(1, groups)]

    half = pltpu.VMEM((middle, 4, width), jnp.float32)
    *sends, analysed = pl.pallas_call(
        lambda *refs: analysed_kernel(groups, cycles, *refs),
        out_shape=[half] * 4 + [whole],
        in_specs=[vmem()] * (3 + groups),
        out_specs=[vmem()] * 5,
        scratch_shapes=[pltpu.VMEM((count, LANES), jnp.float32)],
        compiler_params=pltpu.CompilerParams(vmem_limit_bytes=16 * MIB),
        cost_estimate=estimate(1),
        name="analysed",
    )(tables, gram, pieces, phases, *messages)
    piece = pl.pallas_call(
        backward_kernel,
        out_shape=pltpu.VMEM((blocks, slots, 4, width), jnp.float32),
        in_specs=[vmem()] * 2,
        out_specs=vmem(),
        compiler_params=pltpu.CompilerParams(vmem_limit_bytes=16 * MIB),
        cost_estimate=estimate(2),
        name="backward",
    )(tables, analysed)

    def add(index, first, value):
        return pl.pallas_call(
            lambda *refs: add_kernel(index, first, *refs),
            out_shape=half,
            in_specs=[vmem()] * 2,
            out_specs=vmem(),
            compiler_params=pltpu.CompilerParams(vmem_limit_bytes=4 * MIB),
            cost_estimate=estimate(0.1),
            name="add",
        )(piece, pltpu.with_memory_space_constraint(value, pltpu.VMEM))

    sent = dict(zip(((1, 0), (-1, middle), (-1, 0), (1, middle)), sends))
    first_hop = {key: turn(sent[key], key[0]) for key in ((1, 0), (-1, middle))}
    for key in ((1, 0), (-1, middle)):
        sent[key] = add((key[0] * (far - 1)) % blocks, key[1], first_hop[key])
    for k in reversed(range(1, far)):
        for key in ((1, middle), (-1, 0), (1, 0), (-1, middle)):
            sent[key] = turn(sent[key], key[0])
            if k > 1:
                sent[key] = add((key[0] * (k - 1)) % blocks, key[1], sent[key])
    received = [sent[key] for key in ((1, 0), (1, middle), (-1, 0), (-1, middle))]
    refined = pl.pallas_call(
        final_kernel,
        out_shape=shape(*harmonics.shape),
        in_specs=[vmem()] * 7,
        out_specs=vmem(),
        compiler_params=pltpu.CompilerParams(vmem_limit_bytes=8 * MIB),
        cost_estimate=pl.CostEstimate(flops=10**5, bytes_accessed=10**6, transcendentals=0),
        name="refine",
    )(
        meta, harmonics, piece,
        *[pltpu.with_memory_space_constraint(value, pltpu.VMEM) for value in received],
    )

    residual = pl.pallas_call(
        lambda *refs: residual_kernel(groups, slots, cycles, *refs),
        out_shape=shape(cycles, 2 * rows, LANES),
        in_specs=[vmem()] * (4 + 2 * groups),
        out_specs=vmem(),
        scratch_shapes=[pltpu.VMEM((4, count, 2 * every), jnp.float32)],
        compiler_params=pltpu.CompilerParams(vmem_limit_bytes=16 * MIB),
        cost_estimate=pl.CostEstimate(flops=10**8, bytes_accessed=2 * MIB, transcendentals=0),
        name="residual",
    )(*metas, section, acs, asc, fine, phases, *messages)
    residual = residual.reshape(cycles, rows, 2, LANES).transpose(0, 2, 1, 3)
    return (refined, residual.reshape(sky_map.shape))


def solution(mesh):
    return jax.shard_map(
        body,
        mesh=mesh,
        in_specs=(
            P("order", None, "blk"),
            P("order", None, "blk", None),
            P(("blk", "order"), None, None),
            P(("blk", "order")),
            P(("blk", "order")),
            P(("blk", "order")),
            P("order"),
        ),
        out_specs=(P("order", None, "blk"), P(("blk", "order"), None, None)),
        check_vma=False,
    )
```

time: 73.6 us -> 64.2 us (0.87)
  waiting for transfers between devices: 34.5 us -> 17.5 us
  starting transfers between devices: 25.6 us -> 32.2 us
  Pallas kernels: 11.5 us -> 13.5 us
  local copies, waits for them, and re-layouts: 0.98 us -> 0.04 us
    ppermute x16 -> x26, waiting for transfers between devices: 29 us -> 14.5 us  [turn(): return lax.ppermute(value, 'blk', pairs)]
    ppermute x16 -> x26, starting transfers between devices: 21.6 us -> 28.2 us  [turn(): return lax.ppermute(value, 'blk', pairs)]
    pallas_call x8 -> x16, Pallas kernels: 4.66 us -> 8.92 us  [the longest x1 2.31 us: body(): pl.pallas_call(tables_kernel, out_shape=pltpu.VMEM(legendre.shape, jnp.fl...]
    ppermute x6, waiting for transfers between devices: 5.59 us -> 3.02 us  [swap(): return lax.ppermute(value, axis, [(i, i ^ step) for i in range(size)])]
    pallas_call x1, Pallas kernels: 3.58 us -> 1.77 us  [body(): pl.pallas_call(lambda *refs: sky_kernel(normalise, groups, slots, cycles,...]
    unnamed x6 -> x2, local copies, waits for them, and re-layouts: 0.96 us -> 0.01 us
  transfers between devices with their start and end apart: 22 -> 32, of which waited for: 16 -> 21; matrix products, arithmetic and copies ran while one was open for 0% -> 0% of each run, Pallas kernels for 8% -> 16%
where the time goes in v3:
time: 64.2 us; the launch traced here: 64 us
  starting transfers between devices  32.2 us (50%)
  waiting for transfers between devices  17.5 us (27%)
  Pallas kernels  13.5 us (21%)
  between operations  0.8 us (1%)
    ppermute x26, starting transfers between devices, turn(): return lax.ppermute(value, 'blk', pairs)  28.2 us
    ppermute x26, waiting for transfers between devices, turn(): return lax.ppermute(value, 'blk', pairs)  14.5 us
    ppermute x6, starting transfers between devices, swap(): return lax.ppermute(value, axis, [(i, i ^ step) for i in range(size)])  4 us
    ppermute x6, waiting for transfers between devices, swap(): return lax.ppermute(value, axis, [(i, i ^ step) for i in range(size)])  3.02 us
    pallas_call x1, Pallas kernels, body(): pl.pallas_call(tables_kernel, out_shape=pltpu.VMEM(legendre.shape, jnp.fl...  2.31 us
    pallas_call x1, Pallas kernels, body(): pl.pallas_call(backward_kernel, out_shape=pltpu.VMEM((blocks, slots, 4, w...  1.92 us
    pallas_call x1, Pallas kernels, body(): pl.pallas_call(lambda *refs: sky_kernel(normalise, groups, slots, cycles,...  1.77 us
    pallas_call x1, Pallas kernels, body(): pl.pallas_call(lambda *refs: forward_kernel(steps, firsts, *refs), out_sh...  1.52 us
  transfers between devices with their start and end apart: 32, of which 21 were waited for; matrix products, arithmetic and copies ran while one was open for 0% of the time, Pallas kernels for 16%

profile of v3, /device:TPU:0, one launch (start us, length us, event | category | flops | bytes accessed | tf_op | source)
XLA Modules:
  0.0 64.0 jit_solution(2255306711462741869)
XLA Ops:
  0.6 3.0 %collective-permute-start = (f32[16,4,1024]{2,1,0:T(4,128)}, f32[16,4,1024]{2,1,0:T(4,128)S(1)}, u32[]{:S(2)}, u32[]{:S(2)}) collective-permute-start(f32[16,4,1024]{2,1,0:T(4,128)} %harmonics_ref.1), channel_id=1, source_target_pairs={{0,4},{8,0},{16,8},{24,16},{28,24},{20,28},{12,20},{4,12},{1,5},{9... | collective-permute-start | bytes 786440 | tf_op jit(solution)/shard_map/ppermute | solution.py:466
  4.6 1.9 %collective-permute-start.2 = (f32[1,128]{1,0:T(1,128)S(1)}, f32[1,128]{1,0:T(1,128)S(1)}, u32[]{:S(2)}, u32[]{:S(2)}) collective-permute-start(f32[1,128]{1,0:T(1,128)S(1)} %meta.1.refs_0_.meta_ref), channel_id=1, source_target_pairs={{0,2},{1,3},{2,0},{3,1},{4,6},{5,7},{6,4},{7,5},{8,10},{9,11},{10,... | collective-permute-start | bytes 1544 | tf_op jit(solution)/shard_map/ppermute | solution.py:460
  6.6 2.3 %tables.1.refs_1_.refs_0_ = f32[16,2,8,8192]{3,2,1,0:T(8,128)S(1)} custom-call(f32[16,2,8,8192]{3,2,1,0:T(8,128)} %legendre.1), custom_call_target="tpu_custom_call" | custom-call | bytes 4500000 | tf_op jit(solution)/shard_map/tables/pallas_call | solution.py:489
  10.2 1.7 %collective-permute-start.9 = (f32[8,4,1024]{2,1,0:T(4,128)S(1)}, f32[8,4,1024]{2,1,0:T(4,128)S(1)}, u32[]{:S(2)}, u32[]{:S(2)}) collective-permute-start(f32[8,4,1024]{2,1,0:T(4,128)S(1)} %get-tuple-element.48), channel_id=1, source_target_pairs={{0,4},{8,0},{16,8},{24,16},{28,24},{20,28},{12,20},{4,12},{1,5},{9... | collective-permute-start | bytes 393224 | tf_op jit(solution)/shard_map/ppermute | solution.py:466
  12.4 1.7 %collective-permute-start.4 = (f32[8,4,1024]{2,1,0:T(4,128)S(1)}, f32[8,4,1024]{2,1,0:T(4,128)S(1)}, u32[]{:S(2)}, u32[]{:S(2)}) collective-permute-start(f32[8,4,1024]{2,1,0:T(4,128)S(1)} %get-tuple-element.49), channel_id=1, source_target_pairs={{0,4},{8,0},{16,8},{24,16},{28,24},{20,28},{12,20},{4,12},{1,5},{9... | collective-permute-start | bytes 393224 | tf_op jit(solution)/shard_map/ppermute | solution.py:466
  14.4 2.3 %collective-permute-done.9.refs_8_ = f32[8,4,1024]{2,1,0:T(4,128)S(1)} collective-permute-done((f32[8,4,1024]{2,1,0:T(4,128)S(1)}, f32[8,4,1024]{2,1,0:T(4,128)S(1)}, u32[]{:S(2)}, u32[]{:S(2)}) %collective-permute-start.9) | collective-permute-done | bytes 131104 | tf_op jit(solution)/shard_map/ppermute | solution.py:466
  16.7 1.5 %collective-permute-start.12 = (f32[8,4,1024]{2,1,0:T(4,128)S(1)}, f32[8,4,1024]{2,1,0:T(4,128)S(1)}, u32[]{:S(2)}, u32[]{:S(2)}) collective-permute-start(f32[8,4,1024]{2,1,0:T(4,128)S(1)} %collective-permute-done.9.refs_8_), channel_id=1, source_target_pairs={{0,4},{8,0},{16,8},{24,16},{28,24},{20,28},{12,20},{4,12},{1,5},{9... | collective-permute-start | bytes 393224 | tf_op jit(solution)/shard_map/ppermute | solution.py:466
  18.8 1.8 %sky_analysis.1 = (f32[4,8,128]{2,1,0:T(8,128)S(1)}, f32[2,256,128]{2,1,0:T(8,128)S(1)}, f32[2,256,128]{2,1,0:T(8,128)S(1)}, f32[2,128,128]{2,1,0:T(8,128)S(1)}, f32[2,256,128]{2,1,0:T(8,128)S(1)}) custom-call(f32[1,128]{1,0:T(1,128)S(1)} %meta.1.refs_0_.meta_ref, f32[1,128]{1,0:T(1,128)S(1)} %collective-permute-done.1.refs_1_, ...), custom_call_target="tpu_custom_call" | custom-call | bytes 9000000 | tf_op jit(solution)/shard_map/sky_analysis/pallas_call | solution.py:505
  20.6 1.6 %collective-permute-start.5 = (f32[8,4,1024]{2,1,0:T(4,128)S(1)}, f32[8,4,1024]{2,1,0:T(4,128)S(1)}, u32[]{:S(2)}, u32[]{:S(2)}) collective-permute-start(f32[8,4,1024]{2,1,0:T(4,128)S(1)} %collective-permute-done.4.refs_7_), channel_id=1, source_target_pairs={{0,4},{8,0},{16,8},{24,16},{28,24},{20,28},{12,20},{4,12},{1,5},{9... | collective-permute-start | bytes 393224 | tf_op jit(solution)/shard_map/ppermute | solution.py:466
  23.1 1.5 %collective-permute-start.14 = (f32[8,4,1024]{2,1,0:T(4,128)S(1)}, f32[8,4,1024]{2,1,0:T(4,128)S(1)}, u32[]{:S(2)}, u32[]{:S(2)}) collective-permute-start(f32[8,4,1024]{2,1,0:T(4,128)S(1)} %collective-permute-done.12.refs_12_), channel_id=1, source_target_pairs={{0,4},{8,0},{16,8},{24,16},{28,24},{20,28},{12,20},{4,12},{1,5},{9... | collective-permute-start | bytes 393224 | tf_op jit(solution)/shard_map/ppermute | solution.py:466
  27.2 1.5 %forward.1.refs_3_ = f32[16,4,8,128]{3,2,1,0:T(8,128)S(1)} custom-call(f32[1,128]{1,0:T(1,128)S(1)} %meta.1.refs_0_.meta_ref, f32[16,2,8,8192]{3,2,1,0:T(8,128)S(1)} %tables.1.refs_1_.refs_0_, f32[16,4,1024]{2,1,0:T(4,128)S(1)} %copy-done, f32[16,4,1024]{2,1,0:T(4,128)S(1)} %collective-permute-done.6.refs_3_, ...), custom_call_target="tpu_custom_call" | custom-call | bytes 6000000 | tf_op jit(solution)/shard_map/forward/pallas_call | solution.py:547
  29.6 1.5 %phases.1 = (f32[8,128]{1,0:T(8,128)S(1)}, f32[16,128]{1,0:T(8,128)S(1)}, f32[16,128]{1,0:T(8,128)S(1)}, f32[16,128]{1,0:T(8,128)S(1)}) custom-call(f32[1,128]{1,0:T(1,128)S(1)} %meta.1.refs_0_.meta_ref, f32[16,2,8,8192]{3,2,1,0:T(8,128)S(1)} %tables.1.refs_1_.refs_0_, f32[4,8,128]{2,1,0:T(8,128)S(1)} %get-tuple-element.34.refs_2_, ...), custom_call_target="tpu_custom_call" | custom-call | bytes 3000000 | tf_op jit(solution)/shard_map/phases/pallas_call | solution.py:557
  31.2 1.6 %collective-permute-start.16 = (f32[16,128]{1,0:T(8,128)S(1)}, f32[16,128]{1,0:T(8,128)S(1)}, u32[]{:S(2)}, u32[]{:S(2)}) collective-permute-start(f32[16,128]{1,0:T(8,128)S(1)} %get-tuple-element.37), channel_id=1, source_target_pairs={{0,2},{1,3},{2,0},{3,1},{4,6},{5,7},{6,4},{7,5},{8,10},{9,11},{10,... | collective-permute-start | bytes 24584 | tf_op jit(solution)/shard_map/ppermute | solution.py:460
  33.4 1.5 %collective-permute-done.16.refs_5_.refs_10_ = f32[16,128]{1,0:T(8,128)S(1)} collective-permute-done((f32[16,128]{1,0:T(8,128)S(1)}, f32[16,128]{1,0:T(8,128)S(1)}, u32[]{:S(2)}, u32[]{:S(2)}) %collective-permute-start.16) | collective-permute-done | bytes 8224 | tf_op jit(solution)/shard_map/ppermute | solution.py:460
  37.0 1.6 %collective-permute-start.28 = (f32[8,4,1024]{2,1,0:T(4,128)S(1)}, f32[8,4,1024]{2,1,0:T(4,128)S(1)}, u32[]{:S(2)}, u32[]{:S(2)}) collective-permute-start(f32[8,4,1024]{2,1,0:T(4,128)S(1)} %get-tuple-element.43), channel_id=1, source_target_pairs={{0,4},{8,0},{16,8},{24,16},{28,24},{20,28},{12,20},{4,12},{1,5},{9... | collective-permute-start | bytes 393224 | tf_op jit(solution)/shard_map/ppermute | solution.py:466
  39.1 1.6 %collective-permute-start.25 = (f32[8,4,1024]{2,1,0:T(4,128)S(1)}, f32[8,4,1024]{2,1,0:T(4,128)S(1)}, u32[]{:S(2)}, u32[]{:S(2)}) collective-permute-start(f32[8,4,1024]{2,1,0:T(4,128)S(1)} %get-tuple-element.42), channel_id=1, source_target_pairs={{0,4},{8,0},{16,8},{24,16},{28,24},{20,28},{12,20},{4,12},{1,5},{9... | collective-permute-start | bytes 393224 | tf_op jit(solution)/shard_map/ppermute | solution.py:466
  40.7 1.9 %backward.1.refs_0_.piece_ref = f32[8,16,4,1024]{3,2,1,0:T(4,128)S(1)} custom-call(f32[16,2,8,8192]{3,2,1,0:T(8,128)S(1)} %tables.1.refs_1_.refs_0_, f32[16,4,8,128]{3,2,1,0:T(8,128)S(1)} %get-tuple-element.39.analysed_ref), custom_call_target="tpu_custom_call" | custom-call | bytes 6000000 | tf_op jit(solution)/shard_map/backward/pallas_call | solution.py:579
  43.4 1.6 %collective-permute-start.29 = (f32[8,4,1024]{2,1,0:T(4,128)S(1)}, f32[8,4,1024]{2,1,0:T(4,128)S(1)}, u32[]{:S(2)}, u32[]{:S(2)}) collective-permute-start(f32[8,4,1024]{2,1,0:T(4,128)S(1)} %add.17), channel_id=1, source_target_pairs={{0,4},{8,0},{16,8},{24,16},{28,24},{20,28},{12,20},{4,12},{1,5},{9... | collective-permute-start | bytes 393224 | tf_op jit(solution)/shard_map/ppermute | solution.py:466
  46.0 1.6 %collective-permute-start.26 = (f32[8,4,1024]{2,1,0:T(4,128)S(1)}, f32[8,4,1024]{2,1,0:T(4,128)S(1)}, u32[]{:S(2)}, u32[]{:S(2)}) collective-permute-start(f32[8,4,1024]{2,1,0:T(4,128)S(1)} %add.15), channel_id=1, source_target_pairs={{0,4},{8,0},{16,8},{24,16},{28,24},{20,28},{12,20},{4,12},{1,5},{9... | collective-permute-start | bytes 393224 | tf_op jit(solution)/shard_map/ppermute | solution.py:466
  47.7 1.3 %collective-permute-done.22.refs_1_ = f32[8,4,1024]{2,1,0:T(4,128)S(1)} collective-permute-done((f32[8,4,1024]{2,1,0:T(4,128)S(1)}, f32[8,4,1024]{2,1,0:T(4,128)S(1)}, u32[]{:S(2)}, u32[]{:S(2)}) %collective-permute-start.22) | collective-permute-done | bytes 131104 | tf_op jit(solution)/shard_map/ppermute | solution.py:466
  49.6 1.6 %collective-permute-start.30 = (f32[8,4,1024]{2,1,0:T(4,128)S(1)}, f32[8,4,1024]{2,1,0:T(4,128)S(1)}, u32[]{:S(2)}, u32[]{:S(2)}) collective-permute-start(f32[8,4,1024]{2,1,0:T(4,128)S(1)} %add.18), channel_id=1, source_target_pairs={{0,4},{8,0},{16,8},{24,16},{28,24},{20,28},{12,20},{4,12},{1,5},{9... | collective-permute-start | bytes 393224 | tf_op jit(solution)/shard_map/ppermute | solution.py:466
  52.5 1.6 %collective-permute-start.27 = (f32[8,4,1024]{2,1,0:T(4,128)S(1)}, f32[8,4,1024]{2,1,0:T(4,128)S(1)}, u32[]{:S(2)}, u32[]{:S(2)}) collective-permute-start(f32[8,4,1024]{2,1,0:T(4,128)S(1)} %add.16), channel_id=1, source_target_pairs={{0,4},{8,0},{16,8},{24,16},{28,24},{20,28},{12,20},{4,12},{1,5},{9... | collective-permute-start | bytes 393224 | tf_op jit(solution)/shard_map/ppermute | solution.py:466
  55.8 1.6 %collective-permute-start.31 = (f32[8,4,1024]{2,1,0:T(4,128)S(1)}, f32[8,4,1024]{2,1,0:T(4,128)S(1)}, u32[]{:S(2)}, u32[]{:S(2)}) collective-permute-start(f32[8,4,1024]{2,1,0:T(4,128)S(1)} %add.19), channel_id=1, source_target_pairs={{0,4},{8,0},{16,8},{24,16},{28,24},{20,28},{12,20},{4,12},{1,5},{9... | collective-permute-start | bytes 393224 | tf_op jit(solution)/shard_map/ppermute | solution.py:466
  60.8 2.3 %collective-permute-done.21.rest_0_ = f32[8,4,1024]{2,1,0:T(4,128)S(1)} collective-permute-done((f32[8,4,1024]{2,1,0:T(4,128)S(1)}, f32[8,4,1024]{2,1,0:T(4,128)S(1)}, u32[]{:S(2)}, u32[]{:S(2)}) %collective-permute-start.21) | collective-permute-done | bytes 131104 | tf_op jit(solution)/shard_map/ppermute | solution.py:466
  (64 shorter events, 20.7 us)
Async XLA Ops:
  0.6 9.6 %collective-permute-start = (f32[16,4,1024]{2,1,0:T(4,128)}, f32[16,4,1024]{2,1,0:T(4,128)S(1)}, u32[]{:S(2)}, u32[]{:S(2)}) collective-permute-start(f32[16,4,1024]{2,1,0:T(4,128)} %harmonics_ref.1), channel_id=1, source_target_pairs={{0,4},{8,0},{16,8},{24,16},{28,24},{20,28},{12,20},{4,12},{1,5},{9... | collective-permute-start | bytes 786440 | tf_op jit(solution)/shard_map/ppermute | solution.py:466
  3.7 8.3 %collective-permute-start.6 = (f32[16,4,1024]{2,1,0:T(4,128)}, f32[16,4,1024]{2,1,0:T(4,128)S(1)}, u32[]{:S(2)}, u32[]{:S(2)}) collective-permute-start(f32[16,4,1024]{2,1,0:T(4,128)} %harmonics_ref.1), channel_id=1, source_target_pairs={{0,8},{8,16},{16,24},{24,28},{28,20},{20,12},{12,4},{4,0},{1,9},{9... | collective-permute-start | bytes 786440 | tf_op jit(solution)/shard_map/ppermute | solution.py:466
  10.2 6.5 %collective-permute-start.9 = (f32[8,4,1024]{2,1,0:T(4,128)S(1)}, f32[8,4,1024]{2,1,0:T(4,128)S(1)}, u32[]{:S(2)}, u32[]{:S(2)}) collective-permute-start(f32[8,4,1024]{2,1,0:T(4,128)S(1)} %get-tuple-element.48), channel_id=1, source_target_pairs={{0,4},{8,0},{16,8},{24,16},{28,24},{20,28},{12,20},{4,12},{1,5},{9... | collective-permute-start | bytes 393224 | tf_op jit(solution)/shard_map/ppermute | solution.py:466
  12.0 6.3 %collective-permute-start.7 = (f32[8,4,1024]{2,1,0:T(4,128)S(1)}, f32[8,4,1024]{2,1,0:T(4,128)S(1)}, u32[]{:S(2)}, u32[]{:S(2)}) collective-permute-start(f32[8,4,1024]{2,1,0:T(4,128)S(1)} %get-tuple-element.51), channel_id=1, source_target_pairs={{0,8},{8,16},{16,24},{24,28},{28,20},{20,12},{12,4},{4,0},{1,9},{9... | collective-permute-start | bytes 393224 | tf_op jit(solution)/shard_map/ppermute | solution.py:466
  12.4 8.2 %collective-permute-start.4 = (f32[8,4,1024]{2,1,0:T(4,128)S(1)}, f32[8,4,1024]{2,1,0:T(4,128)S(1)}, u32[]{:S(2)}, u32[]{:S(2)}) collective-permute-start(f32[8,4,1024]{2,1,0:T(4,128)S(1)} %get-tuple-element.49), channel_id=1, source_target_pairs={{0,4},{8,0},{16,8},{24,16},{28,24},{20,28},{12,20},{4,12},{1,5},{9... | collective-permute-start | bytes 393224 | tf_op jit(solution)/shard_map/ppermute | solution.py:466
  14.1 8.1 %collective-permute-start.8 = (f32[8,4,1024]{2,1,0:T(4,128)S(1)}, f32[8,4,1024]{2,1,0:T(4,128)S(1)}, u32[]{:S(2)}, u32[]{:S(2)}) collective-permute-start(f32[8,4,1024]{2,1,0:T(4,128)S(1)} %get-tuple-element.50), channel_id=1, source_target_pairs={{0,8},{8,16},{16,24},{24,28},{28,20},{20,12},{12,4},{4,0},{1,9},{9... | collective-permute-start | bytes 393224 | tf_op jit(solution)/shard_map/ppermute | solution.py:466
  16.7 6.4 %collective-permute-start.12 = (f32[8,4,1024]{2,1,0:T(4,128)S(1)}, f32[8,4,1024]{2,1,0:T(4,128)S(1)}, u32[]{:S(2)}, u32[]{:S(2)}) collective-permute-start(f32[8,4,1024]{2,1,0:T(4,128)S(1)} %collective-permute-done.9.refs_8_), channel_id=1, source_target_pairs={{0,4},{8,0},{16,8},{24,16},{28,24},{20,28},{12,20},{4,12},{1,5},{9... | collective-permute-start | bytes 393224 | tf_op jit(solution)/shard_map/ppermute | solution.py:466
  18.3 6.3 %collective-permute-start.10 = (f32[8,4,1024]{2,1,0:T(4,128)S(1)}, f32[8,4,1024]{2,1,0:T(4,128)S(1)}, u32[]{:S(2)}, u32[]{:S(2)}) collective-permute-start(f32[8,4,1024]{2,1,0:T(4,128)S(1)} %collective-permute-done.7.refs_5_), channel_id=1, source_target_pairs={{0,8},{8,16},{16,24},{24,28},{28,20},{20,12},{12,4},{4,0},{1,9},{9... | collective-permute-start | bytes 393224 | tf_op jit(solution)/shard_map/ppermute | solution.py:466
  20.6 5.3 %collective-permute-start.5 = (f32[8,4,1024]{2,1,0:T(4,128)S(1)}, f32[8,4,1024]{2,1,0:T(4,128)S(1)}, u32[]{:S(2)}, u32[]{:S(2)}) collective-permute-start(f32[8,4,1024]{2,1,0:T(4,128)S(1)} %collective-permute-done.4.refs_7_), channel_id=1, source_target_pairs={{0,4},{8,0},{16,8},{24,16},{28,24},{20,28},{12,20},{4,12},{1,5},{9... | collective-permute-start | bytes 393224 | tf_op jit(solution)/shard_map/ppermute | solution.py:466
  23.1 5.6 %collective-permute-start.14 = (f32[8,4,1024]{2,1,0:T(4,128)S(1)}, f32[8,4,1024]{2,1,0:T(4,128)S(1)}, u32[]{:S(2)}, u32[]{:S(2)}) collective-permute-start(f32[8,4,1024]{2,1,0:T(4,128)S(1)} %collective-permute-done.12.refs_12_), channel_id=1, source_target_pairs={{0,4},{8,0},{16,8},{24,16},{28,24},{20,28},{12,20},{4,12},{1,5},{9... | collective-permute-start | bytes 393224 | tf_op jit(solution)/shard_map/ppermute | solution.py:466
  37.0 6.4 %collective-permute-start.28 = (f32[8,4,1024]{2,1,0:T(4,128)S(1)}, f32[8,4,1024]{2,1,0:T(4,128)S(1)}, u32[]{:S(2)}, u32[]{:S(2)}) collective-permute-start(f32[8,4,1024]{2,1,0:T(4,128)S(1)} %get-tuple-element.43), channel_id=1, source_target_pairs={{0,4},{8,0},{16,8},{24,16},{28,24},{20,28},{12,20},{4,12},{1,5},{9... | collective-permute-start | bytes 393224 | tf_op jit(solution)/shard_map/ppermute | solution.py:466
  38.6 6.4 %collective-permute-start.18 = (f32[8,4,1024]{2,1,0:T(4,128)S(1)}, f32[8,4,1024]{2,1,0:T(4,128)S(1)}, u32[]{:S(2)}, u32[]{:S(2)}) collective-permute-start(f32[8,4,1024]{2,1,0:T(4,128)S(1)} %get-tuple-element.40), channel_id=1, source_target_pairs={{0,8},{8,16},{16,24},{24,28},{28,20},{20,12},{12,4},{4,0},{1,9},{9... | collective-permute-start | bytes 393224 | tf_op jit(solution)/shard_map/ppermute | solution.py:466
  39.1 6.9 %collective-permute-start.25 = (f32[8,4,1024]{2,1,0:T(4,128)S(1)}, f32[8,4,1024]{2,1,0:T(4,128)S(1)}, u32[]{:S(2)}, u32[]{:S(2)}) collective-permute-start(f32[8,4,1024]{2,1,0:T(4,128)S(1)} %get-tuple-element.42), channel_id=1, source_target_pairs={{0,4},{8,0},{16,8},{24,16},{28,24},{20,28},{12,20},{4,12},{1,5},{9... | collective-permute-start | bytes 393224 | tf_op jit(solution)/shard_map/ppermute | solution.py:466
  42.6 6.4 %collective-permute-start.22 = (f32[8,4,1024]{2,1,0:T(4,128)S(1)}, f32[8,4,1024]{2,1,0:T(4,128)S(1)}, u32[]{:S(2)}, u32[]{:S(2)}) collective-permute-start(f32[8,4,1024]{2,1,0:T(4,128)S(1)} %get-tuple-element.41), channel_id=1, source_target_pairs={{0,8},{8,16},{16,24},{24,28},{28,20},{20,12},{12,4},{4,0},{1,9},{9... | collective-permute-start | bytes 393224 | tf_op jit(solution)/shard_map/ppermute | solution.py:466
  43.4 6.1 %collective-permute-start.29 = (f32[8,4,1024]{2,1,0:T(4,128)S(1)}, f32[8,4,1024]{2,1,0:T(4,128)S(1)}, u32[]{:S(2)}, u32[]{:S(2)}) collective-permute-start(f32[8,4,1024]{2,1,0:T(4,128)S(1)} %add.17), channel_id=1, source_target_pairs={{0,4},{8,0},{16,8},{24,16},{28,24},{20,28},{12,20},{4,12},{1,5},{9... | collective-permute-start | bytes 393224 | tf_op jit(solution)/shard_map/ppermute | solution.py:466
  45.1 6.7 %collective-permute-start.19 = (f32[8,4,1024]{2,1,0:T(4,128)S(1)}, f32[8,4,1024]{2,1,0:T(4,128)S(1)}, u32[]{:S(2)}, u32[]{:S(2)}) collective-permute-start(f32[8,4,1024]{2,1,0:T(4,128)S(1)} %add.10), channel_id=1, source_target_pairs={{0,8},{8,16},{16,24},{24,28},{28,20},{20,12},{12,4},{4,0},{1,9},{9... | collective-permute-start | bytes 393224 | tf_op jit(solution)/shard_map/ppermute | solution.py:466
  46.0 6.5 %collective-permute-start.26 = (f32[8,4,1024]{2,1,0:T(4,128)S(1)}, f32[8,4,1024]{2,1,0:T(4,128)S(1)}, u32[]{:S(2)}, u32[]{:S(2)}) collective-permute-start(f32[8,4,1024]{2,1,0:T(4,128)S(1)} %add.15), channel_id=1, source_target_pairs={{0,4},{8,0},{16,8},{24,16},{28,24},{20,28},{12,20},{4,12},{1,5},{9... | collective-permute-start | bytes 393224 | tf_op jit(solution)/shard_map/ppermute | solution.py:466
  49.0 5.6 %collective-permute-start.23 = (f32[8,4,1024]{2,1,0:T(4,128)S(1)}, f32[8,4,1024]{2,1,0:T(4,128)S(1)}, u32[]{:S(2)}, u32[]{:S(2)}) collective-permute-start(f32[8,4,1024]{2,1,0:T(4,128)S(1)} %add.13), channel_id=1, source_target_pairs={{0,8},{8,16},{16,24},{24,28},{28,20},{20,12},{12,4},{4,0},{1,9},{9... | collective-permute-start | bytes 393224 | tf_op jit(solution)/shard_map/ppermute | solution.py:466
  49.6 6.2 %collective-permute-start.30 = (f32[8,4,1024]{2,1,0:T(4,128)S(1)}, f32[8,4,1024]{2,1,0:T(4,128)S(1)}, u32[]{:S(2)}, u32[]{:S(2)}) collective-permute-start(f32[8,4,1024]{2,1,0:T(4,128)S(1)} %add.18), channel_id=1, source_target_pairs={{0,4},{8,0},{16,8},{24,16},{28,24},{20,28},{12,20},{4,12},{1,5},{9... | collective-permute-start | bytes 393224 | tf_op jit(solution)/shard_map/ppermute | solution.py:466
  51.8 6.3 %collective-permute-start.20 = (f32[8,4,1024]{2,1,0:T(4,128)S(1)}, f32[8,4,1024]{2,1,0:T(4,128)S(1)}, u32[]{:S(2)}, u32[]{:S(2)}) collective-permute-start(f32[8,4,1024]{2,1,0:T(4,128)S(1)} %add.11), channel_id=1, source_target_pairs={{0,8},{8,16},{16,24},{24,28},{28,20},{20,12},{12,4},{4,0},{1,9},{9... | collective-permute-start | bytes 393224 | tf_op jit(solution)/shard_map/ppermute | solution.py:466
  52.5 7.3 %collective-permute-start.27 = (f32[8,4,1024]{2,1,0:T(4,128)S(1)}, f32[8,4,1024]{2,1,0:T(4,128)S(1)}, u32[]{:S(2)}, u32[]{:S(2)}) collective-permute-start(f32[8,4,1024]{2,1,0:T(4,128)S(1)} %add.16), channel_id=1, source_target_pairs={{0,4},{8,0},{16,8},{24,16},{28,24},{20,28},{12,20},{4,12},{1,5},{9... | collective-permute-start | bytes 393224 | tf_op jit(solution)/shard_map/ppermute | solution.py:466
  54.6 5.6 %collective-permute-start.24 = (f32[8,4,1024]{2,1,0:T(4,128)S(1)}, f32[8,4,1024]{2,1,0:T(4,128)S(1)}, u32[]{:S(2)}, u32[]{:S(2)}) collective-permute-start(f32[8,4,1024]{2,1,0:T(4,128)S(1)} %add.14), channel_id=1, source_target_pairs={{0,8},{8,16},{16,24},{24,28},{28,20},{20,12},{12,4},{4,0},{1,9},{9... | collective-permute-start | bytes 393224 | tf_op jit(solution)/shard_map/ppermute | solution.py:466
  55.8 5.0 %collective-permute-start.31 = (f32[8,4,1024]{2,1,0:T(4,128)S(1)}, f32[8,4,1024]{2,1,0:T(4,128)S(1)}, u32[]{:S(2)}, u32[]{:S(2)}) collective-permute-start(f32[8,4,1024]{2,1,0:T(4,128)S(1)} %add.19), channel_id=1, source_target_pairs={{0,4},{8,0},{16,8},{24,16},{28,24},{20,28},{12,20},{4,12},{1,5},{9... | collective-permute-start | bytes 393224 | tf_op jit(solution)/shard_map/ppermute | solution.py:466
  58.2 5.0 %collective-permute-start.21 = (f32[8,4,1024]{2,1,0:T(4,128)S(1)}, f32[8,4,1024]{2,1,0:T(4,128)S(1)}, u32[]{:S(2)}, u32[]{:S(2)}) collective-permute-start(f32[8,4,1024]{2,1,0:T(4,128)S(1)} %add.12), channel_id=1, source_target_pairs={{0,8},{8,16},{16,24},{24,28},{28,20},{20,12},{12,4},{4,0},{1,9},{9... | collective-permute-start | bytes 393224 | tf_op jit(solution)/shard_map/ppermute | solution.py:466
  (9 other events, 53.4 us)

commit v4 on v3

--- a/solution.py
+++ b/solution.py
@@ -211,8 +211,28 @@
         n[a] = n[a] + minus * c
 
 
+def fold_lanes(values, lane):
+    step = 1
+    while step < LANES:
+        if len(values) > 1:
+            low = (lane & step) == 0
+            values = [
+                jnp.where(low, values[i], values[i + 1])
+                + pltpu.roll(jnp.where(low, values[i + 1], values[i]), step, 1)
+                for i in range(0, len(values), 2)
+            ]
+        else:
+            values = [values[0] + pltpu.roll(values[0], step, 1)]
+        step *= 2
+    return values[0]
+
+
 def combine(p, n):
     return [n[3] - p[0], -p[1] - n[2], -p[2] - n[1], n[0] - p[3]]
+
+
+def on_core(core):
+    return lax.axis_index("order") % 2 == core
 
 
 def tables_kernel(legendre, tables, sems):
@@ -261,7 +281,7 @@
     place = ring_place(lax.axis_index("blk"), blocks)
     first = pl.multiple_of(block_at(place + blocks // 2, blocks) * width, LANES)
     lane = lax.broadcasted_iota(jnp.int32, (count, LANES), 1)
-    phases = jnp.zeros((count, LANES), jnp.float32)
+    totals = [None] * (4 * slots)
     for m in range(slots):
         floor = jnp.maximum(entry(meta, m).astype(jnp.int32), 2) - first
         part, at = (low_ref, m) if m < middle else (high_ref, m - middle)
@@ -273,8 +293,8 @@
             span = pl.ds(first + t * LANES, LANES)
             use_tile(tables, m, span, keep, lambda a: part[at, a : a + 1, here], p, n)
         for a, total in enumerate(combine(p, n)):
-            value = jnp.sum(total + sums_ref[m, a], axis=1, keepdims=True)
-            phases = jnp.where(lane == a * slots + m, value, phases)
+            totals[a * slots + m] = total + sums_ref[m, a]
+    phases = fold_lanes(totals, lane)
     phases_ref[...] = phases
     for d in range(1, groups):
         messages[d - 1][:count] = phases
@@ -360,7 +380,11 @@
                     part[at, :, u * LANES : (u + 1) * LANES] = folded[4 * k : 4 * k + 4]
 
 
-def backward_kernel(tables, analysed_ref, out):
+def backward_kernel(core, tables, analysed_ref, *rest):
+    pl.when(on_core(core))(lambda: backward_blocks(tables, analysed_ref, rest[-1]))
+
+
+def backward_blocks(tables, analysed_ref, out):
     slots, _, _, degrees = tables.shape
     blocks, _, _, width = out.shape
     stratum = degrees // slots
@@ -496,7 +520,7 @@
         cost_estimate=estimate(1.5),
         name="tables",
     )(pltpu.with_memory_space_constraint(legendre, pltpu.HBM))
-    behind, tables, *metas = lax.optimization_barrier((behind, tables, *metas))
+    ahead, tables, *metas = lax.optimization_barrier((ahead, tables, *metas))
     ahead = [ahead[:middle], ahead[middle:]]
     behind = [behind[:middle], behind[middle:]]
 
@@ -538,9 +562,7 @@
         steps += [-k, -k, k, k]
         firsts += [0, middle] * 2
         if k == 2:
-            behind[0], pieces = lax.optimization_barrier((behind[0], pieces))
-        if k == 3:
-            behind[0], gram = lax.optimization_barrier((behind[0], gram))
+            ahead[0], pieces = lax.optimization_barrier((ahead[0], pieces))
     ends = [turn(ahead[0], 1), turn(behind[1], -1)]
 
     whole = pltpu.VMEM((slots, 4, count, LANES), jnp.float32)
@@ -576,15 +598,24 @@
         cost_estimate=estimate(1),
         name="analysed",
     )(tables, gram, pieces, phases, *messages)
-    piece = pl.pallas_call(
-        backward_kernel,
-        out_shape=pltpu.VMEM((blocks, slots, 4, width), jnp.float32),
-        in_specs=[vmem()] * 2,
-        out_specs=vmem(),
-        compiler_params=pltpu.CompilerParams(vmem_limit_bytes=16 * MIB),
-        cost_estimate=estimate(2),
-        name="backward",
-    )(tables, analysed)
+    def backward(core, *before):
+        return pl.pallas_call(
+            lambda *refs: backward_kernel(core, *refs),
+            out_shape=pltpu.VMEM((blocks, slots, 4, width), jnp.float32),
+            in_specs=[vmem()] * 2 + [hbm] * len(before),
+            out_specs=vmem(),
+            input_output_aliases={2: 0} if before else {},
+            compiler_params=pltpu.CompilerParams(vmem_limit_bytes=16 * MIB),
+            cost_estimate=estimate(2),
+            name="backward",
+        )(
+            tables, analysed,
+            *[pltpu.with_memory_space_constraint(value, pltpu.VMEM) for value in before],
+        )
+
+    piece = backward(1)
+    *sends, piece = lax.optimization_barrier((*sends, piece))
+    piece = backward(0, piece)
 
     def add(index, first, value):
         return pl.pallas_call(

time: 64.2 us -> 62 us (0.966)
  waiting for transfers between devices: 17.5 us -> 15.8 us
    ppermute x26, waiting for transfers between devices: 14.5 us -> 13.5 us  [turn(): return lax.ppermute(value, 'blk', pairs)]
    ppermute x6, waiting for transfers between devices: 3.02 us -> 2.27 us  [swap(): return lax.ppermute(value, axis, [(i, i ^ step) for i in range(size)])]
    pallas_call x1 -> x2, Pallas kernels: 1.92 us -> 1.94 us  [backward(): pl.pallas_call(lambda *refs: backward_kernel(core, *refs), out_shape=pltp...]
  transfers between devices with their start and end apart: 32 -> 32, of which waited for: 21 -> 20; matrix products, arithmetic and copies ran while one was open for 0% -> 0% of each run, Pallas kernels for 16% -> 16%
where the time goes in v4:
time: 62 us; the launch traced here: 61.8 us
  starting transfers between devices  32.1 us (52%)
  waiting for transfers between devices  15.8 us (25%)
  Pallas kernels  13.1 us (21%)
  between operations  0.78 us (1%)
    ppermute x26, starting transfers between devices, turn(): return lax.ppermute(value, 'blk', pairs)  28.1 us
    ppermute x26, waiting for transfers between devices, turn(): return lax.ppermute(value, 'blk', pairs)  13.5 us
    ppermute x6, starting transfers between devices, swap(): return lax.ppermute(value, axis, [(i, i ^ step) for i in range(size)])  3.98 us
    pallas_call x1, Pallas kernels, body(): pl.pallas_call(tables_kernel, out_shape=pltpu.VMEM(legendre.shape, jnp.fl...  2.31 us
    ppermute x6, waiting for transfers between devices, swap(): return lax.ppermute(value, axis, [(i, i ^ step) for i in range(size)])  2.27 us
    pallas_call x2, Pallas kernels, backward(): pl.pallas_call(lambda *refs: backward_kernel(core, *refs), out_shape=pltp...  1.94 us
    pallas_call x1, Pallas kernels, body(): pl.pallas_call(lambda *refs: sky_kernel(normalise, groups, slots, cycles,...  1.77 us
    pallas_call x1, Pallas kernels, body(): pl.pallas_call(lambda *refs: forward_kernel(steps, firsts, *refs), out_sh...  1.52 us
  transfers between devices with their start and end apart: 32, of which 20 were waited for; matrix products, arithmetic and copies ran while one was open for 0% of the time, Pallas kernels for 16%

profile of v4, /device:TPU:0, one launch (start us, length us, event | category | flops | bytes accessed | tf_op | source)
XLA Modules:
  0.0 61.8 jit_solution(14497638855242903576)
XLA Ops:
  0.6 3.1 %collective-permute-start = (f32[16,4,1024]{2,1,0:T(4,128)}, f32[16,4,1024]{2,1,0:T(4,128)S(1)}, u32[]{:S(2)}, u32[]{:S(2)}) collective-permute-start(f32[16,4,1024]{2,1,0:T(4,128)} %harmonics_ref.1), channel_id=1, source_target_pairs={{0,8},{8,16},{16,24},{24,28},{28,20},{20,12},{12,4},{4,0},{1,9},{9... | collective-permute-start | bytes 786440 | tf_op jit(solution)/shard_map/ppermute | solution.py:490
  5.4 1.2 %collective-permute-start.2 = (f32[1,128]{1,0:T(1,128)S(1)}, f32[1,128]{1,0:T(1,128)S(1)}, u32[]{:S(2)}, u32[]{:S(2)}) collective-permute-start(f32[1,128]{1,0:T(1,128)S(1)} %meta.1.refs_0_.meta_ref), channel_id=1, source_target_pairs={{0,2},{1,3},{2,0},{3,1},{4,6},{5,7},{6,4},{7,5},{8,10},{9,11},{10,... | collective-permute-start | bytes 1544 | tf_op jit(solution)/shard_map/ppermute | solution.py:484
  6.6 2.3 %tables.1.refs_1_.refs_0_ = f32[16,2,8,8192]{3,2,1,0:T(8,128)S(1)} custom-call(f32[16,2,8,8192]{3,2,1,0:T(8,128)} %legendre.1), custom_call_target="tpu_custom_call" | custom-call | bytes 4500000 | tf_op jit(solution)/shard_map/tables/pallas_call | solution.py:513
  8.9 1.2 %collective-permute-done.refs_3_ = f32[16,4,1024]{2,1,0:T(4,128)S(1)} collective-permute-done((f32[16,4,1024]{2,1,0:T(4,128)}, f32[16,4,1024]{2,1,0:T(4,128)S(1)}, u32[]{:S(2)}, u32[]{:S(2)}) %collective-permute-start) | collective-permute-done | bytes 262176 | tf_op jit(solution)/shard_map/ppermute | solution.py:490
  10.2 1.8 %collective-permute-start.4 = (f32[8,4,1024]{2,1,0:T(4,128)S(1)}, f32[8,4,1024]{2,1,0:T(4,128)S(1)}, u32[]{:S(2)}, u32[]{:S(2)}) collective-permute-start(f32[8,4,1024]{2,1,0:T(4,128)S(1)} %get-tuple-element.59), channel_id=1, source_target_pairs={{0,8},{8,16},{16,24},{24,28},{28,20},{20,12},{12,4},{4,0},{1,9},{9... | collective-permute-start | bytes 393224 | tf_op jit(solution)/shard_map/ppermute | solution.py:490
  12.3 1.7 %collective-permute-start.7 = (f32[8,4,1024]{2,1,0:T(4,128)S(1)}, f32[8,4,1024]{2,1,0:T(4,128)S(1)}, u32[]{:S(2)}, u32[]{:S(2)}) collective-permute-start(f32[8,4,1024]{2,1,0:T(4,128)S(1)} %get-tuple-element.57), channel_id=1, source_target_pairs={{0,4},{8,0},{16,8},{24,16},{28,24},{20,28},{12,20},{4,12},{1,5},{9... | collective-permute-start | bytes 393224 | tf_op jit(solution)/shard_map/ppermute | solution.py:490
  14.4 1.8 %sky_analysis.1 = (f32[4,8,128]{2,1,0:T(8,128)S(1)}, f32[2,256,128]{2,1,0:T(8,128)S(1)}, f32[2,256,128]{2,1,0:T(8,128)S(1)}, f32[2,128,128]{2,1,0:T(8,128)S(1)}, f32[2,256,128]{2,1,0:T(8,128)S(1)}) custom-call(f32[1,128]{1,0:T(1,128)S(1)} %meta.1.refs_0_.meta_ref, f32[1,128]{1,0:T(1,128)S(1)} %collective-permute-done.1.refs_1_, ...), custom_call_target="tpu_custom_call" | custom-call | bytes 9000000 | tf_op jit(solution)/shard_map/sky_analysis/pallas_call | solution.py:529
  16.2 1.6 %collective-permute-done.8.refs_8_ = f32[8,4,1024]{2,1,0:T(4,128)S(1)} collective-permute-done((f32[8,4,1024]{2,1,0:T(4,128)S(1)}, f32[8,4,1024]{2,1,0:T(4,128)S(1)}, u32[]{:S(2)}, u32[]{:S(2)}) %collective-permute-start.8) | collective-permute-done | bytes 131104 | tf_op jit(solution)/shard_map/ppermute | solution.py:490
  18.2 1.6 %collective-permute-start.9 = (f32[8,4,1024]{2,1,0:T(4,128)S(1)}, f32[8,4,1024]{2,1,0:T(4,128)S(1)}, u32[]{:S(2)}, u32[]{:S(2)}) collective-permute-start(f32[8,4,1024]{2,1,0:T(4,128)S(1)} %collective-permute-done.4.refs_5_), channel_id=1, source_target_pairs={{0,8},{8,16},{16,24},{24,28},{28,20},{20,12},{12,4},{4,0},{1,9},{9... | collective-permute-start | bytes 393224 | tf_op jit(solution)/shard_map/ppermute | solution.py:490
  20.6 2.0 %collective-permute-start.10 = (f32[8,4,1024]{2,1,0:T(4,128)S(1)}, f32[8,4,1024]{2,1,0:T(4,128)S(1)}, u32[]{:S(2)}, u32[]{:S(2)}) collective-permute-start(f32[8,4,1024]{2,1,0:T(4,128)S(1)} %collective-permute-done.6.refs_6_), channel_id=1, source_target_pairs={{0,8},{8,16},{16,24},{24,28},{28,20},{20,12},{12,4},{4,0},{1,9},{9... | collective-permute-start | bytes 393224 | tf_op jit(solution)/shard_map/ppermute | solution.py:490
  23.8 1.6 %collective-permute-start.13 = (f32[8,4,1024]{2,1,0:T(4,128)S(1)}, f32[8,4,1024]{2,1,0:T(4,128)S(1)}, u32[]{:S(2)}, u32[]{:S(2)}) collective-permute-start(f32[8,4,1024]{2,1,0:T(4,128)S(1)} %collective-permute-done.9.refs_9_), channel_id=1, source_target_pairs={{0,8},{8,16},{16,24},{24,28},{28,20},{20,12},{12,4},{4,0},{1,9},{9... | collective-permute-start | bytes 393224 | tf_op jit(solution)/shard_map/ppermute | solution.py:490
  26.2 1.5 %forward.1.refs_3_ = f32[16,4,8,128]{3,2,1,0:T(8,128)S(1)} custom-call(f32[1,128]{1,0:T(1,128)S(1)} %meta.1.refs_0_.meta_ref, f32[16,2,8,8192]{3,2,1,0:T(8,128)S(1)} %tables.1.refs_1_.refs_0_, f32[16,4,1024]{2,1,0:T(4,128)S(1)} %copy-done, f32[16,4,1024]{2,1,0:T(4,128)S(1)} %collective-permute-done.refs_3_, ...), custom_call_target="tpu_custom_call" | custom-call | bytes 6000000 | tf_op jit(solution)/shard_map/forward/pallas_call | solution.py:569
  29.9 1.4 %collective-permute-start.16 = (f32[16,128]{1,0:T(8,128)S(1)}, f32[16,128]{1,0:T(8,128)S(1)}, u32[]{:S(2)}, u32[]{:S(2)}) collective-permute-start(f32[16,128]{1,0:T(8,128)S(1)} %get-tuple-element.40), channel_id=1, source_target_pairs={{0,2},{1,3},{2,0},{3,1},{4,6},{5,7},{6,4},{7,5},{8,10},{9,11},{10,... | collective-permute-start | bytes 24584 | tf_op jit(solution)/shard_map/ppermute | solution.py:484
  32.1 1.4 %collective-permute-done.16.refs_5_.refs_10_ = f32[16,128]{1,0:T(8,128)S(1)} collective-permute-done((f32[16,128]{1,0:T(8,128)S(1)}, f32[16,128]{1,0:T(8,128)S(1)}, u32[]{:S(2)}, u32[]{:S(2)}) %collective-permute-start.16) | collective-permute-done | bytes 8224 | tf_op jit(solution)/shard_map/ppermute | solution.py:484
  35.6 1.7 %collective-permute-start.18 = (f32[8,4,1024]{2,1,0:T(4,128)S(1)}, f32[8,4,1024]{2,1,0:T(4,128)S(1)}, u32[]{:S(2)}, u32[]{:S(2)}) collective-permute-start(f32[8,4,1024]{2,1,0:T(4,128)S(1)} %get-tuple-element.48), channel_id=1, source_target_pairs={{0,8},{8,16},{16,24},{24,28},{28,20},{20,12},{12,4},{4,0},{1,9},{9... | collective-permute-start | bytes 393224 | tf_op jit(solution)/shard_map/ppermute | solution.py:490
  37.6 1.6 %collective-permute-start.22 = (f32[8,4,1024]{2,1,0:T(4,128)S(1)}, f32[8,4,1024]{2,1,0:T(4,128)S(1)}, u32[]{:S(2)}, u32[]{:S(2)}) collective-permute-start(f32[8,4,1024]{2,1,0:T(4,128)S(1)} %get-tuple-element.49), channel_id=1, source_target_pairs={{0,8},{8,16},{16,24},{24,28},{28,20},{20,12},{12,4},{4,0},{1,9},{9... | collective-permute-start | bytes 393224 | tf_op jit(solution)/shard_map/ppermute | solution.py:490
  39.2 1.9 %backward.3.refs_0_.piece_ref = f32[8,16,4,1024]{3,2,1,0:T(4,128)S(1)} custom-call(f32[16,2,8,8192]{3,2,1,0:T(8,128)S(1)} %tables.1.refs_1_.refs_0_, f32[16,4,8,128]{3,2,1,0:T(8,128)S(1)} %get-tuple-element.42.refs_1_, f32[8,16,4,1024]{3,2,1,0:T(4,128)S(1)} %backward.2.refs_2_), custom_call_target="tpu_custom_call", output_to_operand_aliasing={{}: (2, {})} | custom-call | bytes 6000000 | tf_op jit(solution)/shard_map/backward/pallas_call | solution.py:602
  41.7 1.7 %collective-permute-start.19 = (f32[8,4,1024]{2,1,0:T(4,128)S(1)}, f32[8,4,1024]{2,1,0:T(4,128)S(1)}, u32[]{:S(2)}, u32[]{:S(2)}) collective-permute-start(f32[8,4,1024]{2,1,0:T(4,128)S(1)} %add.10), channel_id=1, source_target_pairs={{0,8},{8,16},{16,24},{24,28},{28,20},{20,12},{12,4},{4,0},{1,9},{9... | collective-permute-start | bytes 393224 | tf_op jit(solution)/shard_map/ppermute | solution.py:490
  44.0 1.7 %collective-permute-start.23 = (f32[8,4,1024]{2,1,0:T(4,128)S(1)}, f32[8,4,1024]{2,1,0:T(4,128)S(1)}, u32[]{:S(2)}, u32[]{:S(2)}) collective-permute-start(f32[8,4,1024]{2,1,0:T(4,128)S(1)} %add.13), channel_id=1, source_target_pairs={{0,8},{8,16},{16,24},{24,28},{28,20},{20,12},{12,4},{4,0},{1,9},{9... | collective-permute-start | bytes 393224 | tf_op jit(solution)/shard_map/ppermute | solution.py:490
  47.8 1.7 %collective-permute-start.20 = (f32[8,4,1024]{2,1,0:T(4,128)S(1)}, f32[8,4,1024]{2,1,0:T(4,128)S(1)}, u32[]{:S(2)}, u32[]{:S(2)}) collective-permute-start(f32[8,4,1024]{2,1,0:T(4,128)S(1)} %add.11), channel_id=1, source_target_pairs={{0,8},{8,16},{16,24},{24,28},{28,20},{20,12},{12,4},{4,0},{1,9},{9... | collective-permute-start | bytes 393224 | tf_op jit(solution)/shard_map/ppermute | solution.py:490
  50.6 1.7 %collective-permute-start.24 = (f32[8,4,1024]{2,1,0:T(4,128)S(1)}, f32[8,4,1024]{2,1,0:T(4,128)S(1)}, u32[]{:S(2)}, u32[]{:S(2)}) collective-permute-start(f32[8,4,1024]{2,1,0:T(4,128)S(1)} %add.14), channel_id=1, source_target_pairs={{0,8},{8,16},{16,24},{24,28},{28,20},{20,12},{12,4},{4,0},{1,9},{9... | collective-permute-start | bytes 393224 | tf_op jit(solution)/shard_map/ppermute | solution.py:490
  54.2 1.7 %collective-permute-start.21 = (f32[8,4,1024]{2,1,0:T(4,128)S(1)}, f32[8,4,1024]{2,1,0:T(4,128)S(1)}, u32[]{:S(2)}, u32[]{:S(2)}) collective-permute-start(f32[8,4,1024]{2,1,0:T(4,128)S(1)} %add.12), channel_id=1, source_target_pairs={{0,8},{8,16},{16,24},{24,28},{28,20},{20,12},{12,4},{4,0},{1,9},{9... | collective-permute-start | bytes 393224 | tf_op jit(solution)/shard_map/ppermute | solution.py:490
  56.3 1.2 %residual.1 = f32[2,256,128]{2,1,0:T(8,128)} custom-call(f32[1,128]{1,0:T(1,128)S(1)} %meta.1.refs_0_.meta_ref, f32[1,128]{1,0:T(1,128)S(1)} %collective-permute-done.1.refs_1_, f32[1,128]{1,0:T(1,128)S(1)} %collective-permute-done.2.refs_2_, f32[1,128]{1,0:T(1,128)S(1)} %collective-permute-done.3.refs_3_, f32[2,256,128]{2,1,0:T(8,128)S(1)} %get-tuple-element.52.refs_4_, ...), custom_call_target="tpu_custom_call" | custom-call | flops 100000000 | bytes 2097152 | tf_op jit(solution)/shard_map/residual/pallas_call | solution.py:654
  59.6 1.4 %collective-permute-done.31.rest_3_ = f32[8,4,1024]{2,1,0:T(4,128)S(1)} collective-permute-done((f32[8,4,1024]{2,1,0:T(4,128)S(1)}, f32[8,4,1024]{2,1,0:T(4,128)S(1)}, u32[]{:S(2)}, u32[]{:S(2)}) %collective-permute-start.31) | collective-permute-done | bytes 131104 | tf_op jit(solution)/shard_map/ppermute | solution.py:490
  (65 shorter events, 20.6 us)
Async XLA Ops:
  0.6 9.5 %collective-permute-start = (f32[16,4,1024]{2,1,0:T(4,128)}, f32[16,4,1024]{2,1,0:T(4,128)S(1)}, u32[]{:S(2)}, u32[]{:S(2)}) collective-permute-start(f32[16,4,1024]{2,1,0:T(4,128)} %harmonics_ref.1), channel_id=1, source_target_pairs={{0,8},{8,16},{16,24},{24,28},{28,20},{20,12},{12,4},{4,0},{1,9},{9... | collective-permute-start | bytes 786440 | tf_op jit(solution)/shard_map/ppermute | solution.py:490
  3.7 8.3 %collective-permute-start.5 = (f32[16,4,1024]{2,1,0:T(4,128)}, f32[16,4,1024]{2,1,0:T(4,128)S(1)}, u32[]{:S(2)}, u32[]{:S(2)}) collective-permute-start(f32[16,4,1024]{2,1,0:T(4,128)} %harmonics_ref.1), channel_id=1, source_target_pairs={{0,4},{8,0},{16,8},{24,16},{28,24},{20,28},{12,20},{4,12},{1,5},{9... | collective-permute-start | bytes 786440 | tf_op jit(solution)/shard_map/ppermute | solution.py:490
  10.2 6.0 %collective-permute-start.4 = (f32[8,4,1024]{2,1,0:T(4,128)S(1)}, f32[8,4,1024]{2,1,0:T(4,128)S(1)}, u32[]{:S(2)}, u32[]{:S(2)}) collective-permute-start(f32[8,4,1024]{2,1,0:T(4,128)S(1)} %get-tuple-element.59), channel_id=1, source_target_pairs={{0,8},{8,16},{16,24},{24,28},{28,20},{20,12},{12,4},{4,0},{1,9},{9... | collective-permute-start | bytes 393224 | tf_op jit(solution)/shard_map/ppermute | solution.py:490
  12.1 5.7 %collective-permute-start.8 = (f32[8,4,1024]{2,1,0:T(4,128)S(1)}, f32[8,4,1024]{2,1,0:T(4,128)S(1)}, u32[]{:S(2)}, u32[]{:S(2)}) collective-permute-start(f32[8,4,1024]{2,1,0:T(4,128)S(1)} %get-tuple-element.56), channel_id=1, source_target_pairs={{0,4},{8,0},{16,8},{24,16},{28,24},{20,28},{12,20},{4,12},{1,5},{9... | collective-permute-start | bytes 393224 | tf_op jit(solution)/shard_map/ppermute | solution.py:490
  12.3 8.2 %collective-permute-start.7 = (f32[8,4,1024]{2,1,0:T(4,128)S(1)}, f32[8,4,1024]{2,1,0:T(4,128)S(1)}, u32[]{:S(2)}, u32[]{:S(2)}) collective-permute-start(f32[8,4,1024]{2,1,0:T(4,128)S(1)} %get-tuple-element.57), channel_id=1, source_target_pairs={{0,4},{8,0},{16,8},{24,16},{28,24},{20,28},{12,20},{4,12},{1,5},{9... | collective-permute-start | bytes 393224 | tf_op jit(solution)/shard_map/ppermute | solution.py:490
  14.1 6.5 %collective-permute-start.6 = (f32[8,4,1024]{2,1,0:T(4,128)S(1)}, f32[8,4,1024]{2,1,0:T(4,128)S(1)}, u32[]{:S(2)}, u32[]{:S(2)}) collective-permute-start(f32[8,4,1024]{2,1,0:T(4,128)S(1)} %get-tuple-element.58), channel_id=1, source_target_pairs={{0,8},{8,16},{16,24},{24,28},{28,20},{20,12},{12,4},{4,0},{1,9},{9... | collective-permute-start | bytes 393224 | tf_op jit(solution)/shard_map/ppermute | solution.py:490
  17.7 5.7 %collective-permute-start.12 = (f32[8,4,1024]{2,1,0:T(4,128)S(1)}, f32[8,4,1024]{2,1,0:T(4,128)S(1)}, u32[]{:S(2)}, u32[]{:S(2)}) collective-permute-start(f32[8,4,1024]{2,1,0:T(4,128)S(1)} %collective-permute-done.8.refs_8_), channel_id=1, source_target_pairs={{0,4},{8,0},{16,8},{24,16},{28,24},{20,28},{12,20},{4,12},{1,5},{9... | collective-permute-start | bytes 393224 | tf_op jit(solution)/shard_map/ppermute | solution.py:490
  18.2 5.7 %collective-permute-start.9 = (f32[8,4,1024]{2,1,0:T(4,128)S(1)}, f32[8,4,1024]{2,1,0:T(4,128)S(1)}, u32[]{:S(2)}, u32[]{:S(2)}) collective-permute-start(f32[8,4,1024]{2,1,0:T(4,128)S(1)} %collective-permute-done.4.refs_5_), channel_id=1, source_target_pairs={{0,8},{8,16},{16,24},{24,28},{28,20},{20,12},{12,4},{4,0},{1,9},{9... | collective-permute-start | bytes 393224 | tf_op jit(solution)/shard_map/ppermute | solution.py:490
  20.5 5.6 %collective-permute-start.11 = (f32[8,4,1024]{2,1,0:T(4,128)S(1)}, f32[8,4,1024]{2,1,0:T(4,128)S(1)}, u32[]{:S(2)}, u32[]{:S(2)}) collective-permute-start(f32[8,4,1024]{2,1,0:T(4,128)S(1)} %collective-permute-done.7.refs_7_), channel_id=1, source_target_pairs={{0,4},{8,0},{16,8},{24,16},{28,24},{20,28},{12,20},{4,12},{1,5},{9... | collective-permute-start | bytes 393224 | tf_op jit(solution)/shard_map/ppermute | solution.py:490
  20.6 5.6 %collective-permute-start.10 = (f32[8,4,1024]{2,1,0:T(4,128)S(1)}, f32[8,4,1024]{2,1,0:T(4,128)S(1)}, u32[]{:S(2)}, u32[]{:S(2)}) collective-permute-start(f32[8,4,1024]{2,1,0:T(4,128)S(1)} %collective-permute-done.6.refs_6_), channel_id=1, source_target_pairs={{0,8},{8,16},{16,24},{24,28},{28,20},{20,12},{12,4},{4,0},{1,9},{9... | collective-permute-start | bytes 393224 | tf_op jit(solution)/shard_map/ppermute | solution.py:490
  35.6 6.1 %collective-permute-start.18 = (f32[8,4,1024]{2,1,0:T(4,128)S(1)}, f32[8,4,1024]{2,1,0:T(4,128)S(1)}, u32[]{:S(2)}, u32[]{:S(2)}) collective-permute-start(f32[8,4,1024]{2,1,0:T(4,128)S(1)} %get-tuple-element.48), channel_id=1, source_target_pairs={{0,8},{8,16},{16,24},{24,28},{28,20},{20,12},{12,4},{4,0},{1,9},{9... | collective-permute-start | bytes 393224 | tf_op jit(solution)/shard_map/ppermute | solution.py:490
  37.2 6.1 %collective-permute-start.28 = (f32[8,4,1024]{2,1,0:T(4,128)S(1)}, f32[8,4,1024]{2,1,0:T(4,128)S(1)}, u32[]{:S(2)}, u32[]{:S(2)}) collective-permute-start(f32[8,4,1024]{2,1,0:T(4,128)S(1)} %get-tuple-element.51), channel_id=1, source_target_pairs={{0,4},{8,0},{16,8},{24,16},{28,24},{20,28},{12,20},{4,12},{1,5},{9... | collective-permute-start | bytes 393224 | tf_op jit(solution)/shard_map/ppermute | solution.py:490
  37.6 6.3 %collective-permute-start.22 = (f32[8,4,1024]{2,1,0:T(4,128)S(1)}, f32[8,4,1024]{2,1,0:T(4,128)S(1)}, u32[]{:S(2)}, u32[]{:S(2)}) collective-permute-start(f32[8,4,1024]{2,1,0:T(4,128)S(1)} %get-tuple-element.49), channel_id=1, source_target_pairs={{0,8},{8,16},{16,24},{24,28},{28,20},{20,12},{12,4},{4,0},{1,9},{9... | collective-permute-start | bytes 393224 | tf_op jit(solution)/shard_map/ppermute | solution.py:490
  41.2 5.2 %collective-permute-start.25 = (f32[8,4,1024]{2,1,0:T(4,128)S(1)}, f32[8,4,1024]{2,1,0:T(4,128)S(1)}, u32[]{:S(2)}, u32[]{:S(2)}) collective-permute-start(f32[8,4,1024]{2,1,0:T(4,128)S(1)} %get-tuple-element.50), channel_id=1, source_target_pairs={{0,4},{8,0},{16,8},{24,16},{28,24},{20,28},{12,20},{4,12},{1,5},{9... | collective-permute-start | bytes 393224 | tf_op jit(solution)/shard_map/ppermute | solution.py:490
  41.7 6.1 %collective-permute-start.19 = (f32[8,4,1024]{2,1,0:T(4,128)S(1)}, f32[8,4,1024]{2,1,0:T(4,128)S(1)}, u32[]{:S(2)}, u32[]{:S(2)}) collective-permute-start(f32[8,4,1024]{2,1,0:T(4,128)S(1)} %add.10), channel_id=1, source_target_pairs={{0,8},{8,16},{16,24},{24,28},{28,20},{20,12},{12,4},{4,0},{1,9},{9... | collective-permute-start | bytes 393224 | tf_op jit(solution)/shard_map/ppermute | solution.py:490
  43.3 6.4 %collective-permute-start.29 = (f32[8,4,1024]{2,1,0:T(4,128)S(1)}, f32[8,4,1024]{2,1,0:T(4,128)S(1)}, u32[]{:S(2)}, u32[]{:S(2)}) collective-permute-start(f32[8,4,1024]{2,1,0:T(4,128)S(1)} %add.17), channel_id=1, source_target_pairs={{0,4},{8,0},{16,8},{24,16},{28,24},{20,28},{12,20},{4,12},{1,5},{9... | collective-permute-start | bytes 393224 | tf_op jit(solution)/shard_map/ppermute | solution.py:490
  44.0 6.6 %collective-permute-start.23 = (f32[8,4,1024]{2,1,0:T(4,128)S(1)}, f32[8,4,1024]{2,1,0:T(4,128)S(1)}, u32[]{:S(2)}, u32[]{:S(2)}) collective-permute-start(f32[8,4,1024]{2,1,0:T(4,128)S(1)} %add.13), channel_id=1, source_target_pairs={{0,8},{8,16},{16,24},{24,28},{28,20},{20,12},{12,4},{4,0},{1,9},{9... | collective-permute-start | bytes 393224 | tf_op jit(solution)/shard_map/ppermute | solution.py:490
  46.4 6.2 %collective-permute-start.26 = (f32[8,4,1024]{2,1,0:T(4,128)S(1)}, f32[8,4,1024]{2,1,0:T(4,128)S(1)}, u32[]{:S(2)}, u32[]{:S(2)}) collective-permute-start(f32[8,4,1024]{2,1,0:T(4,128)S(1)} %add.15), channel_id=1, source_target_pairs={{0,4},{8,0},{16,8},{24,16},{28,24},{20,28},{12,20},{4,12},{1,5},{9... | collective-permute-start | bytes 393224 | tf_op jit(solution)/shard_map/ppermute | solution.py:490
  47.8 6.3 %collective-permute-start.20 = (f32[8,4,1024]{2,1,0:T(4,128)S(1)}, f32[8,4,1024]{2,1,0:T(4,128)S(1)}, u32[]{:S(2)}, u32[]{:S(2)}) collective-permute-start(f32[8,4,1024]{2,1,0:T(4,128)S(1)} %add.11), channel_id=1, source_target_pairs={{0,8},{8,16},{16,24},{24,28},{28,20},{20,12},{12,4},{4,0},{1,9},{9... | collective-permute-start | bytes 393224 | tf_op jit(solution)/shard_map/ppermute | solution.py:490
  49.8 6.1 %collective-permute-start.30 = (f32[8,4,1024]{2,1,0:T(4,128)S(1)}, f32[8,4,1024]{2,1,0:T(4,128)S(1)}, u32[]{:S(2)}, u32[]{:S(2)}) collective-permute-start(f32[8,4,1024]{2,1,0:T(4,128)S(1)} %add.18), channel_id=1, source_target_pairs={{0,4},{8,0},{16,8},{24,16},{28,24},{20,28},{12,20},{4,12},{1,5},{9... | collective-permute-start | bytes 393224 | tf_op jit(solution)/shard_map/ppermute | solution.py:490
  50.6 6.9 %collective-permute-start.24 = (f32[8,4,1024]{2,1,0:T(4,128)S(1)}, f32[8,4,1024]{2,1,0:T(4,128)S(1)}, u32[]{:S(2)}, u32[]{:S(2)}) collective-permute-start(f32[8,4,1024]{2,1,0:T(4,128)S(1)} %add.14), channel_id=1, source_target_pairs={{0,8},{8,16},{16,24},{24,28},{28,20},{20,12},{12,4},{4,0},{1,9},{9... | collective-permute-start | bytes 393224 | tf_op jit(solution)/shard_map/ppermute | solution.py:490
  52.6 5.9 %collective-permute-start.27 = (f32[8,4,1024]{2,1,0:T(4,128)S(1)}, f32[8,4,1024]{2,1,0:T(4,128)S(1)}, u32[]{:S(2)}, u32[]{:S(2)}) collective-permute-start(f32[8,4,1024]{2,1,0:T(4,128)S(1)} %add.16), channel_id=1, source_target_pairs={{0,4},{8,0},{16,8},{24,16},{28,24},{20,28},{12,20},{4,12},{1,5},{9... | collective-permute-start | bytes 393224 | tf_op jit(solution)/shard_map/ppermute | solution.py:490
  54.2 5.4 %collective-permute-start.21 = (f32[8,4,1024]{2,1,0:T(4,128)S(1)}, f32[8,4,1024]{2,1,0:T(4,128)S(1)}, u32[]{:S(2)}, u32[]{:S(2)}) collective-permute-start(f32[8,4,1024]{2,1,0:T(4,128)S(1)} %add.12), channel_id=1, source_target_pairs={{0,8},{8,16},{16,24},{24,28},{28,20},{20,12},{12,4},{4,0},{1,9},{9... | collective-permute-start | bytes 393224 | tf_op jit(solution)/shard_map/ppermute | solution.py:490
  55.9 5.1 %collective-permute-start.31 = (f32[8,4,1024]{2,1,0:T(4,128)S(1)}, f32[8,4,1024]{2,1,0:T(4,128)S(1)}, u32[]{:S(2)}, u32[]{:S(2)}) collective-permute-start(f32[8,4,1024]{2,1,0:T(4,128)S(1)} %add.19), channel_id=1, source_target_pairs={{0,4},{8,0},{16,8},{24,16},{28,24},{20,28},{12,20},{4,12},{1,5},{9... | collective-permute-start | bytes 393224 | tf_op jit(solution)/shard_map/ppermute | solution.py:490
  (9 other events, 51.0 us)

commit v5 on v4

--- a/solution.py
+++ b/solution.py
@@ -328,6 +328,14 @@
     return fold_rows(values, row8)
 
 
+def update_block(tables, m, first, an, ng, row8, out, at):
+    for t in range(0, out.shape[2] // LANES, 2):
+        spans = [pl.ds(first + u * LANES, LANES) for u in (t, t + 1)]
+        folded = update_tiles(tables, m, spans, an, ng, row8)
+        for k, u in enumerate((t, t + 1)):
+            out[at, :, u * LANES : (u + 1) * LANES] = folded[4 * k : 4 * k + 4]
+
+
 def analysed_kernel(groups, cycles, tables, gram_ref, pieces_ref, phases_ref, *rest):
     messages = rest[: groups - 1]
     *sends, analysed_ref, sky = rest[groups - 1 :]
@@ -336,10 +344,7 @@
     blocks = degrees // width
     far = blocks // 2
     place = ring_place(lax.axis_index("blk"), blocks)
-    firsts = [
-        pl.multiple_of(block_at(place + step, blocks) * width, LANES)
-        for step in (far, -far, 1 - far, far - 1)
-    ]
+    first = pl.multiple_of(block_at(place + far, blocks) * width, LANES)
     owner = lax.axis_index("order")
     wide = 4 * slots
     pairs = []
@@ -372,12 +377,22 @@
             analysed_ref[m, a] = an[a]
         ng = [-value for value in an]
         half, at = divmod(m, middle)
-        for part, first in zip(sends[half::2], firsts[half::2]):
-            for t in range(0, width // LANES, 2):
-                spans = [pl.ds(first + u * LANES, LANES) for u in (t, t + 1)]
-                folded = update_tiles(tables, m, spans, an, ng, row8)
-                for k, u in enumerate((t, t + 1)):
-                    part[at, :, u * LANES : (u + 1) * LANES] = folded[4 * k : 4 * k + 4]
+        update_block(tables, m, first, an, ng, row8, sends[half], at)
+
+
+def second_kernel(tables, analysed_ref, low_ref, high_ref):
+    slots, _, _, degrees = tables.shape
+    middle, _, width = low_ref.shape
+    blocks = degrees // width
+    place = ring_place(lax.axis_index("blk"), blocks)
+    row8 = lax.broadcasted_iota(jnp.int32, (8, LANES), 0)
+    for m in range(slots):
+        half, at = divmod(m, middle)
+        step = (1 - blocks // 2, blocks // 2 - 1)[half]
+        first = pl.multiple_of(block_at(place + step, blocks) * width, LANES)
+        an = [analysed_ref[m, a] for a in range(4)]
+        ng = [-value for value in an]
+        update_block(tables, m, first, an, ng, row8, (low_ref, high_ref)[half], at)
 
 
 def backward_kernel(core, tables, analysed_ref, *rest):
@@ -590,14 +605,24 @@
     half = pltpu.VMEM((middle, 4, width), jnp.float32)
     *sends, analysed = pl.pallas_call(
         lambda *refs: analysed_kernel(groups, cycles, *refs),
-        out_shape=[half] * 4 + [whole],
+        out_shape=[half] * 2 + [whole],
         in_specs=[vmem()] * (3 + groups),
-        out_specs=[vmem()] * 5,
+        out_specs=[vmem()] * 3,
         scratch_shapes=[pltpu.VMEM((count, LANES), jnp.float32)],
         compiler_params=pltpu.CompilerParams(vmem_limit_bytes=16 * MIB),
         cost_estimate=estimate(1),
         name="analysed",
     )(tables, gram, pieces, phases, *messages)
+    second = pl.pallas_call(
+        second_kernel,
+        out_shape=[half] * 2,
+        in_specs=[vmem()] * 2,
+        out_specs=[vmem()] * 2,
+        compiler_params=pltpu.CompilerParams(vmem_limit_bytes=16 * MIB),
+        cost_estimate=estimate(0.5),
+        name="second",
+    )(tables, analysed)
+
     def backward(core, *before):
         return pl.pallas_call(
             lambda *refs: backward_kernel(core, *refs),
@@ -628,7 +653,7 @@
             name="add",
         )(piece, pltpu.with_memory_space_constraint(value, pltpu.VMEM))
 
-    sent = dict(zip(((1, 0), (-1, middle), (-1, 0), (1, middle)), sends))
+    sent = dict(zip(((1, 0), (-1, middle), (-1, 0), (1, middle)), (*sends, *second)))
     first_hop = {key: turn(sent[key], key[0]) for key in ((1, 0), (-1, middle))}
     for key in ((1, 0), (-1, middle)):
         sent[key] = add((key[0] * (far - 1)) % blocks, key[1], first_hop[key])

time: 62 us -> 60.7 us (0.979)
  waiting for transfers between devices: 15.8 us -> 14.4 us
    ppermute x26, waiting for transfers between devices: 13.5 us -> 11.8 us  [turn(): return lax.ppermute(value, 'blk', pairs)]
  transfers between devices with their start and end apart: 32 -> 32, of which waited for: 20 -> 20; matrix products, arithmetic and copies ran while one was open for 0% -> 0% of each run, Pallas kernels for 16% -> 17%
where the time goes in v5:
time: 60.7 us; the launch traced here: 60.5 us
  starting transfers between devices  32.3 us (53%)
  waiting for transfers between devices  14.4 us (24%)
  Pallas kernels  13 us (21%)
  between operations  0.78 us (1%)
    ppermute x26, starting transfers between devices, turn(): return lax.ppermute(value, 'blk', pairs)  28.3 us
    ppermute x26, waiting for transfers between devices, turn(): return lax.ppermute(value, 'blk', pairs)  11.8 us
    ppermute x6, starting transfers between devices, swap(): return lax.ppermute(value, axis, [(i, i ^ step) for i in range(size)])  4 us
    ppermute x6, waiting for transfers between devices, swap(): return lax.ppermute(value, axis, [(i, i ^ step) for i in range(size)])  2.58 us
    pallas_call x1, Pallas kernels, body(): pl.pallas_call(tables_kernel, out_shape=pltpu.VMEM(legendre.shape, jnp.fl...  2.31 us
    pallas_call x2, Pallas kernels, backward(): pl.pallas_call(lambda *refs: backward_kernel(core, *refs), out_shape=pltp...  1.94 us
    pallas_call x1, Pallas kernels, body(): pl.pallas_call(lambda *refs: sky_kernel(normalise, groups, slots, cycles,...  1.77 us
    pallas_call x1, Pallas kernels, body(): pl.pallas_call(lambda *refs: forward_kernel(steps, firsts, *refs), out_sh...  1.52 us
  transfers between devices with their start and end apart: 32, of which 20 were waited for; matrix products, arithmetic and copies ran while one was open for 0% of the time, Pallas kernels for 17%

profile of v5, /device:TPU:0, one launch (start us, length us, event | category | flops | bytes accessed | tf_op | source)
XLA Modules:
  0.0 60.5 jit_solution(11377151664232281366)
XLA Ops:
  0.6 3.1 %collective-permute-start = (f32[16,4,1024]{2,1,0:T(4,128)}, f32[16,4,1024]{2,1,0:T(4,128)S(1)}, u32[]{:S(2)}, u32[]{:S(2)}) collective-permute-start(f32[16,4,1024]{2,1,0:T(4,128)} %harmonics_ref.1), channel_id=1, source_target_pairs={{0,8},{8,16},{16,24},{24,28},{28,20},{20,12},{12,4},{4,0},{1,9},{9... | collective-permute-start | bytes 786440 | tf_op jit(solution)/shard_map/ppermute | solution.py:505
  4.6 2.0 %collective-permute-start.2 = (f32[1,128]{1,0:T(1,128)S(1)}, f32[1,128]{1,0:T(1,128)S(1)}, u32[]{:S(2)}, u32[]{:S(2)}) collective-permute-start(f32[1,128]{1,0:T(1,128)S(1)} %meta.1.refs_0_.meta_ref), channel_id=1, source_target_pairs={{0,2},{1,3},{2,0},{3,1},{4,6},{5,7},{6,4},{7,5},{8,10},{9,11},{10,... | collective-permute-start | bytes 1544 | tf_op jit(solution)/shard_map/ppermute | solution.py:499
  6.6 2.3 %tables.1.refs_1_.refs_0_ = f32[16,2,8,8192]{3,2,1,0:T(8,128)S(1)} custom-call(f32[16,2,8,8192]{3,2,1,0:T(8,128)} %legendre.1), custom_call_target="tpu_custom_call" | custom-call | bytes 4500000 | tf_op jit(solution)/shard_map/tables/pallas_call | solution.py:528
  10.2 1.8 %collective-permute-start.4 = (f32[8,4,1024]{2,1,0:T(4,128)S(1)}, f32[8,4,1024]{2,1,0:T(4,128)S(1)}, u32[]{:S(2)}, u32[]{:S(2)}) collective-permute-start(f32[8,4,1024]{2,1,0:T(4,128)S(1)} %get-tuple-element.55), channel_id=1, source_target_pairs={{0,8},{8,16},{16,24},{24,28},{28,20},{20,12},{12,4},{4,0},{1,9},{9... | collective-permute-start | bytes 393224 | tf_op jit(solution)/shard_map/ppermute | solution.py:505
  12.3 1.8 %collective-permute-start.6 = (f32[8,4,1024]{2,1,0:T(4,128)S(1)}, f32[8,4,1024]{2,1,0:T(4,128)S(1)}, u32[]{:S(2)}, u32[]{:S(2)}) collective-permute-start(f32[8,4,1024]{2,1,0:T(4,128)S(1)} %get-tuple-element.54), channel_id=1, source_target_pairs={{0,8},{8,16},{16,24},{24,28},{28,20},{20,12},{12,4},{4,0},{1,9},{9... | collective-permute-start | bytes 393224 | tf_op jit(solution)/shard_map/ppermute | solution.py:505
  14.4 1.8 %sky_analysis.1 = (f32[4,8,128]{2,1,0:T(8,128)S(1)}, f32[2,256,128]{2,1,0:T(8,128)S(1)}, f32[2,256,128]{2,1,0:T(8,128)S(1)}, f32[2,128,128]{2,1,0:T(8,128)S(1)}, f32[2,256,128]{2,1,0:T(8,128)S(1)}) custom-call(f32[1,128]{1,0:T(1,128)S(1)} %meta.1.refs_0_.meta_ref, f32[1,128]{1,0:T(1,128)S(1)} %collective-permute-done.1.refs_1_, ...), custom_call_target="tpu_custom_call" | custom-call | bytes 9000000 | tf_op jit(solution)/shard_map/sky_analysis/pallas_call | solution.py:544
  16.6 1.7 %collective-permute-start.9 = (f32[8,4,1024]{2,1,0:T(4,128)S(1)}, f32[8,4,1024]{2,1,0:T(4,128)S(1)}, u32[]{:S(2)}, u32[]{:S(2)}) collective-permute-start(f32[8,4,1024]{2,1,0:T(4,128)S(1)} %collective-permute-done.4.refs_5_), channel_id=1, source_target_pairs={{0,8},{8,16},{16,24},{24,28},{28,20},{20,12},{12,4},{4,0},{1,9},{9... | collective-permute-start | bytes 393224 | tf_op jit(solution)/shard_map/ppermute | solution.py:505
  19.0 1.6 %collective-permute-start.10 = (f32[8,4,1024]{2,1,0:T(4,128)S(1)}, f32[8,4,1024]{2,1,0:T(4,128)S(1)}, u32[]{:S(2)}, u32[]{:S(2)}) collective-permute-start(f32[8,4,1024]{2,1,0:T(4,128)S(1)} %collective-permute-done.6.refs_6_), channel_id=1, source_target_pairs={{0,8},{8,16},{16,24},{24,28},{28,20},{20,12},{12,4},{4,0},{1,9},{9... | collective-permute-start | bytes 393224 | tf_op jit(solution)/shard_map/ppermute | solution.py:505
  21.0 1.8 %collective-permute-done.9.refs_9_ = f32[8,4,1024]{2,1,0:T(4,128)S(1)} collective-permute-done((f32[8,4,1024]{2,1,0:T(4,128)S(1)}, f32[8,4,1024]{2,1,0:T(4,128)S(1)}, u32[]{:S(2)}, u32[]{:S(2)}) %collective-permute-start.9) | collective-permute-done | bytes 131104 | tf_op jit(solution)/shard_map/ppermute | solution.py:505
  22.8 1.4 %collective-permute-start.13 = (f32[8,4,1024]{2,1,0:T(4,128)S(1)}, f32[8,4,1024]{2,1,0:T(4,128)S(1)}, u32[]{:S(2)}, u32[]{:S(2)}) collective-permute-start(f32[8,4,1024]{2,1,0:T(4,128)S(1)} %collective-permute-done.9.refs_9_), channel_id=1, source_target_pairs={{0,8},{8,16},{16,24},{24,28},{28,20},{20,12},{12,4},{4,0},{1,9},{9... | collective-permute-start | bytes 393224 | tf_op jit(solution)/shard_map/ppermute | solution.py:505
  25.4 1.3 %collective-permute-done.11.refs_11_ = f32[8,4,1024]{2,1,0:T(4,128)S(1)} collective-permute-done((f32[8,4,1024]{2,1,0:T(4,128)S(1)}, f32[8,4,1024]{2,1,0:T(4,128)S(1)}, u32[]{:S(2)}, u32[]{:S(2)}) %collective-permute-start.11) | collective-permute-done | bytes 131104 | tf_op jit(solution)/shard_map/ppermute | solution.py:505
  26.7 1.5 %forward.1.refs_3_ = f32[16,4,8,128]{3,2,1,0:T(8,128)S(1)} custom-call(f32[1,128]{1,0:T(1,128)S(1)} %meta.1.refs_0_.meta_ref, f32[16,2,8,8192]{3,2,1,0:T(8,128)S(1)} %tables.1.refs_1_.refs_0_, f32[16,4,1024]{2,1,0:T(4,128)S(1)} %copy-done, f32[16,4,1024]{2,1,0:T(4,128)S(1)} %collective-permute-done.refs_3_, ...), custom_call_target="tpu_custom_call" | custom-call | bytes 6000000 | tf_op jit(solution)/shard_map/forward/pallas_call | solution.py:584
  29.1 1.1 %phases.1 = (f32[8,128]{1,0:T(8,128)S(1)}, f32[16,128]{1,0:T(8,128)S(1)}, f32[16,128]{1,0:T(8,128)S(1)}, f32[16,128]{1,0:T(8,128)S(1)}) custom-call(f32[1,128]{1,0:T(1,128)S(1)} %meta.1.refs_0_.meta_ref, f32[16,2,8,8192]{3,2,1,0:T(8,128)S(1)} %tables.1.refs_1_.refs_0_, f32[4,8,128]{2,1,0:T(8,128)S(1)} %get-tuple-element.34.refs_2_, ...), custom_call_target="tpu_custom_call" | custom-call | bytes 3000000 | tf_op jit(solution)/shard_map/phases/pallas_call | solution.py:594
  30.2 1.2 %collective-permute-start.16 = (f32[16,128]{1,0:T(8,128)S(1)}, f32[16,128]{1,0:T(8,128)S(1)}, u32[]{:S(2)}, u32[]{:S(2)}) collective-permute-start(f32[16,128]{1,0:T(8,128)S(1)} %get-tuple-element.38), channel_id=1, source_target_pairs={{0,2},{1,3},{2,0},{3,1},{4,6},{5,7},{6,4},{7,5},{8,10},{9,11},{10,... | collective-permute-start | bytes 24584 | tf_op jit(solution)/shard_map/ppermute | solution.py:499
  32.5 1.4 %collective-permute-done.16.refs_5_.refs_10_ = f32[16,128]{1,0:T(8,128)S(1)} collective-permute-done((f32[16,128]{1,0:T(8,128)S(1)}, f32[16,128]{1,0:T(8,128)S(1)}, u32[]{:S(2)}, u32[]{:S(2)}) %collective-permute-start.16) | collective-permute-done | bytes 8224 | tf_op jit(solution)/shard_map/ppermute | solution.py:499
  35.6 1.6 %collective-permute-start.18 = (f32[8,4,1024]{2,1,0:T(4,128)S(1)}, f32[8,4,1024]{2,1,0:T(4,128)S(1)}, u32[]{:S(2)}, u32[]{:S(2)}) collective-permute-start(f32[8,4,1024]{2,1,0:T(4,128)S(1)} %get-tuple-element.44), channel_id=1, source_target_pairs={{0,8},{8,16},{16,24},{24,28},{28,20},{20,12},{12,4},{4,0},{1,9},{9... | collective-permute-start | bytes 393224 | tf_op jit(solution)/shard_map/ppermute | solution.py:505
  38.2 1.9 %backward.3.refs_0_.piece_ref = f32[8,16,4,1024]{3,2,1,0:T(4,128)S(1)} custom-call(f32[16,2,8,8192]{3,2,1,0:T(8,128)S(1)} %tables.1.refs_1_.refs_0_, f32[16,4,8,128]{3,2,1,0:T(8,128)S(1)} %get-tuple-element.40.refs_1_.analysed_ref, f32[8,16,4,1024]{3,2,1,0:T(4,128)S(1)} %backward.2.refs_2_), custom_call_target="tpu_custom_call", output_to_operand_aliasing={{}: (2, {})} | custom-call | bytes 6000000 | tf_op jit(solution)/shard_map/backward/pallas_call | solution.py:627
  40.1 1.6 %collective-permute-start.22 = (f32[8,4,1024]{2,1,0:T(4,128)S(1)}, f32[8,4,1024]{2,1,0:T(4,128)S(1)}, u32[]{:S(2)}, u32[]{:S(2)}) collective-permute-start(f32[8,4,1024]{2,1,0:T(4,128)S(1)} %get-tuple-element.45), channel_id=1, source_target_pairs={{0,8},{8,16},{16,24},{24,28},{28,20},{20,12},{12,4},{4,0},{1,9},{9... | collective-permute-start | bytes 393224 | tf_op jit(solution)/shard_map/ppermute | solution.py:505
  42.3 1.6 %collective-permute-start.19 = (f32[8,4,1024]{2,1,0:T(4,128)S(1)}, f32[8,4,1024]{2,1,0:T(4,128)S(1)}, u32[]{:S(2)}, u32[]{:S(2)}) collective-permute-start(f32[8,4,1024]{2,1,0:T(4,128)S(1)} %add.10), channel_id=1, source_target_pairs={{0,8},{8,16},{16,24},{24,28},{28,20},{20,12},{12,4},{4,0},{1,9},{9... | collective-permute-start | bytes 393224 | tf_op jit(solution)/shard_map/ppermute | solution.py:505
  45.4 1.7 %collective-permute-start.23 = (f32[8,4,1024]{2,1,0:T(4,128)S(1)}, f32[8,4,1024]{2,1,0:T(4,128)S(1)}, u32[]{:S(2)}, u32[]{:S(2)}) collective-permute-start(f32[8,4,1024]{2,1,0:T(4,128)S(1)} %add.13), channel_id=1, source_target_pairs={{0,8},{8,16},{16,24},{24,28},{28,20},{20,12},{12,4},{4,0},{1,9},{9... | collective-permute-start | bytes 393224 | tf_op jit(solution)/shard_map/ppermute | solution.py:505
  48.6 1.5 %collective-permute-start.20 = (f32[8,4,1024]{2,1,0:T(4,128)S(1)}, f32[8,4,1024]{2,1,0:T(4,128)S(1)}, u32[]{:S(2)}, u32[]{:S(2)}) collective-permute-start(f32[8,4,1024]{2,1,0:T(4,128)S(1)} %add.11), channel_id=1, source_target_pairs={{0,8},{8,16},{16,24},{24,28},{28,20},{20,12},{12,4},{4,0},{1,9},{9... | collective-permute-start | bytes 393224 | tf_op jit(solution)/shard_map/ppermute | solution.py:505
  51.5 1.7 %collective-permute-start.24 = (f32[8,4,1024]{2,1,0:T(4,128)S(1)}, f32[8,4,1024]{2,1,0:T(4,128)S(1)}, u32[]{:S(2)}, u32[]{:S(2)}) collective-permute-start(f32[8,4,1024]{2,1,0:T(4,128)S(1)} %add.14), channel_id=1, source_target_pairs={{0,8},{8,16},{16,24},{24,28},{28,20},{20,12},{12,4},{4,0},{1,9},{9... | collective-permute-start | bytes 393224 | tf_op jit(solution)/shard_map/ppermute | solution.py:505
  54.4 1.5 %collective-permute-start.21 = (f32[8,4,1024]{2,1,0:T(4,128)S(1)}, f32[8,4,1024]{2,1,0:T(4,128)S(1)}, u32[]{:S(2)}, u32[]{:S(2)}) collective-permute-start(f32[8,4,1024]{2,1,0:T(4,128)S(1)} %add.12), channel_id=1, source_target_pairs={{0,8},{8,16},{16,24},{24,28},{28,20},{20,12},{12,4},{4,0},{1,9},{9... | collective-permute-start | bytes 393224 | tf_op jit(solution)/shard_map/ppermute | solution.py:505
  55.9 1.2 %residual.1 = f32[2,256,128]{2,1,0:T(8,128)} custom-call(f32[1,128]{1,0:T(1,128)S(1)} %meta.1.refs_0_.meta_ref, f32[1,128]{1,0:T(1,128)S(1)} %collective-permute-done.1.refs_1_, f32[1,128]{1,0:T(1,128)S(1)} %collective-permute-done.2.refs_2_, f32[1,128]{1,0:T(1,128)S(1)} %collective-permute-done.3.refs_3_, f32[2,256,128]{2,1,0:T(8,128)S(1)} %get-tuple-element.48.refs_4_, ...), custom_call_target="tpu_custom_call" | custom-call | flops 100000000 | bytes 2097152 | tf_op jit(solution)/shard_map/residual/pallas_call | solution.py:679
  (66 shorter events, 19.6 us)
Async XLA Ops:
  0.6 9.5 %collective-permute-start = (f32[16,4,1024]{2,1,0:T(4,128)}, f32[16,4,1024]{2,1,0:T(4,128)S(1)}, u32[]{:S(2)}, u32[]{:S(2)}) collective-permute-start(f32[16,4,1024]{2,1,0:T(4,128)} %harmonics_ref.1), channel_id=1, source_target_pairs={{0,8},{8,16},{16,24},{24,28},{28,20},{20,12},{12,4},{4,0},{1,9},{9... | collective-permute-start | bytes 786440 | tf_op jit(solution)/shard_map/ppermute | solution.py:505
  3.7 8.3 %collective-permute-start.5 = (f32[16,4,1024]{2,1,0:T(4,128)}, f32[16,4,1024]{2,1,0:T(4,128)S(1)}, u32[]{:S(2)}, u32[]{:S(2)}) collective-permute-start(f32[16,4,1024]{2,1,0:T(4,128)} %harmonics_ref.1), channel_id=1, source_target_pairs={{0,4},{8,0},{16,8},{24,16},{28,24},{20,28},{12,20},{4,12},{1,5},{9... | collective-permute-start | bytes 786440 | tf_op jit(solution)/shard_map/ppermute | solution.py:505
  10.2 6.4 %collective-permute-start.4 = (f32[8,4,1024]{2,1,0:T(4,128)S(1)}, f32[8,4,1024]{2,1,0:T(4,128)S(1)}, u32[]{:S(2)}, u32[]{:S(2)}) collective-permute-start(f32[8,4,1024]{2,1,0:T(4,128)S(1)} %get-tuple-element.55), channel_id=1, source_target_pairs={{0,8},{8,16},{16,24},{24,28},{28,20},{20,12},{12,4},{4,0},{1,9},{9... | collective-permute-start | bytes 393224 | tf_op jit(solution)/shard_map/ppermute | solution.py:505
  12.1 6.3 %collective-permute-start.8 = (f32[8,4,1024]{2,1,0:T(4,128)S(1)}, f32[8,4,1024]{2,1,0:T(4,128)S(1)}, u32[]{:S(2)}, u32[]{:S(2)}) collective-permute-start(f32[8,4,1024]{2,1,0:T(4,128)S(1)} %get-tuple-element.52), channel_id=1, source_target_pairs={{0,4},{8,0},{16,8},{24,16},{28,24},{20,28},{12,20},{4,12},{1,5},{9... | collective-permute-start | bytes 393224 | tf_op jit(solution)/shard_map/ppermute | solution.py:505
  12.3 6.6 %collective-permute-start.6 = (f32[8,4,1024]{2,1,0:T(4,128)S(1)}, f32[8,4,1024]{2,1,0:T(4,128)S(1)}, u32[]{:S(2)}, u32[]{:S(2)}) collective-permute-start(f32[8,4,1024]{2,1,0:T(4,128)S(1)} %get-tuple-element.54), channel_id=1, source_target_pairs={{0,8},{8,16},{16,24},{24,28},{28,20},{20,12},{12,4},{4,0},{1,9},{9... | collective-permute-start | bytes 393224 | tf_op jit(solution)/shard_map/ppermute | solution.py:505
  14.1 6.4 %collective-permute-start.7 = (f32[8,4,1024]{2,1,0:T(4,128)S(1)}, f32[8,4,1024]{2,1,0:T(4,128)S(1)}, u32[]{:S(2)}, u32[]{:S(2)}) collective-permute-start(f32[8,4,1024]{2,1,0:T(4,128)S(1)} %get-tuple-element.53), channel_id=1, source_target_pairs={{0,4},{8,0},{16,8},{24,16},{28,24},{20,28},{12,20},{4,12},{1,5},{9... | collective-permute-start | bytes 393224 | tf_op jit(solution)/shard_map/ppermute | solution.py:505
  16.6 6.1 %collective-permute-start.9 = (f32[8,4,1024]{2,1,0:T(4,128)S(1)}, f32[8,4,1024]{2,1,0:T(4,128)S(1)}, u32[]{:S(2)}, u32[]{:S(2)}) collective-permute-start(f32[8,4,1024]{2,1,0:T(4,128)S(1)} %collective-permute-done.4.refs_5_), channel_id=1, source_target_pairs={{0,8},{8,16},{16,24},{24,28},{28,20},{20,12},{12,4},{4,0},{1,9},{9... | collective-permute-start | bytes 393224 | tf_op jit(solution)/shard_map/ppermute | solution.py:505
  18.3 5.8 %collective-permute-start.12 = (f32[8,4,1024]{2,1,0:T(4,128)S(1)}, f32[8,4,1024]{2,1,0:T(4,128)S(1)}, u32[]{:S(2)}, u32[]{:S(2)}) collective-permute-start(f32[8,4,1024]{2,1,0:T(4,128)S(1)} %collective-permute-done.8.refs_8_), channel_id=1, source_target_pairs={{0,4},{8,0},{16,8},{24,16},{28,24},{20,28},{12,20},{4,12},{1,5},{9... | collective-permute-start | bytes 393224 | tf_op jit(solution)/shard_map/ppermute | solution.py:505
  19.0 6.5 %collective-permute-start.10 = (f32[8,4,1024]{2,1,0:T(4,128)S(1)}, f32[8,4,1024]{2,1,0:T(4,128)S(1)}, u32[]{:S(2)}, u32[]{:S(2)}) collective-permute-start(f32[8,4,1024]{2,1,0:T(4,128)S(1)} %collective-permute-done.6.refs_6_), channel_id=1, source_target_pairs={{0,8},{8,16},{16,24},{24,28},{28,20},{20,12},{12,4},{4,0},{1,9},{9... | collective-permute-start | bytes 393224 | tf_op jit(solution)/shard_map/ppermute | solution.py:505
  20.5 6.2 %collective-permute-start.11 = (f32[8,4,1024]{2,1,0:T(4,128)S(1)}, f32[8,4,1024]{2,1,0:T(4,128)S(1)}, u32[]{:S(2)}, u32[]{:S(2)}) collective-permute-start(f32[8,4,1024]{2,1,0:T(4,128)S(1)} %collective-permute-done.7.refs_7_), channel_id=1, source_target_pairs={{0,4},{8,0},{16,8},{24,16},{28,24},{20,28},{12,20},{4,12},{1,5},{9... | collective-permute-start | bytes 393224 | tf_op jit(solution)/shard_map/ppermute | solution.py:505
  22.8 5.5 %collective-permute-start.13 = (f32[8,4,1024]{2,1,0:T(4,128)S(1)}, f32[8,4,1024]{2,1,0:T(4,128)S(1)}, u32[]{:S(2)}, u32[]{:S(2)}) collective-permute-start(f32[8,4,1024]{2,1,0:T(4,128)S(1)} %collective-permute-done.9.refs_9_), channel_id=1, source_target_pairs={{0,8},{8,16},{16,24},{24,28},{28,20},{20,12},{12,4},{4,0},{1,9},{9... | collective-permute-start | bytes 393224 | tf_op jit(solution)/shard_map/ppermute | solution.py:505
  35.1 6.6 %collective-permute-start.28 = (f32[8,4,1024]{2,1,0:T(4,128)S(1)}, f32[8,4,1024]{2,1,0:T(4,128)S(1)}, u32[]{:S(2)}, u32[]{:S(2)}) collective-permute-start(f32[8,4,1024]{2,1,0:T(4,128)S(1)} %get-tuple-element.47), channel_id=1, source_target_pairs={{0,4},{8,0},{16,8},{24,16},{28,24},{20,28},{12,20},{4,12},{1,5},{9... | collective-permute-start | bytes 393224 | tf_op jit(solution)/shard_map/ppermute | solution.py:505
  35.6 6.6 %collective-permute-start.18 = (f32[8,4,1024]{2,1,0:T(4,128)S(1)}, f32[8,4,1024]{2,1,0:T(4,128)S(1)}, u32[]{:S(2)}, u32[]{:S(2)}) collective-permute-start(f32[8,4,1024]{2,1,0:T(4,128)S(1)} %get-tuple-element.44), channel_id=1, source_target_pairs={{0,8},{8,16},{16,24},{24,28},{28,20},{20,12},{12,4},{4,0},{1,9},{9... | collective-permute-start | bytes 393224 | tf_op jit(solution)/shard_map/ppermute | solution.py:505
  37.7 6.3 %collective-permute-start.25 = (f32[8,4,1024]{2,1,0:T(4,128)S(1)}, f32[8,4,1024]{2,1,0:T(4,128)S(1)}, u32[]{:S(2)}, u32[]{:S(2)}) collective-permute-start(f32[8,4,1024]{2,1,0:T(4,128)S(1)} %get-tuple-element.46), channel_id=1, source_target_pairs={{0,4},{8,0},{16,8},{24,16},{28,24},{20,28},{12,20},{4,12},{1,5},{9... | collective-permute-start | bytes 393224 | tf_op jit(solution)/shard_map/ppermute | solution.py:505
  41.7 5.8 %collective-permute-start.29 = (f32[8,4,1024]{2,1,0:T(4,128)S(1)}, f32[8,4,1024]{2,1,0:T(4,128)S(1)}, u32[]{:S(2)}, u32[]{:S(2)}) collective-permute-start(f32[8,4,1024]{2,1,0:T(4,128)S(1)} %add.17), channel_id=1, source_target_pairs={{0,4},{8,0},{16,8},{24,16},{28,24},{20,28},{12,20},{4,12},{1,5},{9... | collective-permute-start | bytes 393224 | tf_op jit(solution)/shard_map/ppermute | solution.py:505
  42.3 6.3 %collective-permute-start.19 = (f32[8,4,1024]{2,1,0:T(4,128)S(1)}, f32[8,4,1024]{2,1,0:T(4,128)S(1)}, u32[]{:S(2)}, u32[]{:S(2)}) collective-permute-start(f32[8,4,1024]{2,1,0:T(4,128)S(1)} %add.10), channel_id=1, source_target_pairs={{0,8},{8,16},{16,24},{24,28},{28,20},{20,12},{12,4},{4,0},{1,9},{9... | collective-permute-start | bytes 393224 | tf_op jit(solution)/shard_map/ppermute | solution.py:505
  44.0 6.4 %collective-permute-start.26 = (f32[8,4,1024]{2,1,0:T(4,128)S(1)}, f32[8,4,1024]{2,1,0:T(4,128)S(1)}, u32[]{:S(2)}, u32[]{:S(2)}) collective-permute-start(f32[8,4,1024]{2,1,0:T(4,128)S(1)} %add.15), channel_id=1, source_target_pairs={{0,4},{8,0},{16,8},{24,16},{28,24},{20,28},{12,20},{4,12},{1,5},{9... | collective-permute-start | bytes 393224 | tf_op jit(solution)/shard_map/ppermute | solution.py:505
  45.4 6.1 %collective-permute-start.23 = (f32[8,4,1024]{2,1,0:T(4,128)S(1)}, f32[8,4,1024]{2,1,0:T(4,128)S(1)}, u32[]{:S(2)}, u32[]{:S(2)}) collective-permute-start(f32[8,4,1024]{2,1,0:T(4,128)S(1)} %add.13), channel_id=1, source_target_pairs={{0,8},{8,16},{16,24},{24,28},{28,20},{20,12},{12,4},{4,0},{1,9},{9... | collective-permute-start | bytes 393224 | tf_op jit(solution)/shard_map/ppermute | solution.py:505
  47.5 5.7 %collective-permute-start.30 = (f32[8,4,1024]{2,1,0:T(4,128)S(1)}, f32[8,4,1024]{2,1,0:T(4,128)S(1)}, u32[]{:S(2)}, u32[]{:S(2)}) collective-permute-start(f32[8,4,1024]{2,1,0:T(4,128)S(1)} %add.18), channel_id=1, source_target_pairs={{0,4},{8,0},{16,8},{24,16},{28,24},{20,28},{12,20},{4,12},{1,5},{9... | collective-permute-start | bytes 393224 | tf_op jit(solution)/shard_map/ppermute | solution.py:505
  48.6 5.8 %collective-permute-start.20 = (f32[8,4,1024]{2,1,0:T(4,128)S(1)}, f32[8,4,1024]{2,1,0:T(4,128)S(1)}, u32[]{:S(2)}, u32[]{:S(2)}) collective-permute-start(f32[8,4,1024]{2,1,0:T(4,128)S(1)} %add.11), channel_id=1, source_target_pairs={{0,8},{8,16},{16,24},{24,28},{28,20},{20,12},{12,4},{4,0},{1,9},{9... | collective-permute-start | bytes 393224 | tf_op jit(solution)/shard_map/ppermute | solution.py:505
  50.5 6.6 %collective-permute-start.27 = (f32[8,4,1024]{2,1,0:T(4,128)S(1)}, f32[8,4,1024]{2,1,0:T(4,128)S(1)}, u32[]{:S(2)}, u32[]{:S(2)}) collective-permute-start(f32[8,4,1024]{2,1,0:T(4,128)S(1)} %add.16), channel_id=1, source_target_pairs={{0,4},{8,0},{16,8},{24,16},{28,24},{20,28},{12,20},{4,12},{1,5},{9... | collective-permute-start | bytes 393224 | tf_op jit(solution)/shard_map/ppermute | solution.py:505
  51.5 6.3 %collective-permute-start.24 = (f32[8,4,1024]{2,1,0:T(4,128)S(1)}, f32[8,4,1024]{2,1,0:T(4,128)S(1)}, u32[]{:S(2)}, u32[]{:S(2)}) collective-permute-start(f32[8,4,1024]{2,1,0:T(4,128)S(1)} %add.14), channel_id=1, source_target_pairs={{0,8},{8,16},{16,24},{24,28},{28,20},{20,12},{12,4},{4,0},{1,9},{9... | collective-permute-start | bytes 393224 | tf_op jit(solution)/shard_map/ppermute | solution.py:505
  53.3 5.3 %collective-permute-start.31 = (f32[8,4,1024]{2,1,0:T(4,128)S(1)}, f32[8,4,1024]{2,1,0:T(4,128)S(1)}, u32[]{:S(2)}, u32[]{:S(2)}) collective-permute-start(f32[8,4,1024]{2,1,0:T(4,128)S(1)} %add.19), channel_id=1, source_target_pairs={{0,4},{8,0},{16,8},{24,16},{28,24},{20,28},{12,20},{4,12},{1,5},{9... | collective-permute-start | bytes 393224 | tf_op jit(solution)/shard_map/ppermute | solution.py:505
  54.4 5.3 %collective-permute-start.21 = (f32[8,4,1024]{2,1,0:T(4,128)S(1)}, f32[8,4,1024]{2,1,0:T(4,128)S(1)}, u32[]{:S(2)}, u32[]{:S(2)}) collective-permute-start(f32[8,4,1024]{2,1,0:T(4,128)S(1)} %add.12), channel_id=1, source_target_pairs={{0,8},{8,16},{16,24},{24,28},{28,20},{20,12},{12,4},{4,0},{1,9},{9... | collective-permute-start | bytes 393224 | tf_op jit(solution)/shard_map/ppermute | solution.py:505
  (9 other events, 53.3 us)

commit v6 on v5

--- a/solution.py
+++ b/solution.py
@@ -205,8 +205,6 @@
         minus = jnp.where(keep, minus, 0.0)
     for a in range(4):
         c = coefs(a)
-        if keep is not None:
-            c = jnp.where(keep[:1], c, 0.0)
         p[a] = p[a] + plus * c
         n[a] = n[a] + minus * c
 
@@ -380,7 +378,7 @@
         update_block(tables, m, first, an, ng, row8, sends[half], at)
 
 
-def second_kernel(tables, analysed_ref, low_ref, high_ref):
+def second_kernel(ways, tables, analysed_ref, low_ref, high_ref):
     slots, _, _, degrees = tables.shape
     middle, _, width = low_ref.shape
     blocks = degrees // width
@@ -388,7 +386,7 @@
     row8 = lax.broadcasted_iota(jnp.int32, (8, LANES), 0)
     for m in range(slots):
         half, at = divmod(m, middle)
-        step = (1 - blocks // 2, blocks // 2 - 1)[half]
+        step = ways[half] * (blocks // 2 - 1)
         first = pl.multiple_of(block_at(place + step, blocks) * width, LANES)
         an = [analysed_ref[m, a] for a in range(4)]
         ng = [-value for value in an]
@@ -396,7 +394,10 @@
 
 
 def backward_kernel(core, tables, analysed_ref, *rest):
-    pl.when(on_core(core))(lambda: backward_blocks(tables, analysed_ref, rest[-1]))
+    if core is None:
+        backward_blocks(tables, analysed_ref, rest[-1])
+    else:
+        pl.when(on_core(core))(lambda: backward_blocks(tables, analysed_ref, rest[-1]))
 
 
 def backward_blocks(tables, analysed_ref, out):
@@ -458,6 +459,10 @@
         out_ref[c] = section_ref[c] - jnp.where(inside, model, 0.0)
 
 
+def join_kernel(own_ref, value_ref, out_ref):
+    out_ref[...] = own_ref[...] + value_ref[...]
+
+
 def add_kernel(index, first, piece_ref, value_ref, out_ref):
     out_ref[...] = piece_ref[index, first : first + out_ref.shape[0]] + value_ref[...]
 
@@ -613,15 +618,19 @@
         cost_estimate=estimate(1),
         name="analysed",
     )(tables, gram, pieces, phases, *messages)
-    second = pl.pallas_call(
-        second_kernel,
-        out_shape=[half] * 2,
-        in_specs=[vmem()] * 2,
-        out_specs=[vmem()] * 2,
-        compiler_params=pltpu.CompilerParams(vmem_limit_bytes=16 * MIB),
-        cost_estimate=estimate(0.5),
-        name="second",
-    )(tables, analysed)
+    def nearer(ways):
+        return pl.pallas_call(
+            lambda *refs: second_kernel(ways, *refs),
+            out_shape=[half] * 2,
+            in_specs=[vmem()] * 2,
+            out_specs=[vmem()] * 2,
+            compiler_params=pltpu.CompilerParams(vmem_limit_bytes=16 * MIB),
+            cost_estimate=estimate(0.5),
+            name="second",
+        )(tables, analysed)
+
+    second = nearer((-1, 1))
+    third = nearer((1, -1))
 
     def backward(core, *before):
         return pl.pallas_call(
@@ -638,9 +647,7 @@
             *[pltpu.with_memory_space_constraint(value, pltpu.VMEM) for value in before],
         )
 
-    piece = backward(1)
-    *sends, piece = lax.optimization_barrier((*sends, piece))
-    piece = backward(0, piece)
+    piece = backward(None)
 
     def add(index, first, value):
         return pl.pallas_call(
@@ -655,8 +662,16 @@
 
     sent = dict(zip(((1, 0), (-1, middle), (-1, 0), (1, middle)), (*sends, *second)))
     first_hop = {key: turn(sent[key], key[0]) for key in ((1, 0), (-1, middle))}
-    for key in ((1, 0), (-1, middle)):
-        sent[key] = add((key[0] * (far - 1)) % blocks, key[1], first_hop[key])
+    for key, own in zip(((1, 0), (-1, middle)), third):
+        sent[key] = pl.pallas_call(
+            join_kernel,
+            out_shape=half,
+            in_specs=[vmem()] * 2,
+            out_specs=vmem(),
+            compiler_params=pltpu.CompilerParams(vmem_limit_bytes=4 * MIB),
+            cost_estimate=estimate(0.1),
+            name="join",
+        )(own, pltpu.with_memory_space_constraint(first_hop[key], pltpu.VMEM))
     for k in reversed(range(1, far)):
         for key in ((1, middle), (-1, 0), (1, 0), (-1, middle)):
             sent[key] = turn(sent[key], key[0])

time: 60.7 us -> 60.4 us (level)
    pallas_call x2 -> x1, Pallas kernels: 1.94 us -> 1.92 us  [backward(): pl.pallas_call(lambda *refs: backward_kernel(core, *refs), out_shape=pltp...]
  transfers between devices with their start and end apart: 32 -> 32, of which waited for: 20 -> 15; matrix products, arithmetic and copies ran while one was open for 0% -> 0% of each run, Pallas kernels for 17% -> 18%
where the time goes in v6:
time: 60.4 us; the launch traced here: 60.2 us
  starting transfers between devices  32.2 us (53%)
  waiting for transfers between devices  13.9 us (23%)
  Pallas kernels  13.3 us (22%)
  between operations  0.79 us (1%)
    ppermute x26, starting transfers between devices, turn(): return lax.ppermute(value, 'blk', pairs)  28.2 us
    ppermute x26, waiting for transfers between devices, turn(): return lax.ppermute(value, 'blk', pairs)  11.3 us
    ppermute x6, starting transfers between devices, swap(): return lax.ppermute(value, axis, [(i, i ^ step) for i in range(size)])  4 us
    ppermute x6, waiting for transfers between devices, swap(): return lax.ppermute(value, axis, [(i, i ^ step) for i in range(size)])  2.58 us
    pallas_call x1, Pallas kernels, body(): pl.pallas_call(tables_kernel, out_shape=pltpu.VMEM(legendre.shape, jnp.fl...  2.31 us
    pallas_call x1, Pallas kernels, backward(): pl.pallas_call(lambda *refs: backward_kernel(core, *refs), out_shape=pltp...  1.92 us
    pallas_call x1, Pallas kernels, body(): pl.pallas_call(lambda *refs: sky_kernel(normalise, groups, slots, cycles,...  1.77 us
    pallas_call x1, Pallas kernels, body(): pl.pallas_call(lambda *refs: forward_kernel(steps, firsts, *refs), out_sh...  1.44 us
  transfers between devices with their start and end apart: 32, of which 15 were waited for; matrix products, arithmetic and copies ran while one was open for 0% of the time, Pallas kernels for 18%

profile of v6, /device:TPU:0, one launch (start us, length us, event | category | flops | bytes accessed | tf_op | source)
XLA Modules:
  0.0 60.2 jit_solution(9093614568556760833)
XLA Ops:
  0.6 3.1 %collective-permute-start = (f32[16,4,1024]{2,1,0:T(4,128)}, f32[16,4,1024]{2,1,0:T(4,128)S(1)}, u32[]{:S(2)}, u32[]{:S(2)}) collective-permute-start(f32[16,4,1024]{2,1,0:T(4,128)} %harmonics_ref.1), channel_id=1, source_target_pairs={{0,8},{8,16},{16,24},{24,28},{28,20},{20,12},{12,4},{4,0},{1,9},{9... | collective-permute-start | bytes 786440 | tf_op jit(solution)/shard_map/ppermute | solution.py:510
  4.6 2.0 %collective-permute-start.2 = (f32[1,128]{1,0:T(1,128)S(1)}, f32[1,128]{1,0:T(1,128)S(1)}, u32[]{:S(2)}, u32[]{:S(2)}) collective-permute-start(f32[1,128]{1,0:T(1,128)S(1)} %meta.1.refs_0_.meta_ref), channel_id=1, source_target_pairs={{0,2},{1,3},{2,0},{3,1},{4,6},{5,7},{6,4},{7,5},{8,10},{9,11},{10,... | collective-permute-start | bytes 1544 | tf_op jit(solution)/shard_map/ppermute | solution.py:504
  6.6 2.3 %tables.1.refs_1_.refs_0_ = f32[16,2,8,8192]{3,2,1,0:T(8,128)S(1)} custom-call(f32[16,2,8,8192]{3,2,1,0:T(8,128)} %legendre.1), custom_call_target="tpu_custom_call" | custom-call | bytes 4500000 | tf_op jit(solution)/shard_map/tables/pallas_call | solution.py:533
  10.2 1.8 %collective-permute-start.4 = (f32[8,4,1024]{2,1,0:T(4,128)S(1)}, f32[8,4,1024]{2,1,0:T(4,128)S(1)}, u32[]{:S(2)}, u32[]{:S(2)}) collective-permute-start(f32[8,4,1024]{2,1,0:T(4,128)S(1)} %get-tuple-element.53), channel_id=1, source_target_pairs={{0,8},{8,16},{16,24},{24,28},{28,20},{20,12},{12,4},{4,0},{1,9},{9... | collective-permute-start | bytes 393224 | tf_op jit(solution)/shard_map/ppermute | solution.py:510
  12.3 1.8 %collective-permute-start.6 = (f32[8,4,1024]{2,1,0:T(4,128)S(1)}, f32[8,4,1024]{2,1,0:T(4,128)S(1)}, u32[]{:S(2)}, u32[]{:S(2)}) collective-permute-start(f32[8,4,1024]{2,1,0:T(4,128)S(1)} %get-tuple-element.52), channel_id=1, source_target_pairs={{0,8},{8,16},{16,24},{24,28},{28,20},{20,12},{12,4},{4,0},{1,9},{9... | collective-permute-start | bytes 393224 | tf_op jit(solution)/shard_map/ppermute | solution.py:510
  14.4 1.8 %sky_analysis.1 = (f32[4,8,128]{2,1,0:T(8,128)S(1)}, f32[2,256,128]{2,1,0:T(8,128)S(1)}, f32[2,256,128]{2,1,0:T(8,128)S(1)}, f32[2,128,128]{2,1,0:T(8,128)S(1)}, f32[2,256,128]{2,1,0:T(8,128)S(1)}) custom-call(f32[1,128]{1,0:T(1,128)S(1)} %meta.1.refs_0_.meta_ref, f32[1,128]{1,0:T(1,128)S(1)} %collective-permute-done.1.refs_1_, ...), custom_call_target="tpu_custom_call" | custom-call | bytes 9000000 | tf_op jit(solution)/shard_map/sky_analysis/pallas_call | solution.py:549
  16.6 1.7 %collective-permute-start.9 = (f32[8,4,1024]{2,1,0:T(4,128)S(1)}, f32[8,4,1024]{2,1,0:T(4,128)S(1)}, u32[]{:S(2)}, u32[]{:S(2)}) collective-permute-start(f32[8,4,1024]{2,1,0:T(4,128)S(1)} %collective-permute-done.4.refs_5_), channel_id=1, source_target_pairs={{0,8},{8,16},{16,24},{24,28},{28,20},{20,12},{12,4},{4,0},{1,9},{9... | collective-permute-start | bytes 393224 | tf_op jit(solution)/shard_map/ppermute | solution.py:510
  19.0 1.6 %collective-permute-start.10 = (f32[8,4,1024]{2,1,0:T(4,128)S(1)}, f32[8,4,1024]{2,1,0:T(4,128)S(1)}, u32[]{:S(2)}, u32[]{:S(2)}) collective-permute-start(f32[8,4,1024]{2,1,0:T(4,128)S(1)} %collective-permute-done.6.refs_6_), channel_id=1, source_target_pairs={{0,8},{8,16},{16,24},{24,28},{28,20},{20,12},{12,4},{4,0},{1,9},{9... | collective-permute-start | bytes 393224 | tf_op jit(solution)/shard_map/ppermute | solution.py:510
  21.0 1.8 %collective-permute-done.9.refs_9_ = f32[8,4,1024]{2,1,0:T(4,128)S(1)} collective-permute-done((f32[8,4,1024]{2,1,0:T(4,128)S(1)}, f32[8,4,1024]{2,1,0:T(4,128)S(1)}, u32[]{:S(2)}, u32[]{:S(2)}) %collective-permute-start.9) | collective-permute-done | bytes 131104 | tf_op jit(solution)/shard_map/ppermute | solution.py:510
  22.8 1.4 %collective-permute-start.13 = (f32[8,4,1024]{2,1,0:T(4,128)S(1)}, f32[8,4,1024]{2,1,0:T(4,128)S(1)}, u32[]{:S(2)}, u32[]{:S(2)}) collective-permute-start(f32[8,4,1024]{2,1,0:T(4,128)S(1)} %collective-permute-done.9.refs_9_), channel_id=1, source_target_pairs={{0,8},{8,16},{16,24},{24,28},{28,20},{20,12},{12,4},{4,0},{1,9},{9... | collective-permute-start | bytes 393224 | tf_op jit(solution)/shard_map/ppermute | solution.py:510
  25.4 1.3 %collective-permute-done.11.refs_11_ = f32[8,4,1024]{2,1,0:T(4,128)S(1)} collective-permute-done((f32[8,4,1024]{2,1,0:T(4,128)S(1)}, f32[8,4,1024]{2,1,0:T(4,128)S(1)}, u32[]{:S(2)}, u32[]{:S(2)}) %collective-permute-start.11) | collective-permute-done | bytes 131104 | tf_op jit(solution)/shard_map/ppermute | solution.py:510
  26.7 1.4 %forward.1.refs_3_ = f32[16,4,8,128]{3,2,1,0:T(8,128)S(1)} custom-call(f32[1,128]{1,0:T(1,128)S(1)} %meta.1.refs_0_.meta_ref, f32[16,2,8,8192]{3,2,1,0:T(8,128)S(1)} %tables.1.refs_1_.refs_0_, f32[16,4,1024]{2,1,0:T(4,128)S(1)} %copy-done, f32[16,4,1024]{2,1,0:T(4,128)S(1)} %collective-permute-done.refs_3_, ...), custom_call_target="tpu_custom_call" | custom-call | bytes 6000000 | tf_op jit(solution)/shard_map/forward/pallas_call | solution.py:589
  32.3 1.4 %collective-permute-done.16.refs_5_.refs_10_ = f32[16,128]{1,0:T(8,128)S(1)} collective-permute-done((f32[16,128]{1,0:T(8,128)S(1)}, f32[16,128]{1,0:T(8,128)S(1)}, u32[]{:S(2)}, u32[]{:S(2)}) %collective-permute-start.16) | collective-permute-done | bytes 8224 | tf_op jit(solution)/shard_map/ppermute | solution.py:504
  35.5 1.6 %collective-permute-start.18 = (f32[8,4,1024]{2,1,0:T(4,128)S(1)}, f32[8,4,1024]{2,1,0:T(4,128)S(1)}, u32[]{:S(2)}, u32[]{:S(2)}) collective-permute-start(f32[8,4,1024]{2,1,0:T(4,128)S(1)} %get-tuple-element.41), channel_id=1, source_target_pairs={{0,8},{8,16},{16,24},{24,28},{28,20},{20,12},{12,4},{4,0},{1,9},{9... | collective-permute-start | bytes 393224 | tf_op jit(solution)/shard_map/ppermute | solution.py:510
  38.5 1.6 %collective-permute-start.22 = (f32[8,4,1024]{2,1,0:T(4,128)S(1)}, f32[8,4,1024]{2,1,0:T(4,128)S(1)}, u32[]{:S(2)}, u32[]{:S(2)}) collective-permute-start(f32[8,4,1024]{2,1,0:T(4,128)S(1)} %get-tuple-element.42), channel_id=1, source_target_pairs={{0,8},{8,16},{16,24},{24,28},{28,20},{20,12},{12,4},{4,0},{1,9},{9... | collective-permute-start | bytes 393224 | tf_op jit(solution)/shard_map/ppermute | solution.py:510
  41.4 1.7 %collective-permute-start.19 = (f32[8,4,1024]{2,1,0:T(4,128)S(1)}, f32[8,4,1024]{2,1,0:T(4,128)S(1)}, u32[]{:S(2)}, u32[]{:S(2)}) collective-permute-start(f32[8,4,1024]{2,1,0:T(4,128)S(1)} %join.2), channel_id=1, source_target_pairs={{0,8},{8,16},{16,24},{24,28},{28,20},{20,12},{12,4},{4,0},{1,9},{9... | collective-permute-start | bytes 393224 | tf_op jit(solution)/shard_map/ppermute | solution.py:510
  43.1 1.9 %backward.1.refs_0_.piece_ref = f32[8,16,4,1024]{3,2,1,0:T(4,128)S(1)} custom-call(f32[16,2,8,8192]{3,2,1,0:T(8,128)S(1)} %tables.1.refs_1_.refs_0_, f32[16,4,8,128]{3,2,1,0:T(8,128)S(1)} %get-tuple-element.39.refs_1_), custom_call_target="tpu_custom_call" | custom-call | bytes 6000000 | tf_op jit(solution)/shard_map/backward/pallas_call | solution.py:636
  45.5 1.7 %collective-permute-start.23 = (f32[8,4,1024]{2,1,0:T(4,128)S(1)}, f32[8,4,1024]{2,1,0:T(4,128)S(1)}, u32[]{:S(2)}, u32[]{:S(2)}) collective-permute-start(f32[8,4,1024]{2,1,0:T(4,128)S(1)} %add.10), channel_id=1, source_target_pairs={{0,8},{8,16},{16,24},{24,28},{28,20},{20,12},{12,4},{4,0},{1,9},{9... | collective-permute-start | bytes 393224 | tf_op jit(solution)/shard_map/ppermute | solution.py:510
  47.7 1.7 %collective-permute-start.20 = (f32[8,4,1024]{2,1,0:T(4,128)S(1)}, f32[8,4,1024]{2,1,0:T(4,128)S(1)}, u32[]{:S(2)}, u32[]{:S(2)}) collective-permute-start(f32[8,4,1024]{2,1,0:T(4,128)S(1)} %add.8), channel_id=1, source_target_pairs={{0,8},{8,16},{16,24},{24,28},{28,20},{20,12},{12,4},{4,0},{1,9},{9... | collective-permute-start | bytes 393224 | tf_op jit(solution)/shard_map/ppermute | solution.py:510
  49.4 1.8 %collective-permute-done.26.refs_1_ = f32[8,4,1024]{2,1,0:T(4,128)S(1)} collective-permute-done((f32[8,4,1024]{2,1,0:T(4,128)S(1)}, f32[8,4,1024]{2,1,0:T(4,128)S(1)}, u32[]{:S(2)}, u32[]{:S(2)}) %collective-permute-start.26) | collective-permute-done | bytes 131104 | tf_op jit(solution)/shard_map/ppermute | solution.py:510
  51.5 1.8 %collective-permute-start.24 = (f32[8,4,1024]{2,1,0:T(4,128)S(1)}, f32[8,4,1024]{2,1,0:T(4,128)S(1)}, u32[]{:S(2)}, u32[]{:S(2)}) collective-permute-start(f32[8,4,1024]{2,1,0:T(4,128)S(1)} %add.11), channel_id=1, source_target_pairs={{0,8},{8,16},{16,24},{24,28},{28,20},{20,12},{12,4},{4,0},{1,9},{9... | collective-permute-start | bytes 393224 | tf_op jit(solution)/shard_map/ppermute | solution.py:510
  54.3 1.8 %collective-permute-start.21 = (f32[8,4,1024]{2,1,0:T(4,128)S(1)}, f32[8,4,1024]{2,1,0:T(4,128)S(1)}, u32[]{:S(2)}, u32[]{:S(2)}) collective-permute-start(f32[8,4,1024]{2,1,0:T(4,128)S(1)} %add.9), channel_id=1, source_target_pairs={{0,8},{8,16},{16,24},{24,28},{28,20},{20,12},{12,4},{4,0},{1,9},{9... | collective-permute-start | bytes 393224 | tf_op jit(solution)/shard_map/ppermute | solution.py:510
  56.2 1.2 %residual.1 = f32[2,256,128]{2,1,0:T(8,128)} custom-call(f32[1,128]{1,0:T(1,128)S(1)} %meta.1.refs_0_.meta_ref, f32[1,128]{1,0:T(1,128)S(1)} %collective-permute-done.1.refs_1_, f32[1,128]{1,0:T(1,128)S(1)} %collective-permute-done.2.refs_2_, f32[1,128]{1,0:T(1,128)S(1)} %collective-permute-done.3.refs_3_, f32[2,256,128]{2,1,0:T(8,128)S(1)} %get-tuple-element.46.refs_4_, ...), custom_call_target="tpu_custom_call" | custom-call | flops 100000000 | bytes 2097152 | tf_op jit(solution)/shard_map/residual/pallas_call | solution.py:694
  57.4 1.6 %collective-permute-done.31.rest_3_ = f32[8,4,1024]{2,1,0:T(4,128)S(1)} collective-permute-done((f32[8,4,1024]{2,1,0:T(4,128)S(1)}, f32[8,4,1024]{2,1,0:T(4,128)S(1)}, u32[]{:S(2)}, u32[]{:S(2)}) %collective-permute-start.31) | collective-permute-done | bytes 131104 | tf_op jit(solution)/shard_map/ppermute | solution.py:510
  (66 shorter events, 17.5 us)
Async XLA Ops:
  0.6 9.5 %collective-permute-start = (f32[16,4,1024]{2,1,0:T(4,128)}, f32[16,4,1024]{2,1,0:T(4,128)S(1)}, u32[]{:S(2)}, u32[]{:S(2)}) collective-permute-start(f32[16,4,1024]{2,1,0:T(4,128)} %harmonics_ref.1), channel_id=1, source_target_pairs={{0,8},{8,16},{16,24},{24,28},{28,20},{20,12},{12,4},{4,0},{1,9},{9... | collective-permute-start | bytes 786440 | tf_op jit(solution)/shard_map/ppermute | solution.py:510
  3.7 8.3 %collective-permute-start.5 = (f32[16,4,1024]{2,1,0:T(4,128)}, f32[16,4,1024]{2,1,0:T(4,128)S(1)}, u32[]{:S(2)}, u32[]{:S(2)}) collective-permute-start(f32[16,4,1024]{2,1,0:T(4,128)} %harmonics_ref.1), channel_id=1, source_target_pairs={{0,4},{8,0},{16,8},{24,16},{28,24},{20,28},{12,20},{4,12},{1,5},{9... | collective-permute-start | bytes 786440 | tf_op jit(solution)/shard_map/ppermute | solution.py:510
  10.2 6.4 %collective-permute-start.4 = (f32[8,4,1024]{2,1,0:T(4,128)S(1)}, f32[8,4,1024]{2,1,0:T(4,128)S(1)}, u32[]{:S(2)}, u32[]{:S(2)}) collective-permute-start(f32[8,4,1024]{2,1,0:T(4,128)S(1)} %get-tuple-element.53), channel_id=1, source_target_pairs={{0,8},{8,16},{16,24},{24,28},{28,20},{20,12},{12,4},{4,0},{1,9},{9... | collective-permute-start | bytes 393224 | tf_op jit(solution)/shard_map/ppermute | solution.py:510
  12.1 6.3 %collective-permute-start.8 = (f32[8,4,1024]{2,1,0:T(4,128)S(1)}, f32[8,4,1024]{2,1,0:T(4,128)S(1)}, u32[]{:S(2)}, u32[]{:S(2)}) collective-permute-start(f32[8,4,1024]{2,1,0:T(4,128)S(1)} %get-tuple-element.50), channel_id=1, source_target_pairs={{0,4},{8,0},{16,8},{24,16},{28,24},{20,28},{12,20},{4,12},{1,5},{9... | collective-permute-start | bytes 393224 | tf_op jit(solution)/shard_map/ppermute | solution.py:510
  12.3 6.6 %collective-permute-start.6 = (f32[8,4,1024]{2,1,0:T(4,128)S(1)}, f32[8,4,1024]{2,1,0:T(4,128)S(1)}, u32[]{:S(2)}, u32[]{:S(2)}) collective-permute-start(f32[8,4,1024]{2,1,0:T(4,128)S(1)} %get-tuple-element.52), channel_id=1, source_target_pairs={{0,8},{8,16},{16,24},{24,28},{28,20},{20,12},{12,4},{4,0},{1,9},{9... | collective-permute-start | bytes 393224 | tf_op jit(solution)/shard_map/ppermute | solution.py:510
  14.1 6.4 %collective-permute-start.7 = (f32[8,4,1024]{2,1,0:T(4,128)S(1)}, f32[8,4,1024]{2,1,0:T(4,128)S(1)}, u32[]{:S(2)}, u32[]{:S(2)}) collective-permute-start(f32[8,4,1024]{2,1,0:T(4,128)S(1)} %get-tuple-element.51), channel_id=1, source_target_pairs={{0,4},{8,0},{16,8},{24,16},{28,24},{20,28},{12,20},{4,12},{1,5},{9... | collective-permute-start | bytes 393224 | tf_op jit(solution)/shard_map/ppermute | solution.py:510
  16.6 6.1 %collective-permute-start.9 = (f32[8,4,1024]{2,1,0:T(4,128)S(1)}, f32[8,4,1024]{2,1,0:T(4,128)S(1)}, u32[]{:S(2)}, u32[]{:S(2)}) collective-permute-start(f32[8,4,1024]{2,1,0:T(4,128)S(1)} %collective-permute-done.4.refs_5_), channel_id=1, source_target_pairs={{0,8},{8,16},{16,24},{24,28},{28,20},{20,12},{12,4},{4,0},{1,9},{9... | collective-permute-start | bytes 393224 | tf_op jit(solution)/shard_map/ppermute | solution.py:510
  18.3 5.8 %collective-permute-start.12 = (f32[8,4,1024]{2,1,0:T(4,128)S(1)}, f32[8,4,1024]{2,1,0:T(4,128)S(1)}, u32[]{:S(2)}, u32[]{:S(2)}) collective-permute-start(f32[8,4,1024]{2,1,0:T(4,128)S(1)} %collective-permute-done.8.refs_8_), channel_id=1, source_target_pairs={{0,4},{8,0},{16,8},{24,16},{28,24},{20,28},{12,20},{4,12},{1,5},{9... | collective-permute-start | bytes 393224 | tf_op jit(solution)/shard_map/ppermute | solution.py:510
  19.0 6.5 %collective-permute-start.10 = (f32[8,4,1024]{2,1,0:T(4,128)S(1)}, f32[8,4,1024]{2,1,0:T(4,128)S(1)}, u32[]{:S(2)}, u32[]{:S(2)}) collective-permute-start(f32[8,4,1024]{2,1,0:T(4,128)S(1)} %collective-permute-done.6.refs_6_), channel_id=1, source_target_pairs={{0,8},{8,16},{16,24},{24,28},{28,20},{20,12},{12,4},{4,0},{1,9},{9... | collective-permute-start | bytes 393224 | tf_op jit(solution)/shard_map/ppermute | solution.py:510
  20.5 6.2 %collective-permute-start.11 = (f32[8,4,1024]{2,1,0:T(4,128)S(1)}, f32[8,4,1024]{2,1,0:T(4,128)S(1)}, u32[]{:S(2)}, u32[]{:S(2)}) collective-permute-start(f32[8,4,1024]{2,1,0:T(4,128)S(1)} %collective-permute-done.7.refs_7_), channel_id=1, source_target_pairs={{0,4},{8,0},{16,8},{24,16},{28,24},{20,28},{12,20},{4,12},{1,5},{9... | collective-permute-start | bytes 393224 | tf_op jit(solution)/shard_map/ppermute | solution.py:510
  22.8 5.4 %collective-permute-start.13 = (f32[8,4,1024]{2,1,0:T(4,128)S(1)}, f32[8,4,1024]{2,1,0:T(4,128)S(1)}, u32[]{:S(2)}, u32[]{:S(2)}) collective-permute-start(f32[8,4,1024]{2,1,0:T(4,128)S(1)} %collective-permute-done.9.refs_9_), channel_id=1, source_target_pairs={{0,8},{8,16},{16,24},{24,28},{28,20},{20,12},{12,4},{4,0},{1,9},{9... | collective-permute-start | bytes 393224 | tf_op jit(solution)/shard_map/ppermute | solution.py:510
  35.0 5.9 %collective-permute-start.28 = (f32[8,4,1024]{2,1,0:T(4,128)S(1)}, f32[8,4,1024]{2,1,0:T(4,128)S(1)}, u32[]{:S(2)}, u32[]{:S(2)}) collective-permute-start(f32[8,4,1024]{2,1,0:T(4,128)S(1)} %get-tuple-element.45), channel_id=1, source_target_pairs={{0,4},{8,0},{16,8},{24,16},{28,24},{20,28},{12,20},{4,12},{1,5},{9... | collective-permute-start | bytes 393224 | tf_op jit(solution)/shard_map/ppermute | solution.py:510
  35.5 5.9 %collective-permute-start.18 = (f32[8,4,1024]{2,1,0:T(4,128)S(1)}, f32[8,4,1024]{2,1,0:T(4,128)S(1)}, u32[]{:S(2)}, u32[]{:S(2)}) collective-permute-start(f32[8,4,1024]{2,1,0:T(4,128)S(1)} %get-tuple-element.41), channel_id=1, source_target_pairs={{0,8},{8,16},{16,24},{24,28},{28,20},{20,12},{12,4},{4,0},{1,9},{9... | collective-permute-start | bytes 393224 | tf_op jit(solution)/shard_map/ppermute | solution.py:510
  38.0 7.0 %collective-permute-start.25 = (f32[8,4,1024]{2,1,0:T(4,128)S(1)}, f32[8,4,1024]{2,1,0:T(4,128)S(1)}, u32[]{:S(2)}, u32[]{:S(2)}) collective-permute-start(f32[8,4,1024]{2,1,0:T(4,128)S(1)} %get-tuple-element.43), channel_id=1, source_target_pairs={{0,4},{8,0},{16,8},{24,16},{28,24},{20,28},{12,20},{4,12},{1,5},{9... | collective-permute-start | bytes 393224 | tf_op jit(solution)/shard_map/ppermute | solution.py:510
  38.5 7.0 %collective-permute-start.22 = (f32[8,4,1024]{2,1,0:T(4,128)S(1)}, f32[8,4,1024]{2,1,0:T(4,128)S(1)}, u32[]{:S(2)}, u32[]{:S(2)}) collective-permute-start(f32[8,4,1024]{2,1,0:T(4,128)S(1)} %get-tuple-element.42), channel_id=1, source_target_pairs={{0,8},{8,16},{16,24},{24,28},{28,20},{20,12},{12,4},{4,0},{1,9},{9... | collective-permute-start | bytes 393224 | tf_op jit(solution)/shard_map/ppermute | solution.py:510
  41.0 6.3 %collective-permute-start.29 = (f32[8,4,1024]{2,1,0:T(4,128)S(1)}, f32[8,4,1024]{2,1,0:T(4,128)S(1)}, u32[]{:S(2)}, u32[]{:S(2)}) collective-permute-start(f32[8,4,1024]{2,1,0:T(4,128)S(1)} %join.3), channel_id=1, source_target_pairs={{0,4},{8,0},{16,8},{24,16},{28,24},{20,28},{12,20},{4,12},{1,5},{9... | collective-permute-start | bytes 393224 | tf_op jit(solution)/shard_map/ppermute | solution.py:510
  41.4 6.3 %collective-permute-start.19 = (f32[8,4,1024]{2,1,0:T(4,128)S(1)}, f32[8,4,1024]{2,1,0:T(4,128)S(1)}, u32[]{:S(2)}, u32[]{:S(2)}) collective-permute-start(f32[8,4,1024]{2,1,0:T(4,128)S(1)} %join.2), channel_id=1, source_target_pairs={{0,8},{8,16},{16,24},{24,28},{28,20},{20,12},{12,4},{4,0},{1,9},{9... | collective-permute-start | bytes 393224 | tf_op jit(solution)/shard_map/ppermute | solution.py:510
  45.1 6.1 %collective-permute-start.26 = (f32[8,4,1024]{2,1,0:T(4,128)S(1)}, f32[8,4,1024]{2,1,0:T(4,128)S(1)}, u32[]{:S(2)}, u32[]{:S(2)}) collective-permute-start(f32[8,4,1024]{2,1,0:T(4,128)S(1)} %add.12), channel_id=1, source_target_pairs={{0,4},{8,0},{16,8},{24,16},{28,24},{20,28},{12,20},{4,12},{1,5},{9... | collective-permute-start | bytes 393224 | tf_op jit(solution)/shard_map/ppermute | solution.py:510
  45.5 6.0 %collective-permute-start.23 = (f32[8,4,1024]{2,1,0:T(4,128)S(1)}, f32[8,4,1024]{2,1,0:T(4,128)S(1)}, u32[]{:S(2)}, u32[]{:S(2)}) collective-permute-start(f32[8,4,1024]{2,1,0:T(4,128)S(1)} %add.10), channel_id=1, source_target_pairs={{0,8},{8,16},{16,24},{24,28},{28,20},{20,12},{12,4},{4,0},{1,9},{9... | collective-permute-start | bytes 393224 | tf_op jit(solution)/shard_map/ppermute | solution.py:510
  47.3 6.8 %collective-permute-start.30 = (f32[8,4,1024]{2,1,0:T(4,128)S(1)}, f32[8,4,1024]{2,1,0:T(4,128)S(1)}, u32[]{:S(2)}, u32[]{:S(2)}) collective-permute-start(f32[8,4,1024]{2,1,0:T(4,128)S(1)} %add.14), channel_id=1, source_target_pairs={{0,4},{8,0},{16,8},{24,16},{28,24},{20,28},{12,20},{4,12},{1,5},{9... | collective-permute-start | bytes 393224 | tf_op jit(solution)/shard_map/ppermute | solution.py:510
  47.7 6.6 %collective-permute-start.20 = (f32[8,4,1024]{2,1,0:T(4,128)S(1)}, f32[8,4,1024]{2,1,0:T(4,128)S(1)}, u32[]{:S(2)}, u32[]{:S(2)}) collective-permute-start(f32[8,4,1024]{2,1,0:T(4,128)S(1)} %add.8), channel_id=1, source_target_pairs={{0,8},{8,16},{16,24},{24,28},{28,20},{20,12},{12,4},{4,0},{1,9},{9... | collective-permute-start | bytes 393224 | tf_op jit(solution)/shard_map/ppermute | solution.py:510
  51.2 6.2 %collective-permute-start.27 = (f32[8,4,1024]{2,1,0:T(4,128)S(1)}, f32[8,4,1024]{2,1,0:T(4,128)S(1)}, u32[]{:S(2)}, u32[]{:S(2)}) collective-permute-start(f32[8,4,1024]{2,1,0:T(4,128)S(1)} %add.13), channel_id=1, source_target_pairs={{0,4},{8,0},{16,8},{24,16},{28,24},{20,28},{12,20},{4,12},{1,5},{9... | collective-permute-start | bytes 393224 | tf_op jit(solution)/shard_map/ppermute | solution.py:510
  51.5 5.9 %collective-permute-start.24 = (f32[8,4,1024]{2,1,0:T(4,128)S(1)}, f32[8,4,1024]{2,1,0:T(4,128)S(1)}, u32[]{:S(2)}, u32[]{:S(2)}) collective-permute-start(f32[8,4,1024]{2,1,0:T(4,128)S(1)} %add.11), channel_id=1, source_target_pairs={{0,8},{8,16},{16,24},{24,28},{28,20},{20,12},{12,4},{4,0},{1,9},{9... | collective-permute-start | bytes 393224 | tf_op jit(solution)/shard_map/ppermute | solution.py:510
  54.0 5.0 %collective-permute-start.31 = (f32[8,4,1024]{2,1,0:T(4,128)S(1)}, f32[8,4,1024]{2,1,0:T(4,128)S(1)}, u32[]{:S(2)}, u32[]{:S(2)}) collective-permute-start(f32[8,4,1024]{2,1,0:T(4,128)S(1)} %add.15), channel_id=1, source_target_pairs={{0,4},{8,0},{16,8},{24,16},{28,24},{20,28},{12,20},{4,12},{1,5},{9... | collective-permute-start | bytes 393224 | tf_op jit(solution)/shard_map/ppermute | solution.py:510
  (9 other events, 53.0 us)

commit v7 on v6

--- a/solution.py
+++ b/solution.py
@@ -229,10 +229,6 @@
     return [n[3] - p[0], -p[1] - n[2], -p[2] - n[1], n[0] - p[3]]
 
 
-def on_core(core):
-    return lax.axis_index("order") % 2 == core
-
-
 def tables_kernel(legendre, tables, sems):
     copies = table_copies(legendre, tables, sems)
     for copy in copies:
@@ -362,7 +358,7 @@
                 lane // wide == k, pltpu.roll(pairs[start + k], k * wide, 1), value
             )
         packed.append(value)
-    observed = sky[...]
+    observed = sky[:count]
     for m in range(slots):
         total = jnp.where((lane < wide) & (lane % slots == m), observed, 0.0)
         for k, value in enumerate(packed):
@@ -393,14 +389,7 @@
         update_block(tables, m, first, an, ng, row8, (low_ref, high_ref)[half], at)
 
 
-def backward_kernel(core, tables, analysed_ref, *rest):
-    if core is None:
-        backward_blocks(tables, analysed_ref, rest[-1])
-    else:
-        pl.when(on_core(core))(lambda: backward_blocks(tables, analysed_ref, rest[-1]))
-
-
-def backward_blocks(tables, analysed_ref, out):
+def backward_kernel(tables, analysed_ref, out):
     slots, _, _, degrees = tables.shape
     blocks, _, _, width = out.shape
     stratum = degrees // slots
@@ -445,7 +434,7 @@
                 value = pltpu.roll(value, shift, 1) if shift else value
                 tile = jnp.where(lane // slots == k, value, tile)
             tiles.append(tile)
-        spread[a] = jnp.concatenate(tiles, axis=1) * factor
+        spread[a, :count] = jnp.concatenate(tiles, axis=1) * factor
     even = lax.broadcasted_iota(jnp.int32, (rows, both), 0) % 2 == 0
     for c in range(cycles):
         q_re, q_im, u_re, u_im = [spread[a, pl.ds(owner * cycles + c, 1)] for a in range(4)]
@@ -613,7 +602,7 @@
         out_shape=[half] * 2 + [whole],
         in_specs=[vmem()] * (3 + groups),
         out_specs=[vmem()] * 3,
-        scratch_shapes=[pltpu.VMEM((count, LANES), jnp.float32)],
+        scratch_shapes=[pltpu.VMEM((count + 8, LANES), jnp.float32)],
         compiler_params=pltpu.CompilerParams(vmem_limit_bytes=16 * MIB),
         cost_estimate=estimate(1),
         name="analysed",
@@ -625,29 +614,22 @@
             in_specs=[vmem()] * 2,
             out_specs=[vmem()] * 2,
             compiler_params=pltpu.CompilerParams(vmem_limit_bytes=16 * MIB),
-            cost_estimate=estimate(0.5),
+            cost_estimate=estimate(0.01),
             name="second",
         )(tables, analysed)
 
     second = nearer((-1, 1))
     third = nearer((1, -1))
 
-    def backward(core, *before):
-        return pl.pallas_call(
-            lambda *refs: backward_kernel(core, *refs),
-            out_shape=pltpu.VMEM((blocks, slots, 4, width), jnp.float32),
-            in_specs=[vmem()] * 2 + [hbm] * len(before),
-            out_specs=vmem(),
-            input_output_aliases={2: 0} if before else {},
-            compiler_params=pltpu.CompilerParams(vmem_limit_bytes=16 * MIB),
-            cost_estimate=estimate(2),
-            name="backward",
-        )(
-            tables, analysed,
-            *[pltpu.with_memory_space_constraint(value, pltpu.VMEM) for value in before],
-        )
-
-    piece = backward(None)
+    piece = pl.pallas_call(
+        backward_kernel,
+        out_shape=pltpu.VMEM((blocks, slots, 4, width), jnp.float32),
+        in_specs=[vmem()] * 2,
+        out_specs=vmem(),
+        compiler_params=pltpu.CompilerParams(vmem_limit_bytes=16 * MIB),
+        cost_estimate=estimate(2),
+        name="backward",
+    )(tables, analysed)
 
     def add(index, first, value):
         return pl.pallas_call(
@@ -696,7 +678,7 @@
         out_shape=shape(cycles, 2 * rows, LANES),
         in_specs=[vmem()] * (4 + 2 * groups),
         out_specs=vmem(),
-        scratch_shapes=[pltpu.VMEM((4, count, 2 * every), jnp.float32)],
+        scratch_shapes=[pltpu.VMEM((4, count + 8, 2 * every), jnp.float32)],
         compiler_params=pltpu.CompilerParams(vmem_limit_bytes=16 * MIB),
         cost_estimate=pl.CostEstimate(flops=10**8, bytes_accessed=2 * MIB, transcendentals=0),
         name="residual",

time: 60.4 us -> 60.4 us (level)
  no operation moved by 1% of the time
where the time goes in v7:
time: 60.4 us; the launch traced here: 60.2 us
  starting transfers between devices  32.2 us (53%)
  waiting for transfers between devices  13.9 us (23%)
  Pallas kernels  13.3 us (22%)
  between operations  0.79 us (1%)
    ppermute x26, starting transfers between devices, turn(): return lax.ppermute(value, 'blk', pairs)  28.2 us
    ppermute x26, waiting for transfers between devices, turn(): return lax.ppermute(value, 'blk', pairs)  11.3 us
    ppermute x6, starting transfers between devices, swap(): return lax.ppermute(value, axis, [(i, i ^ step) for i in range(size)])  4 us
    ppermute x6, waiting for transfers between devices, swap(): return lax.ppermute(value, axis, [(i, i ^ step) for i in range(size)])  2.58 us
    pallas_call x1, Pallas kernels, body(): pl.pallas_call(tables_kernel, out_shape=pltpu.VMEM(legendre.shape, jnp.fl...  2.31 us
    pallas_call x1, Pallas kernels, body(): pl.pallas_call(backward_kernel, out_shape=pltpu.VMEM((blocks, slots, 4, w...  1.92 us
    pallas_call x1, Pallas kernels, body(): pl.pallas_call(lambda *refs: sky_kernel(normalise, groups, slots, cycles,...  1.77 us
    pallas_call x1, Pallas kernels, body(): pl.pallas_call(lambda *refs: forward_kernel(steps, firsts, *refs), out_sh...  1.44 us
  transfers between devices with their start and end apart: 32, of which 15 were waited for; matrix products, arithmetic and copies ran while one was open for 0% of the time, Pallas kernels for 18%

profile of v7, /device:TPU:0, one launch (start us, length us, event | category | flops | bytes accessed | tf_op | source)
XLA Modules:
  0.0 60.2 jit_solution(2420884620495784402)
XLA Ops:
  0.6 3.1 %collective-permute-start = (f32[16,4,1024]{2,1,0:T(4,128)}, f32[16,4,1024]{2,1,0:T(4,128)S(1)}, u32[]{:S(2)}, u32[]{:S(2)}) collective-permute-start(f32[16,4,1024]{2,1,0:T(4,128)} %harmonics_ref.1), channel_id=1, source_target_pairs={{0,8},{8,16},{16,24},{24,28},{28,20},{20,12},{12,4},{4,0},{1,9},{9... | collective-permute-start | bytes 786440 | tf_op jit(solution)/shard_map/ppermute | solution.py:499
  4.6 2.0 %collective-permute-start.2 = (f32[1,128]{1,0:T(1,128)S(1)}, f32[1,128]{1,0:T(1,128)S(1)}, u32[]{:S(2)}, u32[]{:S(2)}) collective-permute-start(f32[1,128]{1,0:T(1,128)S(1)} %meta.1.refs_0_.meta_ref), channel_id=1, source_target_pairs={{0,2},{1,3},{2,0},{3,1},{4,6},{5,7},{6,4},{7,5},{8,10},{9,11},{10,... | collective-permute-start | bytes 1544 | tf_op jit(solution)/shard_map/ppermute | solution.py:493
  6.6 2.3 %tables.1.refs_1_.refs_0_ = f32[16,2,8,8192]{3,2,1,0:T(8,128)S(1)} custom-call(f32[16,2,8,8192]{3,2,1,0:T(8,128)} %legendre.1), custom_call_target="tpu_custom_call" | custom-call | bytes 4500000 | tf_op jit(solution)/shard_map/tables/pallas_call | solution.py:522
  10.2 1.8 %collective-permute-start.4 = (f32[8,4,1024]{2,1,0:T(4,128)S(1)}, f32[8,4,1024]{2,1,0:T(4,128)S(1)}, u32[]{:S(2)}, u32[]{:S(2)}) collective-permute-start(f32[8,4,1024]{2,1,0:T(4,128)S(1)} %get-tuple-element.53), channel_id=1, source_target_pairs={{0,8},{8,16},{16,24},{24,28},{28,20},{20,12},{12,4},{4,0},{1,9},{9... | collective-permute-start | bytes 393224 | tf_op jit(solution)/shard_map/ppermute | solution.py:499
  12.3 1.8 %collective-permute-start.6 = (f32[8,4,1024]{2,1,0:T(4,128)S(1)}, f32[8,4,1024]{2,1,0:T(4,128)S(1)}, u32[]{:S(2)}, u32[]{:S(2)}) collective-permute-start(f32[8,4,1024]{2,1,0:T(4,128)S(1)} %get-tuple-element.52), channel_id=1, source_target_pairs={{0,8},{8,16},{16,24},{24,28},{28,20},{20,12},{12,4},{4,0},{1,9},{9... | collective-permute-start | bytes 393224 | tf_op jit(solution)/shard_map/ppermute | solution.py:499
  14.4 1.8 %sky_analysis.1 = (f32[4,8,128]{2,1,0:T(8,128)S(1)}, f32[2,256,128]{2,1,0:T(8,128)S(1)}, f32[2,256,128]{2,1,0:T(8,128)S(1)}, f32[2,128,128]{2,1,0:T(8,128)S(1)}, f32[2,256,128]{2,1,0:T(8,128)S(1)}) custom-call(f32[1,128]{1,0:T(1,128)S(1)} %meta.1.refs_0_.meta_ref, f32[1,128]{1,0:T(1,128)S(1)} %collective-permute-done.1.refs_1_, ...), custom_call_target="tpu_custom_call" | custom-call | bytes 9000000 | tf_op jit(solution)/shard_map/sky_analysis/pallas_call | solution.py:538
  16.6 1.7 %collective-permute-start.9 = (f32[8,4,1024]{2,1,0:T(4,128)S(1)}, f32[8,4,1024]{2,1,0:T(4,128)S(1)}, u32[]{:S(2)}, u32[]{:S(2)}) collective-permute-start(f32[8,4,1024]{2,1,0:T(4,128)S(1)} %collective-permute-done.4.refs_5_), channel_id=1, source_target_pairs={{0,8},{8,16},{16,24},{24,28},{28,20},{20,12},{12,4},{4,0},{1,9},{9... | collective-permute-start | bytes 393224 | tf_op jit(solution)/shard_map/ppermute | solution.py:499
  19.0 1.6 %collective-permute-start.10 = (f32[8,4,1024]{2,1,0:T(4,128)S(1)}, f32[8,4,1024]{2,1,0:T(4,128)S(1)}, u32[]{:S(2)}, u32[]{:S(2)}) collective-permute-start(f32[8,4,1024]{2,1,0:T(4,128)S(1)} %collective-permute-done.6.refs_6_), channel_id=1, source_target_pairs={{0,8},{8,16},{16,24},{24,28},{28,20},{20,12},{12,4},{4,0},{1,9},{9... | collective-permute-start | bytes 393224 | tf_op jit(solution)/shard_map/ppermute | solution.py:499
  21.0 1.8 %collective-permute-done.9.refs_9_ = f32[8,4,1024]{2,1,0:T(4,128)S(1)} collective-permute-done((f32[8,4,1024]{2,1,0:T(4,128)S(1)}, f32[8,4,1024]{2,1,0:T(4,128)S(1)}, u32[]{:S(2)}, u32[]{:S(2)}) %collective-permute-start.9) | collective-permute-done | bytes 131104 | tf_op jit(solution)/shard_map/ppermute | solution.py:499
  22.8 1.4 %collective-permute-start.13 = (f32[8,4,1024]{2,1,0:T(4,128)S(1)}, f32[8,4,1024]{2,1,0:T(4,128)S(1)}, u32[]{:S(2)}, u32[]{:S(2)}) collective-permute-start(f32[8,4,1024]{2,1,0:T(4,128)S(1)} %collective-permute-done.9.refs_9_), channel_id=1, source_target_pairs={{0,8},{8,16},{16,24},{24,28},{28,20},{20,12},{12,4},{4,0},{1,9},{9... | collective-permute-start | bytes 393224 | tf_op jit(solution)/shard_map/ppermute | solution.py:499
  25.4 1.3 %collective-permute-done.11.refs_11_ = f32[8,4,1024]{2,1,0:T(4,128)S(1)} collective-permute-done((f32[8,4,1024]{2,1,0:T(4,128)S(1)}, f32[8,4,1024]{2,1,0:T(4,128)S(1)}, u32[]{:S(2)}, u32[]{:S(2)}) %collective-permute-start.11) | collective-permute-done | bytes 131104 | tf_op jit(solution)/shard_map/ppermute | solution.py:499
  26.7 1.4 %forward.1.refs_3_ = f32[16,4,8,128]{3,2,1,0:T(8,128)S(1)} custom-call(f32[1,128]{1,0:T(1,128)S(1)} %meta.1.refs_0_.meta_ref, f32[16,2,8,8192]{3,2,1,0:T(8,128)S(1)} %tables.1.refs_1_.refs_0_, f32[16,4,1024]{2,1,0:T(4,128)S(1)} %copy-done, f32[16,4,1024]{2,1,0:T(4,128)S(1)} %collective-permute-done.refs_3_, ...), custom_call_target="tpu_custom_call" | custom-call | bytes 6000000 | tf_op jit(solution)/shard_map/forward/pallas_call | solution.py:578
  32.3 1.4 %collective-permute-done.16.refs_5_.refs_10_ = f32[16,128]{1,0:T(8,128)S(1)} collective-permute-done((f32[16,128]{1,0:T(8,128)S(1)}, f32[16,128]{1,0:T(8,128)S(1)}, u32[]{:S(2)}, u32[]{:S(2)}) %collective-permute-start.16) | collective-permute-done | bytes 8224 | tf_op jit(solution)/shard_map/ppermute | solution.py:493
  35.5 1.6 %collective-permute-start.18 = (f32[8,4,1024]{2,1,0:T(4,128)S(1)}, f32[8,4,1024]{2,1,0:T(4,128)S(1)}, u32[]{:S(2)}, u32[]{:S(2)}) collective-permute-start(f32[8,4,1024]{2,1,0:T(4,128)S(1)} %get-tuple-element.41), channel_id=1, source_target_pairs={{0,8},{8,16},{16,24},{24,28},{28,20},{20,12},{12,4},{4,0},{1,9},{9... | collective-permute-start | bytes 393224 | tf_op jit(solution)/shard_map/ppermute | solution.py:499
  38.5 1.6 %collective-permute-start.22 = (f32[8,4,1024]{2,1,0:T(4,128)S(1)}, f32[8,4,1024]{2,1,0:T(4,128)S(1)}, u32[]{:S(2)}, u32[]{:S(2)}) collective-permute-start(f32[8,4,1024]{2,1,0:T(4,128)S(1)} %get-tuple-element.42), channel_id=1, source_target_pairs={{0,8},{8,16},{16,24},{24,28},{28,20},{20,12},{12,4},{4,0},{1,9},{9... | collective-permute-start | bytes 393224 | tf_op jit(solution)/shard_map/ppermute | solution.py:499
  41.4 1.7 %collective-permute-start.19 = (f32[8,4,1024]{2,1,0:T(4,128)S(1)}, f32[8,4,1024]{2,1,0:T(4,128)S(1)}, u32[]{:S(2)}, u32[]{:S(2)}) collective-permute-start(f32[8,4,1024]{2,1,0:T(4,128)S(1)} %join.2), channel_id=1, source_target_pairs={{0,8},{8,16},{16,24},{24,28},{28,20},{20,12},{12,4},{4,0},{1,9},{9... | collective-permute-start | bytes 393224 | tf_op jit(solution)/shard_map/ppermute | solution.py:499
  43.1 1.9 %backward.1.refs_0_.piece_ref = f32[8,16,4,1024]{3,2,1,0:T(4,128)S(1)} custom-call(f32[16,2,8,8192]{3,2,1,0:T(8,128)S(1)} %tables.1.refs_1_.refs_0_, f32[16,4,8,128]{3,2,1,0:T(8,128)S(1)} %get-tuple-element.39.analysed_ref.refs_1_), custom_call_target="tpu_custom_call" | custom-call | bytes 6000000 | tf_op jit(solution)/shard_map/backward/pallas_call | solution.py:624
  45.5 1.7 %collective-permute-start.23 = (f32[8,4,1024]{2,1,0:T(4,128)S(1)}, f32[8,4,1024]{2,1,0:T(4,128)S(1)}, u32[]{:S(2)}, u32[]{:S(2)}) collective-permute-start(f32[8,4,1024]{2,1,0:T(4,128)S(1)} %add.10), channel_id=1, source_target_pairs={{0,8},{8,16},{16,24},{24,28},{28,20},{20,12},{12,4},{4,0},{1,9},{9... | collective-permute-start | bytes 393224 | tf_op jit(solution)/shard_map/ppermute | solution.py:499
  47.7 1.7 %collective-permute-start.20 = (f32[8,4,1024]{2,1,0:T(4,128)S(1)}, f32[8,4,1024]{2,1,0:T(4,128)S(1)}, u32[]{:S(2)}, u32[]{:S(2)}) collective-permute-start(f32[8,4,1024]{2,1,0:T(4,128)S(1)} %add.8), channel_id=1, source_target_pairs={{0,8},{8,16},{16,24},{24,28},{28,20},{20,12},{12,4},{4,0},{1,9},{9... | collective-permute-start | bytes 393224 | tf_op jit(solution)/shard_map/ppermute | solution.py:499
  49.4 1.8 %collective-permute-done.26.refs_1_ = f32[8,4,1024]{2,1,0:T(4,128)S(1)} collective-permute-done((f32[8,4,1024]{2,1,0:T(4,128)S(1)}, f32[8,4,1024]{2,1,0:T(4,128)S(1)}, u32[]{:S(2)}, u32[]{:S(2)}) %collective-permute-start.26) | collective-permute-done | bytes 131104 | tf_op jit(solution)/shard_map/ppermute | solution.py:499
  51.5 1.8 %collective-permute-start.24 = (f32[8,4,1024]{2,1,0:T(4,128)S(1)}, f32[8,4,1024]{2,1,0:T(4,128)S(1)}, u32[]{:S(2)}, u32[]{:S(2)}) collective-permute-start(f32[8,4,1024]{2,1,0:T(4,128)S(1)} %add.11), channel_id=1, source_target_pairs={{0,8},{8,16},{16,24},{24,28},{28,20},{20,12},{12,4},{4,0},{1,9},{9... | collective-permute-start | bytes 393224 | tf_op jit(solution)/shard_map/ppermute | solution.py:499
  54.4 1.8 %collective-permute-start.21 = (f32[8,4,1024]{2,1,0:T(4,128)S(1)}, f32[8,4,1024]{2,1,0:T(4,128)S(1)}, u32[]{:S(2)}, u32[]{:S(2)}) collective-permute-start(f32[8,4,1024]{2,1,0:T(4,128)S(1)} %add.9), channel_id=1, source_target_pairs={{0,8},{8,16},{16,24},{24,28},{28,20},{20,12},{12,4},{4,0},{1,9},{9... | collective-permute-start | bytes 393224 | tf_op jit(solution)/shard_map/ppermute | solution.py:499
  56.2 1.2 %residual.1 = f32[2,256,128]{2,1,0:T(8,128)} custom-call(f32[1,128]{1,0:T(1,128)S(1)} %meta.1.refs_0_.meta_ref, f32[1,128]{1,0:T(1,128)S(1)} %collective-permute-done.1.refs_1_, f32[1,128]{1,0:T(1,128)S(1)} %collective-permute-done.2.refs_2_, f32[1,128]{1,0:T(1,128)S(1)} %collective-permute-done.3.refs_3_, f32[2,256,128]{2,1,0:T(8,128)S(1)} %get-tuple-element.46.refs_4_, ...), custom_call_target="tpu_custom_call" | custom-call | flops 100000000 | bytes 2097152 | tf_op jit(solution)/shard_map/residual/pallas_call | solution.py:676
  57.4 1.6 %collective-permute-done.31.rest_3_ = f32[8,4,1024]{2,1,0:T(4,128)S(1)} collective-permute-done((f32[8,4,1024]{2,1,0:T(4,128)S(1)}, f32[8,4,1024]{2,1,0:T(4,128)S(1)}, u32[]{:S(2)}, u32[]{:S(2)}) %collective-permute-start.31) | collective-permute-done | bytes 131104 | tf_op jit(solution)/shard_map/ppermute | solution.py:499
  (66 shorter events, 17.5 us)
Async XLA Ops:
  0.6 9.5 %collective-permute-start = (f32[16,4,1024]{2,1,0:T(4,128)}, f32[16,4,1024]{2,1,0:T(4,128)S(1)}, u32[]{:S(2)}, u32[]{:S(2)}) collective-permute-start(f32[16,4,1024]{2,1,0:T(4,128)} %harmonics_ref.1), channel_id=1, source_target_pairs={{0,8},{8,16},{16,24},{24,28},{28,20},{20,12},{12,4},{4,0},{1,9},{9... | collective-permute-start | bytes 786440 | tf_op jit(solution)/shard_map/ppermute | solution.py:499
  3.7 8.3 %collective-permute-start.5 = (f32[16,4,1024]{2,1,0:T(4,128)}, f32[16,4,1024]{2,1,0:T(4,128)S(1)}, u32[]{:S(2)}, u32[]{:S(2)}) collective-permute-start(f32[16,4,1024]{2,1,0:T(4,128)} %harmonics_ref.1), channel_id=1, source_target_pairs={{0,4},{8,0},{16,8},{24,16},{28,24},{20,28},{12,20},{4,12},{1,5},{9... | collective-permute-start | bytes 786440 | tf_op jit(solution)/shard_map/ppermute | solution.py:499
  10.2 6.4 %collective-permute-start.4 = (f32[8,4,1024]{2,1,0:T(4,128)S(1)}, f32[8,4,1024]{2,1,0:T(4,128)S(1)}, u32[]{:S(2)}, u32[]{:S(2)}) collective-permute-start(f32[8,4,1024]{2,1,0:T(4,128)S(1)} %get-tuple-element.53), channel_id=1, source_target_pairs={{0,8},{8,16},{16,24},{24,28},{28,20},{20,12},{12,4},{4,0},{1,9},{9... | collective-permute-start | bytes 393224 | tf_op jit(solution)/shard_map/ppermute | solution.py:499
  12.1 6.3 %collective-permute-start.8 = (f32[8,4,1024]{2,1,0:T(4,128)S(1)}, f32[8,4,1024]{2,1,0:T(4,128)S(1)}, u32[]{:S(2)}, u32[]{:S(2)}) collective-permute-start(f32[8,4,1024]{2,1,0:T(4,128)S(1)} %get-tuple-element.50), channel_id=1, source_target_pairs={{0,4},{8,0},{16,8},{24,16},{28,24},{20,28},{12,20},{4,12},{1,5},{9... | collective-permute-start | bytes 393224 | tf_op jit(solution)/shard_map/ppermute | solution.py:499
  12.3 6.6 %collective-permute-start.6 = (f32[8,4,1024]{2,1,0:T(4,128)S(1)}, f32[8,4,1024]{2,1,0:T(4,128)S(1)}, u32[]{:S(2)}, u32[]{:S(2)}) collective-permute-start(f32[8,4,1024]{2,1,0:T(4,128)S(1)} %get-tuple-element.52), channel_id=1, source_target_pairs={{0,8},{8,16},{16,24},{24,28},{28,20},{20,12},{12,4},{4,0},{1,9},{9... | collective-permute-start | bytes 393224 | tf_op jit(solution)/shard_map/ppermute | solution.py:499
  14.1 6.4 %collective-permute-start.7 = (f32[8,4,1024]{2,1,0:T(4,128)S(1)}, f32[8,4,1024]{2,1,0:T(4,128)S(1)}, u32[]{:S(2)}, u32[]{:S(2)}) collective-permute-start(f32[8,4,1024]{2,1,0:T(4,128)S(1)} %get-tuple-element.51), channel_id=1, source_target_pairs={{0,4},{8,0},{16,8},{24,16},{28,24},{20,28},{12,20},{4,12},{1,5},{9... | collective-permute-start | bytes 393224 | tf_op jit(solution)/shard_map/ppermute | solution.py:499
  16.6 6.1 %collective-permute-start.9 = (f32[8,4,1024]{2,1,0:T(4,128)S(1)}, f32[8,4,1024]{2,1,0:T(4,128)S(1)}, u32[]{:S(2)}, u32[]{:S(2)}) collective-permute-start(f32[8,4,1024]{2,1,0:T(4,128)S(1)} %collective-permute-done.4.refs_5_), channel_id=1, source_target_pairs={{0,8},{8,16},{16,24},{24,28},{28,20},{20,12},{12,4},{4,0},{1,9},{9... | collective-permute-start | bytes 393224 | tf_op jit(solution)/shard_map/ppermute | solution.py:499
  18.3 5.8 %collective-permute-start.12 = (f32[8,4,1024]{2,1,0:T(4,128)S(1)}, f32[8,4,1024]{2,1,0:T(4,128)S(1)}, u32[]{:S(2)}, u32[]{:S(2)}) collective-permute-start(f32[8,4,1024]{2,1,0:T(4,128)S(1)} %collective-permute-done.8.refs_8_), channel_id=1, source_target_pairs={{0,4},{8,0},{16,8},{24,16},{28,24},{20,28},{12,20},{4,12},{1,5},{9... | collective-permute-start | bytes 393224 | tf_op jit(solution)/shard_map/ppermute | solution.py:499
  19.0 6.5 %collective-permute-start.10 = (f32[8,4,1024]{2,1,0:T(4,128)S(1)}, f32[8,4,1024]{2,1,0:T(4,128)S(1)}, u32[]{:S(2)}, u32[]{:S(2)}) collective-permute-start(f32[8,4,1024]{2,1,0:T(4,128)S(1)} %collective-permute-done.6.refs_6_), channel_id=1, source_target_pairs={{0,8},{8,16},{16,24},{24,28},{28,20},{20,12},{12,4},{4,0},{1,9},{9... | collective-permute-start | bytes 393224 | tf_op jit(solution)/shard_map/ppermute | solution.py:499
  20.5 6.2 %collective-permute-start.11 = (f32[8,4,1024]{2,1,0:T(4,128)S(1)}, f32[8,4,1024]{2,1,0:T(4,128)S(1)}, u32[]{:S(2)}, u32[]{:S(2)}) collective-permute-start(f32[8,4,1024]{2,1,0:T(4,128)S(1)} %collective-permute-done.7.refs_7_), channel_id=1, source_target_pairs={{0,4},{8,0},{16,8},{24,16},{28,24},{20,28},{12,20},{4,12},{1,5},{9... | collective-permute-start | bytes 393224 | tf_op jit(solution)/shard_map/ppermute | solution.py:499
  22.8 5.4 %collective-permute-start.13 = (f32[8,4,1024]{2,1,0:T(4,128)S(1)}, f32[8,4,1024]{2,1,0:T(4,128)S(1)}, u32[]{:S(2)}, u32[]{:S(2)}) collective-permute-start(f32[8,4,1024]{2,1,0:T(4,128)S(1)} %collective-permute-done.9.refs_9_), channel_id=1, source_target_pairs={{0,8},{8,16},{16,24},{24,28},{28,20},{20,12},{12,4},{4,0},{1,9},{9... | collective-permute-start | bytes 393224 | tf_op jit(solution)/shard_map/ppermute | solution.py:499
  35.0 5.9 %collective-permute-start.28 = (f32[8,4,1024]{2,1,0:T(4,128)S(1)}, f32[8,4,1024]{2,1,0:T(4,128)S(1)}, u32[]{:S(2)}, u32[]{:S(2)}) collective-permute-start(f32[8,4,1024]{2,1,0:T(4,128)S(1)} %get-tuple-element.45), channel_id=1, source_target_pairs={{0,4},{8,0},{16,8},{24,16},{28,24},{20,28},{12,20},{4,12},{1,5},{9... | collective-permute-start | bytes 393224 | tf_op jit(solution)/shard_map/ppermute | solution.py:499
  35.5 5.9 %collective-permute-start.18 = (f32[8,4,1024]{2,1,0:T(4,128)S(1)}, f32[8,4,1024]{2,1,0:T(4,128)S(1)}, u32[]{:S(2)}, u32[]{:S(2)}) collective-permute-start(f32[8,4,1024]{2,1,0:T(4,128)S(1)} %get-tuple-element.41), channel_id=1, source_target_pairs={{0,8},{8,16},{16,24},{24,28},{28,20},{20,12},{12,4},{4,0},{1,9},{9... | collective-permute-start | bytes 393224 | tf_op jit(solution)/shard_map/ppermute | solution.py:499
  38.0 7.0 %collective-permute-start.25 = (f32[8,4,1024]{2,1,0:T(4,128)S(1)}, f32[8,4,1024]{2,1,0:T(4,128)S(1)}, u32[]{:S(2)}, u32[]{:S(2)}) collective-permute-start(f32[8,4,1024]{2,1,0:T(4,128)S(1)} %get-tuple-element.43), channel_id=1, source_target_pairs={{0,4},{8,0},{16,8},{24,16},{28,24},{20,28},{12,20},{4,12},{1,5},{9... | collective-permute-start | bytes 393224 | tf_op jit(solution)/shard_map/ppermute | solution.py:499
  38.5 7.0 %collective-permute-start.22 = (f32[8,4,1024]{2,1,0:T(4,128)S(1)}, f32[8,4,1024]{2,1,0:T(4,128)S(1)}, u32[]{:S(2)}, u32[]{:S(2)}) collective-permute-start(f32[8,4,1024]{2,1,0:T(4,128)S(1)} %get-tuple-element.42), channel_id=1, source_target_pairs={{0,8},{8,16},{16,24},{24,28},{28,20},{20,12},{12,4},{4,0},{1,9},{9... | collective-permute-start | bytes 393224 | tf_op jit(solution)/shard_map/ppermute | solution.py:499
  41.0 6.3 %collective-permute-start.29 = (f32[8,4,1024]{2,1,0:T(4,128)S(1)}, f32[8,4,1024]{2,1,0:T(4,128)S(1)}, u32[]{:S(2)}, u32[]{:S(2)}) collective-permute-start(f32[8,4,1024]{2,1,0:T(4,128)S(1)} %join.3), channel_id=1, source_target_pairs={{0,4},{8,0},{16,8},{24,16},{28,24},{20,28},{12,20},{4,12},{1,5},{9... | collective-permute-start | bytes 393224 | tf_op jit(solution)/shard_map/ppermute | solution.py:499
  41.4 6.3 %collective-permute-start.19 = (f32[8,4,1024]{2,1,0:T(4,128)S(1)}, f32[8,4,1024]{2,1,0:T(4,128)S(1)}, u32[]{:S(2)}, u32[]{:S(2)}) collective-permute-start(f32[8,4,1024]{2,1,0:T(4,128)S(1)} %join.2), channel_id=1, source_target_pairs={{0,8},{8,16},{16,24},{24,28},{28,20},{20,12},{12,4},{4,0},{1,9},{9... | collective-permute-start | bytes 393224 | tf_op jit(solution)/shard_map/ppermute | solution.py:499
  45.1 6.1 %collective-permute-start.26 = (f32[8,4,1024]{2,1,0:T(4,128)S(1)}, f32[8,4,1024]{2,1,0:T(4,128)S(1)}, u32[]{:S(2)}, u32[]{:S(2)}) collective-permute-start(f32[8,4,1024]{2,1,0:T(4,128)S(1)} %add.12), channel_id=1, source_target_pairs={{0,4},{8,0},{16,8},{24,16},{28,24},{20,28},{12,20},{4,12},{1,5},{9... | collective-permute-start | bytes 393224 | tf_op jit(solution)/shard_map/ppermute | solution.py:499
  45.5 6.0 %collective-permute-start.23 = (f32[8,4,1024]{2,1,0:T(4,128)S(1)}, f32[8,4,1024]{2,1,0:T(4,128)S(1)}, u32[]{:S(2)}, u32[]{:S(2)}) collective-permute-start(f32[8,4,1024]{2,1,0:T(4,128)S(1)} %add.10), channel_id=1, source_target_pairs={{0,8},{8,16},{16,24},{24,28},{28,20},{20,12},{12,4},{4,0},{1,9},{9... | collective-permute-start | bytes 393224 | tf_op jit(solution)/shard_map/ppermute | solution.py:499
  47.3 6.8 %collective-permute-start.30 = (f32[8,4,1024]{2,1,0:T(4,128)S(1)}, f32[8,4,1024]{2,1,0:T(4,128)S(1)}, u32[]{:S(2)}, u32[]{:S(2)}) collective-permute-start(f32[8,4,1024]{2,1,0:T(4,128)S(1)} %add.14), channel_id=1, source_target_pairs={{0,4},{8,0},{16,8},{24,16},{28,24},{20,28},{12,20},{4,12},{1,5},{9... | collective-permute-start | bytes 393224 | tf_op jit(solution)/shard_map/ppermute | solution.py:499
  47.7 6.6 %collective-permute-start.20 = (f32[8,4,1024]{2,1,0:T(4,128)S(1)}, f32[8,4,1024]{2,1,0:T(4,128)S(1)}, u32[]{:S(2)}, u32[]{:S(2)}) collective-permute-start(f32[8,4,1024]{2,1,0:T(4,128)S(1)} %add.8), channel_id=1, source_target_pairs={{0,8},{8,16},{16,24},{24,28},{28,20},{20,12},{12,4},{4,0},{1,9},{9... | collective-permute-start | bytes 393224 | tf_op jit(solution)/shard_map/ppermute | solution.py:499
  51.2 6.2 %collective-permute-start.27 = (f32[8,4,1024]{2,1,0:T(4,128)S(1)}, f32[8,4,1024]{2,1,0:T(4,128)S(1)}, u32[]{:S(2)}, u32[]{:S(2)}) collective-permute-start(f32[8,4,1024]{2,1,0:T(4,128)S(1)} %add.13), channel_id=1, source_target_pairs={{0,4},{8,0},{16,8},{24,16},{28,24},{20,28},{12,20},{4,12},{1,5},{9... | collective-permute-start | bytes 393224 | tf_op jit(solution)/shard_map/ppermute | solution.py:499
  51.5 5.9 %collective-permute-start.24 = (f32[8,4,1024]{2,1,0:T(4,128)S(1)}, f32[8,4,1024]{2,1,0:T(4,128)S(1)}, u32[]{:S(2)}, u32[]{:S(2)}) collective-permute-start(f32[8,4,1024]{2,1,0:T(4,128)S(1)} %add.11), channel_id=1, source_target_pairs={{0,8},{8,16},{16,24},{24,28},{28,20},{20,12},{12,4},{4,0},{1,9},{9... | collective-permute-start | bytes 393224 | tf_op jit(solution)/shard_map/ppermute | solution.py:499
  54.0 5.0 %collective-permute-start.31 = (f32[8,4,1024]{2,1,0:T(4,128)S(1)}, f32[8,4,1024]{2,1,0:T(4,128)S(1)}, u32[]{:S(2)}, u32[]{:S(2)}) collective-permute-start(f32[8,4,1024]{2,1,0:T(4,128)S(1)} %add.15), channel_id=1, source_target_pairs={{0,4},{8,0},{16,8},{24,16},{28,24},{20,28},{12,20},{4,12},{1,5},{9... | collective-permute-start | bytes 393224 | tf_op jit(solution)/shard_map/ppermute | solution.py:499
  (9 other events, 53.0 us)

commit v8 on v6

--- a/solution.py
+++ b/solution.py
@@ -468,17 +468,24 @@
 
 
 def final_kernel(meta_ref, harmonics_ref, piece_ref, *rest):
-    *received, out_ref = rest
-    slots, parts, width = out_ref.shape
+    *received, out, held, sems = rest
+    slots, parts, width = held.shape
     middle = slots // 2
     start = lax.axis_index("blk") * width
     degree = start + lax.broadcasted_iota(jnp.int32, (parts, width), 1)
     meta = meta_ref[...]
+    copies = []
     for m in range(slots):
         h, at = divmod(m, middle)
         update = piece_ref[0, m] + (received[h][at] + received[2 + h][at])
         valid = degree >= jnp.maximum(entry(meta, m).astype(jnp.int32), 2)
-        out_ref[m] = jnp.where(valid, harmonics_ref[m] + update, 0.0)
+        held[m] = jnp.where(valid, harmonics_ref[m] + update, 0.0)
+        if at == middle - 1:
+            span = pl.ds(h * middle, middle)
+            copies.append(pltpu.make_async_copy(held.at[span], out.at[span], sems.at[h]))
+            copies[-1].start()
+    for copy in copies:
+        copy.wait()
 
 
 def vmem():
@@ -682,7 +689,11 @@
         final_kernel,
         out_shape=shape(*harmonics.shape),
         in_specs=[vmem()] * 7,
-        out_specs=vmem(),
+        out_specs=hbm,
+        scratch_shapes=[
+            pltpu.VMEM(harmonics.shape, jnp.float32),
+            pltpu.SemaphoreType.DMA((2,)),
+        ],
         compiler_params=pltpu.CompilerParams(vmem_limit_bytes=8 * MIB),
         cost_estimate=pl.CostEstimate(flops=10**5, bytes_accessed=10**6, transcendentals=0),
         name="refine",

time: 60.4 us -> 60.4 us (level)
  no operation moved by 1% of the time
where the time goes in v8:
time: 60.4 us; the launch traced here: 60.2 us
  starting transfers between devices  32.2 us (53%)
  waiting for transfers between devices  13.9 us (23%)
  Pallas kernels  13.3 us (22%)
  between operations  0.79 us (1%)
    ppermute x26, starting transfers between devices, turn(): return lax.ppermute(value, 'blk', pairs)  28.2 us
    ppermute x26, waiting for transfers between devices, turn(): return lax.ppermute(value, 'blk', pairs)  11.3 us
    ppermute x6, starting transfers between devices, swap(): return lax.ppermute(value, axis, [(i, i ^ step) for i in range(size)])  4 us
    ppermute x6, waiting for transfers between devices, swap(): return lax.ppermute(value, axis, [(i, i ^ step) for i in range(size)])  2.58 us
    pallas_call x1, Pallas kernels, body(): pl.pallas_call(tables_kernel, out_shape=pltpu.VMEM(legendre.shape, jnp.fl...  2.31 us
    pallas_call x1, Pallas kernels, backward(): pl.pallas_call(lambda *refs: backward_kernel(core, *refs), out_shape=pltp...  1.92 us
    pallas_call x1, Pallas kernels, body(): pl.pallas_call(lambda *refs: sky_kernel(normalise, groups, slots, cycles,...  1.77 us
    pallas_call x1, Pallas kernels, body(): pl.pallas_call(lambda *refs: forward_kernel(steps, firsts, *refs), out_sh...  1.44 us
  transfers between devices with their start and end apart: 32, of which 15 were waited for; matrix products, arithmetic and copies ran while one was open for 0% of the time, Pallas kernels for 18%

profile of v8, /device:TPU:0, one launch (start us, length us, event | category | flops | bytes accessed | tf_op | source)
XLA Modules:
  0.0 60.2 jit_solution(7070282196470891063)
XLA Ops:
  0.6 3.1 %collective-permute-start = (f32[16,4,1024]{2,1,0:T(4,128)}, f32[16,4,1024]{2,1,0:T(4,128)S(1)}, u32[]{:S(2)}, u32[]{:S(2)}) collective-permute-start(f32[16,4,1024]{2,1,0:T(4,128)} %harmonics_ref.1), channel_id=1, source_target_pairs={{0,8},{8,16},{16,24},{24,28},{28,20},{20,12},{12,4},{4,0},{1,9},{9... | collective-permute-start | bytes 786440 | tf_op jit(solution)/shard_map/ppermute | solution.py:517
  4.6 2.0 %collective-permute-start.2 = (f32[1,128]{1,0:T(1,128)S(1)}, f32[1,128]{1,0:T(1,128)S(1)}, u32[]{:S(2)}, u32[]{:S(2)}) collective-permute-start(f32[1,128]{1,0:T(1,128)S(1)} %meta.1.refs_0_.meta_ref), channel_id=1, source_target_pairs={{0,2},{1,3},{2,0},{3,1},{4,6},{5,7},{6,4},{7,5},{8,10},{9,11},{10,... | collective-permute-start | bytes 1544 | tf_op jit(solution)/shard_map/ppermute | solution.py:511
  6.6 2.3 %tables.1.refs_1_.refs_0_ = f32[16,2,8,8192]{3,2,1,0:T(8,128)S(1)} custom-call(f32[16,2,8,8192]{3,2,1,0:T(8,128)} %legendre.1), custom_call_target="tpu_custom_call" | custom-call | bytes 4500000 | tf_op jit(solution)/shard_map/tables/pallas_call | solution.py:540
  10.2 1.8 %collective-permute-start.4 = (f32[8,4,1024]{2,1,0:T(4,128)S(1)}, f32[8,4,1024]{2,1,0:T(4,128)S(1)}, u32[]{:S(2)}, u32[]{:S(2)}) collective-permute-start(f32[8,4,1024]{2,1,0:T(4,128)S(1)} %get-tuple-element.53), channel_id=1, source_target_pairs={{0,8},{8,16},{16,24},{24,28},{28,20},{20,12},{12,4},{4,0},{1,9},{9... | collective-permute-start | bytes 393224 | tf_op jit(solution)/shard_map/ppermute | solution.py:517
  12.3 1.8 %collective-permute-start.6 = (f32[8,4,1024]{2,1,0:T(4,128)S(1)}, f32[8,4,1024]{2,1,0:T(4,128)S(1)}, u32[]{:S(2)}, u32[]{:S(2)}) collective-permute-start(f32[8,4,1024]{2,1,0:T(4,128)S(1)} %get-tuple-element.52), channel_id=1, source_target_pairs={{0,8},{8,16},{16,24},{24,28},{28,20},{20,12},{12,4},{4,0},{1,9},{9... | collective-permute-start | bytes 393224 | tf_op jit(solution)/shard_map/ppermute | solution.py:517
  14.4 1.8 %sky_analysis.1 = (f32[4,8,128]{2,1,0:T(8,128)S(1)}, f32[2,256,128]{2,1,0:T(8,128)S(1)}, f32[2,256,128]{2,1,0:T(8,128)S(1)}, f32[2,128,128]{2,1,0:T(8,128)S(1)}, f32[2,256,128]{2,1,0:T(8,128)S(1)}) custom-call(f32[1,128]{1,0:T(1,128)S(1)} %meta.1.refs_0_.meta_ref, f32[1,128]{1,0:T(1,128)S(1)} %collective-permute-done.1.refs_1_, ...), custom_call_target="tpu_custom_call" | custom-call | bytes 9000000 | tf_op jit(solution)/shard_map/sky_analysis/pallas_call | solution.py:556
  16.6 1.7 %collective-permute-start.9 = (f32[8,4,1024]{2,1,0:T(4,128)S(1)}, f32[8,4,1024]{2,1,0:T(4,128)S(1)}, u32[]{:S(2)}, u32[]{:S(2)}) collective-permute-start(f32[8,4,1024]{2,1,0:T(4,128)S(1)} %collective-permute-done.4.refs_5_), channel_id=1, source_target_pairs={{0,8},{8,16},{16,24},{24,28},{28,20},{20,12},{12,4},{4,0},{1,9},{9... | collective-permute-start | bytes 393224 | tf_op jit(solution)/shard_map/ppermute | solution.py:517
  19.0 1.6 %collective-permute-start.10 = (f32[8,4,1024]{2,1,0:T(4,128)S(1)}, f32[8,4,1024]{2,1,0:T(4,128)S(1)}, u32[]{:S(2)}, u32[]{:S(2)}) collective-permute-start(f32[8,4,1024]{2,1,0:T(4,128)S(1)} %collective-permute-done.6.refs_6_), channel_id=1, source_target_pairs={{0,8},{8,16},{16,24},{24,28},{28,20},{20,12},{12,4},{4,0},{1,9},{9... | collective-permute-start | bytes 393224 | tf_op jit(solution)/shard_map/ppermute | solution.py:517
  21.0 1.8 %collective-permute-done.9.refs_9_ = f32[8,4,1024]{2,1,0:T(4,128)S(1)} collective-permute-done((f32[8,4,1024]{2,1,0:T(4,128)S(1)}, f32[8,4,1024]{2,1,0:T(4,128)S(1)}, u32[]{:S(2)}, u32[]{:S(2)}) %collective-permute-start.9) | collective-permute-done | bytes 131104 | tf_op jit(solution)/shard_map/ppermute | solution.py:517
  22.8 1.4 %collective-permute-start.13 = (f32[8,4,1024]{2,1,0:T(4,128)S(1)}, f32[8,4,1024]{2,1,0:T(4,128)S(1)}, u32[]{:S(2)}, u32[]{:S(2)}) collective-permute-start(f32[8,4,1024]{2,1,0:T(4,128)S(1)} %collective-permute-done.9.refs_9_), channel_id=1, source_target_pairs={{0,8},{8,16},{16,24},{24,28},{28,20},{20,12},{12,4},{4,0},{1,9},{9... | collective-permute-start | bytes 393224 | tf_op jit(solution)/shard_map/ppermute | solution.py:517
  25.4 1.3 %collective-permute-done.11.refs_11_ = f32[8,4,1024]{2,1,0:T(4,128)S(1)} collective-permute-done((f32[8,4,1024]{2,1,0:T(4,128)S(1)}, f32[8,4,1024]{2,1,0:T(4,128)S(1)}, u32[]{:S(2)}, u32[]{:S(2)}) %collective-permute-start.11) | collective-permute-done | bytes 131104 | tf_op jit(solution)/shard_map/ppermute | solution.py:517
  26.7 1.4 %forward.1.refs_3_ = f32[16,4,8,128]{3,2,1,0:T(8,128)S(1)} custom-call(f32[1,128]{1,0:T(1,128)S(1)} %meta.1.refs_0_.meta_ref, f32[16,2,8,8192]{3,2,1,0:T(8,128)S(1)} %tables.1.refs_1_.refs_0_, f32[16,4,1024]{2,1,0:T(4,128)S(1)} %copy-done, f32[16,4,1024]{2,1,0:T(4,128)S(1)} %collective-permute-done.refs_3_, ...), custom_call_target="tpu_custom_call" | custom-call | bytes 6000000 | tf_op jit(solution)/shard_map/forward/pallas_call | solution.py:596
  32.3 1.4 %collective-permute-done.16.refs_5_.refs_10_ = f32[16,128]{1,0:T(8,128)S(1)} collective-permute-done((f32[16,128]{1,0:T(8,128)S(1)}, f32[16,128]{1,0:T(8,128)S(1)}, u32[]{:S(2)}, u32[]{:S(2)}) %collective-permute-start.16) | collective-permute-done | bytes 8224 | tf_op jit(solution)/shard_map/ppermute | solution.py:511
  35.5 1.6 %collective-permute-start.18 = (f32[8,4,1024]{2,1,0:T(4,128)S(1)}, f32[8,4,1024]{2,1,0:T(4,128)S(1)}, u32[]{:S(2)}, u32[]{:S(2)}) collective-permute-start(f32[8,4,1024]{2,1,0:T(4,128)S(1)} %get-tuple-element.41), channel_id=1, source_target_pairs={{0,8},{8,16},{16,24},{24,28},{28,20},{20,12},{12,4},{4,0},{1,9},{9... | collective-permute-start | bytes 393224 | tf_op jit(solution)/shard_map/ppermute | solution.py:517
  38.5 1.6 %collective-permute-start.22 = (f32[8,4,1024]{2,1,0:T(4,128)S(1)}, f32[8,4,1024]{2,1,0:T(4,128)S(1)}, u32[]{:S(2)}, u32[]{:S(2)}) collective-permute-start(f32[8,4,1024]{2,1,0:T(4,128)S(1)} %get-tuple-element.42), channel_id=1, source_target_pairs={{0,8},{8,16},{16,24},{24,28},{28,20},{20,12},{12,4},{4,0},{1,9},{9... | collective-permute-start | bytes 393224 | tf_op jit(solution)/shard_map/ppermute | solution.py:517
  41.4 1.7 %collective-permute-start.19 = (f32[8,4,1024]{2,1,0:T(4,128)S(1)}, f32[8,4,1024]{2,1,0:T(4,128)S(1)}, u32[]{:S(2)}, u32[]{:S(2)}) collective-permute-start(f32[8,4,1024]{2,1,0:T(4,128)S(1)} %join.2), channel_id=1, source_target_pairs={{0,8},{8,16},{16,24},{24,28},{28,20},{20,12},{12,4},{4,0},{1,9},{9... | collective-permute-start | bytes 393224 | tf_op jit(solution)/shard_map/ppermute | solution.py:517
  43.1 1.9 %backward.1.refs_0_.piece_ref = f32[8,16,4,1024]{3,2,1,0:T(4,128)S(1)} custom-call(f32[16,2,8,8192]{3,2,1,0:T(8,128)S(1)} %tables.1.refs_1_.refs_0_, f32[16,4,8,128]{3,2,1,0:T(8,128)S(1)} %get-tuple-element.39.refs_1_), custom_call_target="tpu_custom_call" | custom-call | bytes 6000000 | tf_op jit(solution)/shard_map/backward/pallas_call | solution.py:643
  45.5 1.7 %collective-permute-start.23 = (f32[8,4,1024]{2,1,0:T(4,128)S(1)}, f32[8,4,1024]{2,1,0:T(4,128)S(1)}, u32[]{:S(2)}, u32[]{:S(2)}) collective-permute-start(f32[8,4,1024]{2,1,0:T(4,128)S(1)} %add.10), channel_id=1, source_target_pairs={{0,8},{8,16},{16,24},{24,28},{28,20},{20,12},{12,4},{4,0},{1,9},{9... | collective-permute-start | bytes 393224 | tf_op jit(solution)/shard_map/ppermute | solution.py:517
  47.7 1.7 %collective-permute-start.20 = (f32[8,4,1024]{2,1,0:T(4,128)S(1)}, f32[8,4,1024]{2,1,0:T(4,128)S(1)}, u32[]{:S(2)}, u32[]{:S(2)}) collective-permute-start(f32[8,4,1024]{2,1,0:T(4,128)S(1)} %add.8), channel_id=1, source_target_pairs={{0,8},{8,16},{16,24},{24,28},{28,20},{20,12},{12,4},{4,0},{1,9},{9... | collective-permute-start | bytes 393224 | tf_op jit(solution)/shard_map/ppermute | solution.py:517
  49.4 1.8 %collective-permute-done.26.refs_1_ = f32[8,4,1024]{2,1,0:T(4,128)S(1)} collective-permute-done((f32[8,4,1024]{2,1,0:T(4,128)S(1)}, f32[8,4,1024]{2,1,0:T(4,128)S(1)}, u32[]{:S(2)}, u32[]{:S(2)}) %collective-permute-start.26) | collective-permute-done | bytes 131104 | tf_op jit(solution)/shard_map/ppermute | solution.py:517
  51.5 1.8 %collective-permute-start.24 = (f32[8,4,1024]{2,1,0:T(4,128)S(1)}, f32[8,4,1024]{2,1,0:T(4,128)S(1)}, u32[]{:S(2)}, u32[]{:S(2)}) collective-permute-start(f32[8,4,1024]{2,1,0:T(4,128)S(1)} %add.11), channel_id=1, source_target_pairs={{0,8},{8,16},{16,24},{24,28},{28,20},{20,12},{12,4},{4,0},{1,9},{9... | collective-permute-start | bytes 393224 | tf_op jit(solution)/shard_map/ppermute | solution.py:517
  54.3 1.8 %collective-permute-start.21 = (f32[8,4,1024]{2,1,0:T(4,128)S(1)}, f32[8,4,1024]{2,1,0:T(4,128)S(1)}, u32[]{:S(2)}, u32[]{:S(2)}) collective-permute-start(f32[8,4,1024]{2,1,0:T(4,128)S(1)} %add.9), channel_id=1, source_target_pairs={{0,8},{8,16},{16,24},{24,28},{28,20},{20,12},{12,4},{4,0},{1,9},{9... | collective-permute-start | bytes 393224 | tf_op jit(solution)/shard_map/ppermute | solution.py:517
  56.2 1.2 %residual.1 = f32[2,256,128]{2,1,0:T(8,128)} custom-call(f32[1,128]{1,0:T(1,128)S(1)} %meta.1.refs_0_.meta_ref, f32[1,128]{1,0:T(1,128)S(1)} %collective-permute-done.1.refs_1_, f32[1,128]{1,0:T(1,128)S(1)} %collective-permute-done.2.refs_2_, f32[1,128]{1,0:T(1,128)S(1)} %collective-permute-done.3.refs_3_, f32[2,256,128]{2,1,0:T(8,128)S(1)} %get-tuple-element.46.refs_4_, ...), custom_call_target="tpu_custom_call" | custom-call | flops 100000000 | bytes 2097152 | tf_op jit(solution)/shard_map/residual/pallas_call | solution.py:705
  57.4 1.6 %collective-permute-done.31.rest_3_ = f32[8,4,1024]{2,1,0:T(4,128)S(1)} collective-permute-done((f32[8,4,1024]{2,1,0:T(4,128)S(1)}, f32[8,4,1024]{2,1,0:T(4,128)S(1)}, u32[]{:S(2)}, u32[]{:S(2)}) %collective-permute-start.31) | collective-permute-done | bytes 131104 | tf_op jit(solution)/shard_map/ppermute | solution.py:517
  (66 shorter events, 17.5 us)
Async XLA Ops:
  0.6 9.5 %collective-permute-start = (f32[16,4,1024]{2,1,0:T(4,128)}, f32[16,4,1024]{2,1,0:T(4,128)S(1)}, u32[]{:S(2)}, u32[]{:S(2)}) collective-permute-start(f32[16,4,1024]{2,1,0:T(4,128)} %harmonics_ref.1), channel_id=1, source_target_pairs={{0,8},{8,16},{16,24},{24,28},{28,20},{20,12},{12,4},{4,0},{1,9},{9... | collective-permute-start | bytes 786440 | tf_op jit(solution)/shard_map/ppermute | solution.py:517
  3.7 8.3 %collective-permute-start.5 = (f32[16,4,1024]{2,1,0:T(4,128)}, f32[16,4,1024]{2,1,0:T(4,128)S(1)}, u32[]{:S(2)}, u32[]{:S(2)}) collective-permute-start(f32[16,4,1024]{2,1,0:T(4,128)} %harmonics_ref.1), channel_id=1, source_target_pairs={{0,4},{8,0},{16,8},{24,16},{28,24},{20,28},{12,20},{4,12},{1,5},{9... | collective-permute-start | bytes 786440 | tf_op jit(solution)/shard_map/ppermute | solution.py:517
  10.2 6.4 %collective-permute-start.4 = (f32[8,4,1024]{2,1,0:T(4,128)S(1)}, f32[8,4,1024]{2,1,0:T(4,128)S(1)}, u32[]{:S(2)}, u32[]{:S(2)}) collective-permute-start(f32[8,4,1024]{2,1,0:T(4,128)S(1)} %get-tuple-element.53), channel_id=1, source_target_pairs={{0,8},{8,16},{16,24},{24,28},{28,20},{20,12},{12,4},{4,0},{1,9},{9... | collective-permute-start | bytes 393224 | tf_op jit(solution)/shard_map/ppermute | solution.py:517
  12.1 6.3 %collective-permute-start.8 = (f32[8,4,1024]{2,1,0:T(4,128)S(1)}, f32[8,4,1024]{2,1,0:T(4,128)S(1)}, u32[]{:S(2)}, u32[]{:S(2)}) collective-permute-start(f32[8,4,1024]{2,1,0:T(4,128)S(1)} %get-tuple-element.50), channel_id=1, source_target_pairs={{0,4},{8,0},{16,8},{24,16},{28,24},{20,28},{12,20},{4,12},{1,5},{9... | collective-permute-start | bytes 393224 | tf_op jit(solution)/shard_map/ppermute | solution.py:517
  12.3 6.6 %collective-permute-start.6 = (f32[8,4,1024]{2,1,0:T(4,128)S(1)}, f32[8,4,1024]{2,1,0:T(4,128)S(1)}, u32[]{:S(2)}, u32[]{:S(2)}) collective-permute-start(f32[8,4,1024]{2,1,0:T(4,128)S(1)} %get-tuple-element.52), channel_id=1, source_target_pairs={{0,8},{8,16},{16,24},{24,28},{28,20},{20,12},{12,4},{4,0},{1,9},{9... | collective-permute-start | bytes 393224 | tf_op jit(solution)/shard_map/ppermute | solution.py:517
  14.1 6.4 %collective-permute-start.7 = (f32[8,4,1024]{2,1,0:T(4,128)S(1)}, f32[8,4,1024]{2,1,0:T(4,128)S(1)}, u32[]{:S(2)}, u32[]{:S(2)}) collective-permute-start(f32[8,4,1024]{2,1,0:T(4,128)S(1)} %get-tuple-element.51), channel_id=1, source_target_pairs={{0,4},{8,0},{16,8},{24,16},{28,24},{20,28},{12,20},{4,12},{1,5},{9... | collective-permute-start | bytes 393224 | tf_op jit(solution)/shard_map/ppermute | solution.py:517
  16.6 6.1 %collective-permute-start.9 = (f32[8,4,1024]{2,1,0:T(4,128)S(1)}, f32[8,4,1024]{2,1,0:T(4,128)S(1)}, u32[]{:S(2)}, u32[]{:S(2)}) collective-permute-start(f32[8,4,1024]{2,1,0:T(4,128)S(1)} %collective-permute-done.4.refs_5_), channel_id=1, source_target_pairs={{0,8},{8,16},{16,24},{24,28},{28,20},{20,12},{12,4},{4,0},{1,9},{9... | collective-permute-start | bytes 393224 | tf_op jit(solution)/shard_map/ppermute | solution.py:517
  18.3 5.8 %collective-permute-start.12 = (f32[8,4,1024]{2,1,0:T(4,128)S(1)}, f32[8,4,1024]{2,1,0:T(4,128)S(1)}, u32[]{:S(2)}, u32[]{:S(2)}) collective-permute-start(f32[8,4,1024]{2,1,0:T(4,128)S(1)} %collective-permute-done.8.refs_8_), channel_id=1, source_target_pairs={{0,4},{8,0},{16,8},{24,16},{28,24},{20,28},{12,20},{4,12},{1,5},{9... | collective-permute-start | bytes 393224 | tf_op jit(solution)/shard_map/ppermute | solution.py:517
  19.0 6.5 %collective-permute-start.10 = (f32[8,4,1024]{2,1,0:T(4,128)S(1)}, f32[8,4,1024]{2,1,0:T(4,128)S(1)}, u32[]{:S(2)}, u32[]{:S(2)}) collective-permute-start(f32[8,4,1024]{2,1,0:T(4,128)S(1)} %collective-permute-done.6.refs_6_), channel_id=1, source_target_pairs={{0,8},{8,16},{16,24},{24,28},{28,20},{20,12},{12,4},{4,0},{1,9},{9... | collective-permute-start | bytes 393224 | tf_op jit(solution)/shard_map/ppermute | solution.py:517
  20.5 6.2 %collective-permute-start.11 = (f32[8,4,1024]{2,1,0:T(4,128)S(1)}, f32[8,4,1024]{2,1,0:T(4,128)S(1)}, u32[]{:S(2)}, u32[]{:S(2)}) collective-permute-start(f32[8,4,1024]{2,1,0:T(4,128)S(1)} %collective-permute-done.7.refs_7_), channel_id=1, source_target_pairs={{0,4},{8,0},{16,8},{24,16},{28,24},{20,28},{12,20},{4,12},{1,5},{9... | collective-permute-start | bytes 393224 | tf_op jit(solution)/shard_map/ppermute | solution.py:517
  22.8 5.4 %collective-permute-start.13 = (f32[8,4,1024]{2,1,0:T(4,128)S(1)}, f32[8,4,1024]{2,1,0:T(4,128)S(1)}, u32[]{:S(2)}, u32[]{:S(2)}) collective-permute-start(f32[8,4,1024]{2,1,0:T(4,128)S(1)} %collective-permute-done.9.refs_9_), channel_id=1, source_target_pairs={{0,8},{8,16},{16,24},{24,28},{28,20},{20,12},{12,4},{4,0},{1,9},{9... | collective-permute-start | bytes 393224 | tf_op jit(solution)/shard_map/ppermute | solution.py:517
  35.0 5.9 %collective-permute-start.28 = (f32[8,4,1024]{2,1,0:T(4,128)S(1)}, f32[8,4,1024]{2,1,0:T(4,128)S(1)}, u32[]{:S(2)}, u32[]{:S(2)}) collective-permute-start(f32[8,4,1024]{2,1,0:T(4,128)S(1)} %get-tuple-element.45), channel_id=1, source_target_pairs={{0,4},{8,0},{16,8},{24,16},{28,24},{20,28},{12,20},{4,12},{1,5},{9... | collective-permute-start | bytes 393224 | tf_op jit(solution)/shard_map/ppermute | solution.py:517
  35.5 5.9 %collective-permute-start.18 = (f32[8,4,1024]{2,1,0:T(4,128)S(1)}, f32[8,4,1024]{2,1,0:T(4,128)S(1)}, u32[]{:S(2)}, u32[]{:S(2)}) collective-permute-start(f32[8,4,1024]{2,1,0:T(4,128)S(1)} %get-tuple-element.41), channel_id=1, source_target_pairs={{0,8},{8,16},{16,24},{24,28},{28,20},{20,12},{12,4},{4,0},{1,9},{9... | collective-permute-start | bytes 393224 | tf_op jit(solution)/shard_map/ppermute | solution.py:517
  38.0 7.0 %collective-permute-start.25 = (f32[8,4,1024]{2,1,0:T(4,128)S(1)}, f32[8,4,1024]{2,1,0:T(4,128)S(1)}, u32[]{:S(2)}, u32[]{:S(2)}) collective-permute-start(f32[8,4,1024]{2,1,0:T(4,128)S(1)} %get-tuple-element.43), channel_id=1, source_target_pairs={{0,4},{8,0},{16,8},{24,16},{28,24},{20,28},{12,20},{4,12},{1,5},{9... | collective-permute-start | bytes 393224 | tf_op jit(solution)/shard_map/ppermute | solution.py:517
  38.5 7.0 %collective-permute-start.22 = (f32[8,4,1024]{2,1,0:T(4,128)S(1)}, f32[8,4,1024]{2,1,0:T(4,128)S(1)}, u32[]{:S(2)}, u32[]{:S(2)}) collective-permute-start(f32[8,4,1024]{2,1,0:T(4,128)S(1)} %get-tuple-element.42), channel_id=1, source_target_pairs={{0,8},{8,16},{16,24},{24,28},{28,20},{20,12},{12,4},{4,0},{1,9},{9... | collective-permute-start | bytes 393224 | tf_op jit(solution)/shard_map/ppermute | solution.py:517
  41.0 6.3 %collective-permute-start.29 = (f32[8,4,1024]{2,1,0:T(4,128)S(1)}, f32[8,4,1024]{2,1,0:T(4,128)S(1)}, u32[]{:S(2)}, u32[]{:S(2)}) collective-permute-start(f32[8,4,1024]{2,1,0:T(4,128)S(1)} %join.3), channel_id=1, source_target_pairs={{0,4},{8,0},{16,8},{24,16},{28,24},{20,28},{12,20},{4,12},{1,5},{9... | collective-permute-start | bytes 393224 | tf_op jit(solution)/shard_map/ppermute | solution.py:517
  41.4 6.3 %collective-permute-start.19 = (f32[8,4,1024]{2,1,0:T(4,128)S(1)}, f32[8,4,1024]{2,1,0:T(4,128)S(1)}, u32[]{:S(2)}, u32[]{:S(2)}) collective-permute-start(f32[8,4,1024]{2,1,0:T(4,128)S(1)} %join.2), channel_id=1, source_target_pairs={{0,8},{8,16},{16,24},{24,28},{28,20},{20,12},{12,4},{4,0},{1,9},{9... | collective-permute-start | bytes 393224 | tf_op jit(solution)/shard_map/ppermute | solution.py:517
  45.1 6.1 %collective-permute-start.26 = (f32[8,4,1024]{2,1,0:T(4,128)S(1)}, f32[8,4,1024]{2,1,0:T(4,128)S(1)}, u32[]{:S(2)}, u32[]{:S(2)}) collective-permute-start(f32[8,4,1024]{2,1,0:T(4,128)S(1)} %add.12), channel_id=1, source_target_pairs={{0,4},{8,0},{16,8},{24,16},{28,24},{20,28},{12,20},{4,12},{1,5},{9... | collective-permute-start | bytes 393224 | tf_op jit(solution)/shard_map/ppermute | solution.py:517
  45.5 6.0 %collective-permute-start.23 = (f32[8,4,1024]{2,1,0:T(4,128)S(1)}, f32[8,4,1024]{2,1,0:T(4,128)S(1)}, u32[]{:S(2)}, u32[]{:S(2)}) collective-permute-start(f32[8,4,1024]{2,1,0:T(4,128)S(1)} %add.10), channel_id=1, source_target_pairs={{0,8},{8,16},{16,24},{24,28},{28,20},{20,12},{12,4},{4,0},{1,9},{9... | collective-permute-start | bytes 393224 | tf_op jit(solution)/shard_map/ppermute | solution.py:517
  47.3 6.8 %collective-permute-start.30 = (f32[8,4,1024]{2,1,0:T(4,128)S(1)}, f32[8,4,1024]{2,1,0:T(4,128)S(1)}, u32[]{:S(2)}, u32[]{:S(2)}) collective-permute-start(f32[8,4,1024]{2,1,0:T(4,128)S(1)} %add.14), channel_id=1, source_target_pairs={{0,4},{8,0},{16,8},{24,16},{28,24},{20,28},{12,20},{4,12},{1,5},{9... | collective-permute-start | bytes 393224 | tf_op jit(solution)/shard_map/ppermute | solution.py:517
  47.7 6.6 %collective-permute-start.20 = (f32[8,4,1024]{2,1,0:T(4,128)S(1)}, f32[8,4,1024]{2,1,0:T(4,128)S(1)}, u32[]{:S(2)}, u32[]{:S(2)}) collective-permute-start(f32[8,4,1024]{2,1,0:T(4,128)S(1)} %add.8), channel_id=1, source_target_pairs={{0,8},{8,16},{16,24},{24,28},{28,20},{20,12},{12,4},{4,0},{1,9},{9... | collective-permute-start | bytes 393224 | tf_op jit(solution)/shard_map/ppermute | solution.py:517
  51.2 6.2 %collective-permute-start.27 = (f32[8,4,1024]{2,1,0:T(4,128)S(1)}, f32[8,4,1024]{2,1,0:T(4,128)S(1)}, u32[]{:S(2)}, u32[]{:S(2)}) collective-permute-start(f32[8,4,1024]{2,1,0:T(4,128)S(1)} %add.13), channel_id=1, source_target_pairs={{0,4},{8,0},{16,8},{24,16},{28,24},{20,28},{12,20},{4,12},{1,5},{9... | collective-permute-start | bytes 393224 | tf_op jit(solution)/shard_map/ppermute | solution.py:517
  51.5 5.9 %collective-permute-start.24 = (f32[8,4,1024]{2,1,0:T(4,128)S(1)}, f32[8,4,1024]{2,1,0:T(4,128)S(1)}, u32[]{:S(2)}, u32[]{:S(2)}) collective-permute-start(f32[8,4,1024]{2,1,0:T(4,128)S(1)} %add.11), channel_id=1, source_target_pairs={{0,8},{8,16},{16,24},{24,28},{28,20},{20,12},{12,4},{4,0},{1,9},{9... | collective-permute-start | bytes 393224 | tf_op jit(solution)/shard_map/ppermute | solution.py:517
  54.0 5.0 %collective-permute-start.31 = (f32[8,4,1024]{2,1,0:T(4,128)S(1)}, f32[8,4,1024]{2,1,0:T(4,128)S(1)}, u32[]{:S(2)}, u32[]{:S(2)}) collective-permute-start(f32[8,4,1024]{2,1,0:T(4,128)S(1)} %add.15), channel_id=1, source_target_pairs={{0,4},{8,0},{16,8},{24,16},{28,24},{20,28},{12,20},{4,12},{1,5},{9... | collective-permute-start | bytes 393224 | tf_op jit(solution)/shard_map/ppermute | solution.py:517
  (9 other events, 53.0 us)
